TPU v7x, 256 devices: a whole 4x4x8 slice. The times are simulated.
256 devices in a mesh: row: 16 (over z, core), col: 16 (over x, y).
Axes of the slice: x: 4, y: 4, z: 8, core: 2. Of those that a mesh axis runs over, the one named last changes fastest.
Arguments:
- density: bfloat16 [2, 6144, 6144], P(None, 'row', 'col'), as said below
- weighted: bfloat16 [6144, 6144], P('row', 'col'), as said below
- ham_deriv: bfloat16 [3, 6144, 6144], P(None, 'row', 'col'), may hold values from -0.1875 to 0.1875
- ovl_deriv: bfloat16 [3, 6144, 6144], P(None, 'row', 'col'), may hold values from -0.1875 to 0.1875
- tile_pattern: int32 [48, 48], P('row', 'col'), may hold values from 0 to 1, as said below
- branch: int32 [2], replicated, may hold values from 0 to 1, each once
- orbital_atom: int32 [16, 384], P('row'), may hold values from 0 to 95, never falling along the last dimension, each value on 1 to 9 neighbouring positions
- positions: float32 [3, 1536], P(None, 'row'), may hold values from -6 to 6
- velocities: float32 [3, 1536], P(None, 'row'), may hold values from -12 to 12
- masses: float32 [1536], P('row'), may hold values from 0.4 to 33
Outputs:
- purified: bfloat16 [2, 6144, 6144], P(None, 'row', 'col')
- forces: float32 [3, 1536], P(None, 'row')
- new_velocities: float32 [3, 1536], P(None, 'row')
- new_positions: float32 [3, 1536], P(None, 'row')
Inputs may be any that keep to these rules, and one draw needn't show every extreme that they name: `orbital_atom`: in each slab the atom numbers never fall and every atom has 1 to 9 orbitals. `tile_pattern`: the pattern is symmetric, and every diagonal block lies on it. `density`: each channel's matrix is symmetric and zero on every block where tile_pattern is 0. `weighted`: symmetric and zero on every block where tile_pattern is 0. `branch`: the two spin channels take different branches.
All inputs are finite; a program needn't handle non-finite values.
Results may differ from a plain program's by a relative error of at most 0.01.
Values may be sent and summed in bfloat16 or wider, within the bound.
No kernel may reach another device: no remote copies, remote signals or barrier semaphores. Data moves between devices by JAX's collectives and lax.ppermute only.
A program may use at most 64 MiB of HBM per device.

v0:
```python
import jax
import jax.numpy as jnp
from jax import lax
from jax.sharding import PartitionSpec as P

TILE = 128


mixing = 0.25
time_step = 0.1
epsilon = 1e-06


def on_pattern(matrix, pattern):
    lead = matrix.shape[:-2]
    block_rows = matrix.shape[-2] // TILE
    block_cols = matrix.shape[-1] // TILE
    shaped = matrix.reshape(lead + (block_rows, TILE, block_cols, TILE))
    weights = pattern.astype(matrix.dtype)[:, None, :, None]
    return (shaped * weights).reshape(matrix.shape)


def fire_update(scaled, velocities, root_mass, force_norm, speed_norm):
    new_velocities = (
        (1.0 - mixing) * velocities
        + mixing * jnp.sqrt(speed_norm) * scaled / jnp.sqrt(force_norm + epsilon)
        + time_step * scaled
    )
    new_positions_step = time_step * new_velocities / root_mass
    return (new_velocities, new_positions_step)


def local(
    density,
    weighted,
    ham_deriv,
    ovl_deriv,
    tile_pattern,
    branch,
    orbital_atom,
    positions,
    velocities,
    masses,
):
    gathered = lax.all_gather(density, "col", axis=2, tiled=True)
    square = jnp.einsum(
        "smk,skn->smn",
        gathered,
        lax.all_gather(density, "row", axis=1, tiled=True),
        preferred_element_type=jnp.float32,
    )
    flip = (branch == 1)[:, None, None]
    raw = jnp.where(flip, 2.0 * density.astype(jnp.float32) - square, square)
    purified = on_pattern(raw, tile_pattern).astype(jnp.bfloat16)
    orbital_terms = jnp.einsum(
        "smn,xmn->xm", purified, ham_deriv, preferred_element_type=jnp.float32
    )
    orbital_terms = orbital_terms - jnp.einsum(
        "mn,xmn->xm", weighted, ovl_deriv, preferred_element_type=jnp.float32
    )
    atoms_slab = positions.shape[1]
    one_hot = (orbital_atom[0][:, None] == jnp.arange(atoms_slab, dtype=jnp.int32)[None, :]).astype(
        jnp.float32
    )
    local_forces = -2.0 * jnp.dot(orbital_terms, one_hot, precision=lax.Precision.HIGHEST)
    forces = lax.psum(local_forces, "col")
    root_mass = jnp.sqrt(masses)[None, :]
    scaled = forces / root_mass
    force_norm, speed_norm = lax.psum(
        (jnp.sum(scaled * scaled), jnp.sum(velocities * velocities)), "row"
    )
    new_velocities, moved = fire_update(scaled, velocities, root_mass, force_norm, speed_norm)
    return (purified, forces, new_velocities, positions + moved)


def solution(mesh):
    in_specs = (
        P(None, "row", "col"),
        P("row", "col"),
        P(None, "row", "col"),
        P(None, "row", "col"),
        P("row", "col"),
        P(),
        P("row", None),
        P(None, "row"),
        P(None, "row"),
        P("row"),
    )
    out_specs = (P(None, "row", "col"), P(None, "row"), P(None, "row"), P(None, "row"))
    return jax.shard_map(local, mesh=mesh, in_specs=in_specs, out_specs=out_specs, check_vma=False)
```

profile of v0, /device:TPU:1, one launch (start us, length us, event | category | flops | bytes accessed | tf_op | source)
XLA Modules:
  0.0 252.2 jit_solution(14334287285596907999)
XLA Ops:
  7.2 0.0 copy-start
  7.2 0.0 all-gather.3.cloned.1.call-start
  7.2 0.7 all-gather.3.cloned.1.call-update
  7.9 0.0 all-gather.5.cloned.1.call-start
  8.0 0.7 all-gather.5.cloned.1.call-update
  8.7 0.0 copy-done.4
  8.7 0.0 copy-start.9
  8.8 0.2 mul.51
  8.9 0.1 copy.30
  9.0 0.4 copy-done.9
  9.4 0.0 copy-done.6
  9.4 0.6 multiply_reduce_fusion.1
  10.0 0.0 copy-start.1
  10.0 1.4 fusion.2
  11.5 90.6 %all-gather.3.cloned.1.call-done = bf16[2,384,6144]{2,1,0:T(8,128)(2,1)} async-done(((bf16[2,384,384]{2,1,0:T(8,128)(2,1)}), bf16[2,384,6144]{2,1,0:T(8,128)(2,1)}) %all-gather.3.cloned.1.call-update) | async-done | bytes 9437200 | tf_op jit(solution)/shard_map/all_gather | solution.py:45
  102.1 63.5 %all-gather.5.cloned.1.call-done = bf16[2,6144,384]{2,1,0:T(8,128)(2,1)} async-done(((bf16[2,384,384]{2,1,0:T(8,128)(2,1)}), bf16[2,6144,384]{2,1,0:T(8,128)(2,1)}) %all-gather.5.cloned.1.call-update) | async-done | bytes 9437200 | tf_op jit(solution)/shard_map/all_gather | solution.py:49
  165.5 11.3 %convert_reduce_fusion = (bf16[384,384]{1,0:T(8,128)(2,1)S(1)}, bf16[2,384,384]{2,1,0:T(8,128)(2,1)}) fusion(f32[384,384]{1,0:T(8,128)S(1)} %bitcast.14, bf16[2,384,384]{2,1,0:T(8,128)(2,1)S(1)} %copy-done.1, pred[2]{0:T(512)(128)(4,1)S(1)} %broadcast_compare_fusion, bf16[2,384,6144]{2,1,0:T(8,128)(2,1)} %all-gather.3.cloned.1.call-done, ...), kind=kOutput, calls=%fused_computation.3 | convolution fusion | flops 3626090496 | bytes 20938754 | tf_op jit(solution)/shard_map/smk,skn->smn/dot_general | solution.py:46
  176.9 0.0 copy-start.5
  176.9 1.4 fusion.4
  178.3 0.4 convolution_multiply_fusion
  178.7 33.2 %psum.21 = f32[3,96]{1,0:T(4,128)S(1)} all-reduce(f32[3,96]{1,0:T(4,128)S(1)} %convolution_multiply_fusion), channel_id=1, replica_groups=mesh['row'=16,'col'=16] {'col'}, use_global_device_ids=true, to_apply=%region_1.2 | all-reduce | flops 288 | bytes 2304 | tf_op jit(solution)/shard_map/psum | solution.py:66
  211.9 0.6 multiply_reduce_fusion
  212.5 30.9 %all-reduce = (f32[]{:T(128)}, f32[]{:T(128)}) all-reduce(f32[]{:T(128)} %multiply_reduce_fusion, f32[]{:T(128)} %multiply_reduce_fusion.1), channel_id=1, replica_groups=mesh['row'=16,'col'=16] {'row'}, use_global_device_ids=true, to_apply=%region_5.6 | all-reduce | flops 2 | bytes 16 | tf_op jit(solution)/shard_map/psum | solution.py:69
  244.8 0.6 divide_add_fusion
  (19 shorter events, 0.1 us)
Async XLA Ops:
  7.2 169.7 %copy-start = (bf16[3,384,384]{2,1,0:T(8,128)(2,1)S(1)}, bf16[3,384,384]{2,1,0:T(8,128)(2,1)}, u32[]{:S(2)}) copy-start(bf16[3,384,384]{2,1,0:T(8,128)(2,1)} %param.12) | copy-start | bytes 2654212
  7.2 1.5 copy-start.4
  7.2 94.9 %all-gather.3.cloned.1.call-start = ((), (), s32[]{:S(2)}) async-start(), calls=%async_computation | async-start | bytes 10027008 | tf_op jit(solution)/shard_map/all_gather | solution.py:45
  7.9 157.6 %all-gather.5.cloned.1.call-start = ((), (), s32[]{:S(2)}) async-start(), calls=%async_computation.1 | async-start | bytes 10027008 | tf_op jit(solution)/shard_map/all_gather | solution.py:49
  8.7 0.7 copy-start.9
  8.7 0.7 copy-start.6
  8.7 0.7 copy-start.3
  8.7 1.3 copy-start.10
  8.7 1.3 copy-start.7
  8.7 1.3 copy-start.8
  10.0 155.5 %copy-start.1 = (bf16[2,384,384]{2,1,0:T(8,128)(2,1)S(1)}, bf16[2,384,384]{2,1,0:T(8,128)(2,1)}, u32[]{:S(2)}) copy-start(bf16[2,384,384]{2,1,0:T(8,128)(2,1)} %param.10) | copy-start | bytes 1769476
  176.9 67.9 %copy-start.5 = (f32[3,96]{1,0:T(4,128)S(1)}, f32[3,96]{1,0:T(4,128)}, u32[]{:S(2)}) copy-start(f32[3,96]{1,0:T(4,128)} %param.17) | copy-start | bytes 3460
  211.9 33.5 %copy-start.2 = (f32[3,96]{1,0:T(4,128)}, f32[3,96]{1,0:T(4,128)S(1)}, u32[]{:S(2)}) copy-start(f32[3,96]{1,0:T(4,128)S(1)} %psum.21) | copy-start | bytes 3460
Sparse Core Ops, SparseCore 0:
  10.4 91.6 all-gather.2
  103.9 61.5 all-gather.4
where the time goes:
time: 252 us
  waiting for transfers between devices  155 us (62%)
  blocking collectives  64.1 us (25%)
  between operations  15.6 us (6%)
  matrix products  14.6 us (6%)
    all_gather x1, waiting for transfers between devices, local(): gathered = lax.all_gather(density, 'col', axis=2, tiled=True)  90.6 us
    all_gather x1, waiting for transfers between devices, local(): lax.all_gather(density, 'row', axis=1, tiled=True)  63.5 us
    psum x1, blocking collectives, local(): forces = lax.psum(local_forces, 'col')  33.2 us
    psum x1, blocking collectives, local(): lax.psum((jnp.sum(scaled * scaled), jnp.sum(velocities * velocities)), 'r...  30.9 us
    dot_general x1, matrix products, local(): jnp.einsum('smk,skn->smn', gathered, lax.all_gather(density, 'row', axis=...  11.3 us
  transfers between devices with their start and end apart: 2, of which 2 were waited for; matrix products, arithmetic and copies ran while one was open for 1% of the time, Pallas kernels for 0%

commit v1 on v0

v1 whole, which is shorter than its diff:
```python
import jax
import jax.numpy as jnp
from jax import lax
from jax.experimental import pallas as pl
from jax.experimental.pallas import tpu as pltpu
from jax.sharding import PartitionSpec as P

TILE = 128
ROWS = 384
SLABS = 16
LANES = 128

mixing = 0.25
time_step = 0.1
epsilon = 1e-06

AXES = ("row", "col")


def place(z, core, x, y):
    return (z % 8 * 2 + core) * 16 + x % 4 * 4 + y % 4


def pairs(move):
    out = []
    for z in range(8):
        for core in range(2):
            for x in range(4):
                for y in range(4):
                    out.append((place(z, core, x, y), place(*move(z, core, x, y))))
    return out


def x_by(k):
    return pairs(lambda z, core, x, y: (z, core, x + k, y))


def y_by(k):
    return pairs(lambda z, core, x, y: (z, core, x, y + k))


def z_by(k):
    return pairs(lambda z, core, x, y: (z + k, core, x, y))


def z_swap():
    return pairs(lambda z, core, x, y: (z ^ 1, core, x, y))


def core_swap():
    return pairs(lambda z, core, x, y: (z, 1 - core, x, y))


def send(value, table):
    return lax.ppermute(value, AXES, table)


def gather_plane(block, first, second):
    one = send(block, first(1))
    two = send(block, first(-1))
    three = send(block, first(2))
    line = jnp.stack([block, one, two, three])
    ahead = send(line, second(1))
    behind = send(line, second(-1))
    far_low = send(ahead[:2], second(1))
    far_high = send(behind[2:], second(-1))
    return (line, ahead, behind, far_low, far_high)


def slots(first_at, second_at):
    line = [0, -1, 1, 2]
    order = [(a, 0) for a in line] + [(a, -1) for a in line] + [(a, 1) for a in line]
    order += [(a, 2) for a in line]
    return [((first_at + a) & 3, (second_at + b) & 3) for a, b in order]


def terms_of(matrix, deriv_ref, one_hot):
    rows = []
    for x in range(3):
        column = jnp.sum(matrix * deriv_ref[x].astype(jnp.float32), axis=1, keepdims=True)
        rows.append(jnp.sum(column * one_hot, axis=0, keepdims=True))
    return rows


def one_hot_of(atom_ref):
    lanes = lax.broadcasted_iota(jnp.int32, (ROWS, LANES), 1)
    return (atom_ref[...] == lanes).astype(jnp.float32)


def overlap_kernel(atom_ref, weighted_ref, ovl_ref, out_ref):
    rows = terms_of(weighted_ref[...].astype(jnp.float32), ovl_ref, one_hot_of(atom_ref))
    out_ref[...] = jnp.zeros_like(out_ref)
    for x in range(3):
        out_ref[x : x + 1, :] = 2.0 * rows[x]


PIECES = (4, 4, 4, 2, 2)
PARTS = 4


def purify(spin, slab_ref, branch_ref, pattern_ref, own_ref, pieces, b_ref, a_buf, b_buf, sems, total):
    copies = []
    t = 0
    for piece, count in zip(pieces, PIECES):
        for i in range(count):
            a_copy = pltpu.make_async_copy(
                piece.at[i], a_buf.at[:, pl.ds(t * ROWS, ROWS)], sems.at[0, t]
            )
            start = pl.multiple_of(slab_ref[t] * ROWS, ROWS)
            b_copy = pltpu.make_async_copy(
                b_ref.at[pl.ds(start, ROWS), :], b_buf.at[pl.ds(t * ROWS, ROWS), :], sems.at[1, t]
            )
            a_copy.start()
            b_copy.start()
            copies.append((a_copy, b_copy))
            t += 1
    each = SLABS // PARTS
    for part in range(PARTS):
        for a_copy, b_copy in copies[part * each : (part + 1) * each]:
            a_copy.wait()
            b_copy.wait()
        ks = pl.ds(part * each * ROWS, each * ROWS)
        product = jnp.dot(a_buf[:, ks], b_buf[ks, :], preferred_element_type=jnp.float32)
        if part == 0:
            total[...] = product
        else:
            total[...] += product
    square = total[...]
    flip = branch_ref[spin] == 1
    raw = jnp.where(flip, 2.0 * own_ref[...].astype(jnp.float32) - square, square)
    blocks = []
    for i in range(3):
        row = []
        for j in range(3):
            weight = pattern_ref[i, j].astype(jnp.float32)
            row.append(raw[i * TILE : (i + 1) * TILE, j * TILE : (j + 1) * TILE] * weight)
        blocks.append(jnp.concatenate(row, axis=1))
    return jnp.concatenate(blocks, axis=0).astype(jnp.bfloat16)


def first_kernel(slab_ref, branch_ref, pattern_ref, own_ref, *rest):
    pieces, (b_ref, out_ref, a_buf, b_buf, sems, total) = rest[:5], rest[5:]
    out_ref[...] = purify(
        0, slab_ref, branch_ref, pattern_ref, own_ref, pieces, b_ref, a_buf, b_buf, sems, total
    )


def second_kernel(slab_ref, branch_ref, pattern_ref, own_ref, *rest):
    pieces, rest = rest[:5], rest[5:]
    b_ref, other_ref, atom_ref, ham_ref, overlap_ref, out_ref, sums_ref = rest[:7]
    a_buf, b_buf, sems, total = rest[7:]
    purified = purify(
        1, slab_ref, branch_ref, pattern_ref, own_ref, pieces, b_ref, a_buf, b_buf, sems, total
    )
    out_ref[...] = purified
    both = purified.astype(jnp.float32) + other_ref[...].astype(jnp.float32)
    rows = terms_of(both, ham_ref, one_hot_of(atom_ref))
    sums_ref[...] = overlap_ref[...]
    for x in range(3):
        sums_ref[x : x + 1, :] += -2.0 * rows[x]


SMEM = pl.BlockSpec(memory_space=pltpu.SMEM)
VMEM = pl.BlockSpec(memory_space=pltpu.VMEM)
ANY = pl.BlockSpec(memory_space=pl.ANY)


def scratch():
    return [
        pltpu.VMEM((ROWS, SLABS * ROWS), jnp.bfloat16),
        pltpu.VMEM((SLABS * ROWS, ROWS), jnp.bfloat16),
        pltpu.SemaphoreType.DMA((2, SLABS)),
        pltpu.VMEM((ROWS, ROWS), jnp.float32),
    ]


COST = pl.CostEstimate(
    flops=2 * ROWS * ROWS * ROWS * SLABS,
    bytes_accessed=4 * ROWS * ROWS * SLABS,
    transcendentals=0,
)
PARAMS = pltpu.CompilerParams(vmem_limit_bytes=40 * 1024 * 1024)


def sum_of_four(value, by):
    one, two, three = send(value, by(1)), send(value, by(2)), send(value, by(3))
    return (value + two) + (one + three)


def local(
    density,
    weighted,
    ham_deriv,
    ovl_deriv,
    tile_pattern,
    branch,
    orbital_atom,
    positions,
    velocities,
    masses,
):
    column = lax.axis_index("col")
    at_x, at_y = column >> 2, column & 3
    slab_zero = jnp.stack([a * 1 + b * 4 for a, b in slots(at_y, at_x)]).astype(jnp.int32)
    slab_one = jnp.stack([a * 4 + b * 1 for a, b in slots(at_x, at_y)]).astype(jnp.int32)

    tall = [lax.all_gather(density[s], "row", axis=0, tiled=True) for s in range(2)]
    wide_zero = gather_plane(density[0], y_by, x_by)
    wide_one = gather_plane(density[1], x_by, y_by)

    atom_column = orbital_atom.reshape(ROWS, 1)
    overlap = pl.pallas_call(
        overlap_kernel,
        out_shape=jax.ShapeDtypeStruct((8, LANES), jnp.float32),
        in_specs=[VMEM] * 3,
        out_specs=VMEM,
    )(atom_column, weighted, ovl_deriv)

    purified_zero = pl.pallas_call(
        first_kernel,
        out_shape=jax.ShapeDtypeStruct((ROWS, ROWS), jnp.bfloat16),
        in_specs=[SMEM, SMEM, SMEM, VMEM] + [ANY] * 6,
        out_specs=VMEM,
        scratch_shapes=scratch(),
        compiler_params=PARAMS,
        cost_estimate=COST,
    )(slab_zero, branch, tile_pattern, density[0], *wide_zero, tall[0])

    purified_one, sums = pl.pallas_call(
        second_kernel,
        out_shape=(
            jax.ShapeDtypeStruct((ROWS, ROWS), jnp.bfloat16),
            jax.ShapeDtypeStruct((8, LANES), jnp.float32),
        ),
        in_specs=[SMEM, SMEM, SMEM, VMEM] + [ANY] * 6 + [VMEM] * 4,
        out_specs=(VMEM, VMEM),
        scratch_shapes=scratch(),
        compiler_params=PARAMS,
        cost_estimate=COST,
    )(
        slab_one,
        branch,
        tile_pattern,
        density[1],
        *wide_one,
        tall[1],
        purified_zero,
        atom_column,
        ham_deriv,
        overlap,
    )
    purified = jnp.stack([purified_zero, purified_one])

    sums = sum_of_four(sums, x_by)
    sums = sum_of_four(sums, y_by)
    forces = sums[:3, : positions.shape[1]]

    root_mass = jnp.sqrt(masses)[None, :]
    scaled = forces / root_mass
    norms = jnp.stack([jnp.sum(scaled * scaled), jnp.sum(velocities * velocities)])
    norms = jnp.broadcast_to(norms[:, None], (2, LANES))
    norms = norms + send(norms, core_swap())
    norms = norms + send(norms, z_swap())
    two, four, six = send(norms, z_by(2)), send(norms, z_by(4)), send(norms, z_by(6))
    norms = (norms + four) + (two + six)
    force_norm, speed_norm = norms[0, 0], norms[1, 0]
    new_velocities = (
        (1.0 - mixing) * velocities
        + mixing * jnp.sqrt(speed_norm) * scaled / jnp.sqrt(force_norm + epsilon)
        + time_step * scaled
    )
    new_positions = positions + time_step * new_velocities / root_mass
    return (purified, forces, new_velocities, new_positions)


def solution(mesh):
    in_specs = (
        P(None, "row", "col"),
        P("row", "col"),
        P(None, "row", "col"),
        P(None, "row", "col"),
        P("row", "col"),
        P(),
        P("row", None),
        P(None, "row"),
        P(None, "row"),
        P("row"),
    )
    out_specs = (P(None, "row", "col"), P(None, "row"), P(None, "row"), P(None, "row"))
    return jax.shard_map(local, mesh=mesh, in_specs=in_specs, out_specs=out_specs, check_vma=False)
```

time: 252 us -> 154 us (0.61)
  waiting for transfers between devices: 155 us -> 49.1 us
  blocking collectives: 64.1 us -> 0 us
  starting transfers between devices: 0.08 us -> 44.5 us
  local copies, waits for them, and re-layouts: 0.66 us -> 23.8 us
  matrix products: 14.6 us -> 0 us
  Pallas kernels: 0 us -> 13.2 us
  other arithmetic: 1.83 us -> 5.59 us
    all_gather x2, waiting for transfers between devices: 154 us -> 16.4 us  [local(): lax.all_gather(density[s], 'row', axis=0, tiled=True)]
    psum x2 -> x0, blocking collectives: 64.1 us -> none  [the longest x1 33.2 us: local(): forces = lax.psum(local_forces, 'col')]
    ppermute x0 -> x25, starting transfers between devices: none -> 44.4 us  [send(): return lax.ppermute(value, AXES, table)]
    ppermute x0 -> x25, waiting for transfers between devices: none -> 31.9 us  [send(): return lax.ppermute(value, AXES, table)]
    unnamed x23 -> x52, local copies, waits for them, and re-layouts: 0.49 us -> 15.9 us
    dot_general x4 -> x0, matrix products: 14.6 us -> none  [the longest x1 11.3 us: local(): jnp.einsum('smk,skn->smn', gathered, lax.all_gather(density, 'row', axis=...]
    pallas_call x0 -> x3, Pallas kernels: none -> 13.2 us  [the longest x1 5.6 us: local(): pl.pallas_call(second_kernel, out_shape=(jax.ShapeDtypeStruct((ROWS, ROWS...]
    slice x0 -> x6, local copies, waits for them, and re-layouts: none -> 6.19 us  [the longest x1 2 us: local(): density[0]]
  transfers between devices with their start and end apart: 2 -> 27, of which waited for: 2 -> 11; matrix products, arithmetic and copies ran while one was open for 1% -> 5% of each run, Pallas kernels for 0% -> 5%
where the time goes in v1:
time: 154 us; the launch traced here: 152 us
  waiting for transfers between devices  49.1 us (32%)
  starting transfers between devices  44.5 us (29%)
  local copies, waits for them, and re-layouts  23.8 us (15%)
  between operations  15.6 us (10%)
  Pallas kernels  13.2 us (9%)
  other arithmetic  5.59 us (4%)
    ppermute x25, starting transfers between devices, send(): return lax.ppermute(value, AXES, table)  44.4 us
    ppermute x25, waiting for transfers between devices, send(): return lax.ppermute(value, AXES, table)  31.9 us
    all_gather x2, waiting for transfers between devices, local(): lax.all_gather(density[s], 'row', axis=0, tiled=True)  16.4 us
    unnamed x52, local copies, waits for them, and re-layouts  15.9 us
    pallas_call x1, Pallas kernels, local(): pl.pallas_call(second_kernel, out_shape=(jax.ShapeDtypeStruct((ROWS, ROWS...  5.6 us
    pallas_call x1, Pallas kernels, local(): pl.pallas_call(first_kernel, out_shape=jax.ShapeDtypeStruct((ROWS, ROWS),...  5.27 us
  transfers between devices with their start and end apart: 27, of which 11 were waited for; matrix products, arithmetic and copies ran while one was open for 5% of the time, Pallas kernels for 5%

profile of v1, /device:TPU:1, one launch (start us, length us, event | category | flops | bytes accessed | tf_op | source)
XLA Modules:
  0.0 151.7 jit_solution(7194630457546905932)
XLA Ops:
  7.2 2.0 %fusion.2 = (bf16[1,384,384]{2,1,0:T(8,128)(2,1)}, bf16[384,384]{1,0:T(8,128)(2,1)S(1)}, bf16[384,384]{1,0:T(8,128)(2,1)S(1)}, bf16[1,384,384]{2,1,0:T(8,128)(2,1)}) fusion(bf16[2,384,384]{2,1,0:T(8,128)(2,1)} %param.10), kind=kLoop, calls=%fused_computation.16 | loop fusion | bytes 1769472 | tf_op jit(solution)/shard_map/slice | solution.py:227
  10.0 2.2 %collective-permute-start = (bf16[384,384]{1,0:T(8,128)(2,1)S(1)}, bf16[384,384]{1,0:T(8,128)(2,1)S(1)}, u32[]{:S(2)}, u32[]{:S(2)}) collective-permute-start(bf16[384,384]{1,0:T(8,128)(2,1)S(1)} %get-tuple-element.13.own_ref), channel_id=1, source_target_pairs={{0,1},{1,2},{2,3},{3,0},{4,5},{5,6},{6,7},{7,4},{8,9},{9,10},{10,1... | collective-permute-start | bytes 884744 | tf_op jit(solution)/shard_map/ppermute | solution.py:55
  12.2 1.5 %collective-permute-start.1 = (bf16[384,384]{1,0:T(8,128)(2,1)S(1)}, bf16[384,384]{1,0:T(8,128)(2,1)S(1)}, u32[]{:S(2)}, u32[]{:S(2)}) collective-permute-start(bf16[384,384]{1,0:T(8,128)(2,1)S(1)} %get-tuple-element.13.own_ref), channel_id=1, source_target_pairs={{0,3},{1,0},{2,1},{3,2},{4,7},{5,4},{6,5},{7,6},{8,11},{9,8},{10,9... | collective-permute-start | bytes 884744 | tf_op jit(solution)/shard_map/ppermute | solution.py:55
  13.7 1.6 %collective-permute-start.2 = (bf16[384,384]{1,0:T(8,128)(2,1)S(1)}, bf16[384,384]{1,0:T(8,128)(2,1)S(1)}, u32[]{:S(2)}, u32[]{:S(2)}) collective-permute-start(bf16[384,384]{1,0:T(8,128)(2,1)S(1)} %get-tuple-element.13.own_ref), channel_id=1, source_target_pairs={{0,2},{1,3},{2,0},{3,1},{4,6},{5,7},{6,4},{7,5},{8,10},{9,11},{10,... | collective-permute-start | bytes 884744 | tf_op jit(solution)/shard_map/ppermute | solution.py:55
  18.3 4.5 %collective-permute-start.9 = (bf16[384,384]{1,0:T(8,128)(2,1)S(1)}, bf16[384,384]{1,0:T(8,128)(2,1)S(1)}, u32[]{:S(2)}, u32[]{:S(2)}) collective-permute-start(bf16[384,384]{1,0:T(8,128)(2,1)S(1)} %get-tuple-element.14.own_ref), channel_id=1, source_target_pairs={{0,8},{1,9},{2,10},{3,11},{4,12},{5,13},{6,14},{7,15},{8,0},{9,1},... | collective-permute-start | bytes 884744 | tf_op jit(solution)/shard_map/ppermute | solution.py:55
  22.9 4.7 %collective-permute-done.2 = bf16[384,384]{1,0:T(8,128)(2,1)S(1)} collective-permute-done((bf16[384,384]{1,0:T(8,128)(2,1)S(1)}, bf16[384,384]{1,0:T(8,128)(2,1)S(1)}, u32[]{:S(2)}, u32[]{:S(2)}) %collective-permute-start.2) | collective-permute-done | bytes 294944 | tf_op jit(solution)/shard_map/ppermute | solution.py:55
  32.3 2.1 %collective-permute-start.11 = (bf16[4,384,384]{2,1,0:T(8,128)(2,1)S(1)}, bf16[4,384,384]{2,1,0:T(8,128)(2,1)S(1)}, u32[]{:S(2)}, u32[]{:S(2)}) collective-permute-start(bf16[4,384,384]{2,1,0:T(8,128)(2,1)S(1)} %pad_maximum_fusion.1.rest_0_), channel_id=1, source_target_pairs={{0,3},{1,0},{2,1},{3,2},{4,7},{5,4},{6,5},{7,6},{8,11},{9,8},{10,9... | collective-permute-start | bytes 3538952 | tf_op jit(solution)/shard_map/ppermute | solution.py:55
  34.5 21.6 %collective-permute-done.3.rest_1_ = bf16[4,384,384]{2,1,0:T(8,128)(2,1)S(1)} collective-permute-done((bf16[4,384,384]{2,1,0:T(8,128)(2,1)S(1)}, bf16[4,384,384]{2,1,0:T(8,128)(2,1)S(1)}, u32[]{:S(2)}, u32[]{:S(2)}) %collective-permute-start.3) | collective-permute-done | bytes 1179680 | tf_op jit(solution)/shard_map/ppermute | solution.py:55
  58.0 2.7 %collective-permute-start.6 = (bf16[2,384,384]{2,1,0:T(8,128)(2,1)}, bf16[2,384,384]{2,1,0:T(8,128)(2,1)}, u32[]{:S(2)}, u32[]{:S(2)}) collective-permute-start(bf16[2,384,384]{2,1,0:T(8,128)(2,1)} %slice.41), channel_id=1, source_target_pairs={{0,12},{1,13},{2,14},{3,15},{4,0},{5,1},{6,2},{7,3},{8,4},{9,5},{1... | collective-permute-start | bytes 1769480 | tf_op jit(solution)/shard_map/ppermute | solution.py:55
  63.7 2.5 %collective-permute-start.13 = (bf16[2,384,384]{2,1,0:T(8,128)(2,1)}, bf16[2,384,384]{2,1,0:T(8,128)(2,1)}, u32[]{:S(2)}, u32[]{:S(2)}) collective-permute-start(bf16[2,384,384]{2,1,0:T(8,128)(2,1)} %slice.43), channel_id=1, source_target_pairs={{0,3},{1,0},{2,1},{3,2},{4,7},{5,4},{6,5},{7,6},{8,11},{9,8},{10,9... | collective-permute-start | bytes 1769480 | tf_op jit(solution)/shard_map/ppermute | solution.py:55
  67.8 2.3 %shard_map.130.rest_9_ = f32[8,128]{1,0:T(8,128)} custom-call(s32[384,1]{1,0:T(8,128)} %copy.15.atom_ref.rest_7_, bf16[384,384]{1,0:T(8,128)(2,1)} %weighted_ref.1, bf16[3,384,384]{2,1,0:T(8,128)(2,1)} %ovl_ref.1), custom_call_target="tpu_custom_call" | custom-call | tf_op jit(solution)/shard_map/pallas_call | solution.py:212
  71.0 2.3 %copy-done.1 = bf16[1,6144,384]{2,1,0:T(8,128)(2,1)S(1)} copy-done((bf16[1,6144,384]{2,1,0:T(8,128)(2,1)S(1)}, bf16[1,6144,384]{2,1,0:T(8,128)(2,1)}, u32[]{:S(2)}) %copy-start.1) | copy-done | bytes 4718616
  77.6 5.3 %shard_map.129.rest_6_ = bf16[384,384]{1,0:T(8,128)(2,1)S(1)} custom-call(s32[16]{0:T(128)S(1)} %copy-done.19, s32[2]{0:T(128)S(1)} %copy-done.18, s32[3,3]{1,0:T(4,128)S(1)} %copy-done.17, bf16[384,384]{1,0:T(8,128)(2,1)S(1)} %copy-done.14, bf16[4,384,384]{2,1,0:T(8,128)(2,1)S(1)} %pad_maximum_fusion.rest_0_, bf16[4,384,384]{2,1,0:T(8,128)(2,1)S(1)} %copy-done.7, ...), custom_call_target="tpu_custom_call" | custom-call | flops 1811939328 | bytes 9437184 | tf_op jit(solution)/shard_map/pallas_call | solution.py:219
  83.6 16.4 %all-gather.7.cloned.1.call-done = bf16[1,6144,384]{2,1,0:T(8,128)(2,1)} async-done(((bf16[1,384,384]{2,1,0:T(8,128)(2,1)}), bf16[1,6144,384]{2,1,0:T(8,128)(2,1)}) %all-gather.7.cloned.1.call-update) | async-done | bytes 4718608 | tf_op jit(solution)/shard_map/all_gather | solution.py:207
  100.0 2.3 %copy-done = bf16[1,6144,384]{2,1,0:T(8,128)(2,1)S(1)} copy-done((bf16[1,6144,384]{2,1,0:T(8,128)(2,1)S(1)}, bf16[1,6144,384]{2,1,0:T(8,128)(2,1)}, u32[]{:S(2)}) %copy-start) | copy-done | bytes 4718616
  107.7 5.6 %shard_map.131 = (bf16[384,384]{1,0:T(8,128)(2,1)S(1)}, f32[8,128]{1,0:T(8,128)S(1)}) custom-call(s32[16]{0:T(128)S(1)} %stack.134.slab_ref, s32[2]{0:T(128)S(1)} %copy-done.18, s32[3,3]{1,0:T(4,128)S(1)} %copy-done.17, bf16[384,384]{1,0:T(8,128)(2,1)S(1)} %copy-done.12, bf16[4,384,384]{2,1,0:T(8,128)(2,1)S(1)} %pad_maximum_fusion.1.rest_0_, ...), custom_call_target="tpu_custom_call" | custom-call | flops 1811939328 | bytes 9437184 | tf_op jit(solution)/shard_map/pallas_call | solution.py:229
  113.3 2.8 %collective-permute-start.14 = (f32[8,128]{1,0:T(8,128)S(1)}, f32[8,128]{1,0:T(8,128)S(1)}, u32[]{:S(2)}, u32[]{:S(2)}) collective-permute-start(f32[8,128]{1,0:T(8,128)S(1)} %get-tuple-element.7), channel_id=1, source_target_pairs={{0,8},{1,9},{2,10},{3,11},{4,12},{5,13},{6,14},{7,15},{8,0},{9,1},... | collective-permute-start | bytes 12296 | tf_op jit(solution)/shard_map/ppermute | solution.py:55
  116.3 2.4 %collective-permute-start.16 = (f32[8,128]{1,0:T(8,128)S(1)}, f32[8,128]{1,0:T(8,128)S(1)}, u32[]{:S(2)}, u32[]{:S(2)}) collective-permute-start(f32[8,128]{1,0:T(8,128)S(1)} %get-tuple-element.7), channel_id=1, source_target_pairs={{0,12},{1,13},{2,14},{3,15},{4,0},{5,1},{6,2},{7,3},{8,4},{9,5},{1... | collective-permute-start | bytes 12296 | tf_op jit(solution)/shard_map/ppermute | solution.py:55
  119.8 2.8 %collective-permute-start.17 = (f32[8,128]{1,0:T(8,128)S(1)}, f32[8,128]{1,0:T(8,128)S(1)}, u32[]{:S(2)}, u32[]{:S(2)}) collective-permute-start(f32[8,128]{1,0:T(8,128)S(1)} %add_add_fusion.1), channel_id=1, source_target_pairs={{0,2},{1,3},{2,0},{3,1},{4,6},{5,7},{6,4},{7,5},{8,10},{9,11},{10,... | collective-permute-start | bytes 12296 | tf_op jit(solution)/shard_map/ppermute | solution.py:55
  122.9 2.3 %collective-permute-start.19 = (f32[8,128]{1,0:T(8,128)S(1)}, f32[8,128]{1,0:T(8,128)S(1)}, u32[]{:S(2)}, u32[]{:S(2)}) collective-permute-start(f32[8,128]{1,0:T(8,128)S(1)} %add_add_fusion.1), channel_id=1, source_target_pairs={{0,3},{1,0},{2,1},{3,2},{4,7},{5,4},{6,5},{7,6},{8,11},{9,8},{10,9... | collective-permute-start | bytes 12296 | tf_op jit(solution)/shard_map/ppermute | solution.py:55
  128.3 3.1 %collective-permute-start.20 = (f32[2,128]{1,0:T(2,128)S(1)}, f32[2,128]{1,0:T(2,128)S(1)}, u32[]{:S(2)}, u32[]{:S(2)}) collective-permute-start(f32[2,128]{1,0:T(2,128)S(1)} %broadcast_in_dim.2), channel_id=1, source_target_pairs={{0,16},{1,17},{2,18},{3,19},{4,20},{5,21},{6,22},{7,23},{8,24},{9,... | collective-permute-start | bytes 3080 | tf_op jit(solution)/shard_map/ppermute | solution.py:55
  133.0 1.7 %collective-permute-done.21 = f32[2,128]{1,0:T(2,128)S(1)} collective-permute-done((f32[2,128]{1,0:T(2,128)S(1)}, f32[2,128]{1,0:T(2,128)S(1)}, u32[]{:S(2)}, u32[]{:S(2)}) %collective-permute-start.21) | collective-permute-done | bytes 1056 | tf_op jit(solution)/shard_map/ppermute | solution.py:55
  134.8 2.8 %collective-permute-start.22 = (f32[2,128]{1,0:T(2,128)S(1)}, f32[2,128]{1,0:T(2,128)S(1)}, u32[]{:S(2)}, u32[]{:S(2)}) collective-permute-start(f32[2,128]{1,0:T(2,128)S(1)} %fusion.4), channel_id=1, source_target_pairs={{0,128},{1,129},{2,130},{3,131},{4,132},{5,133},{6,134},{7,135},{8... | collective-permute-start | bytes 3080 | tf_op jit(solution)/shard_map/ppermute | solution.py:55
  138.8 2.3 %collective-permute-start.24 = (f32[2,128]{1,0:T(2,128)S(1)}, f32[2,128]{1,0:T(2,128)S(1)}, u32[]{:S(2)}, u32[]{:S(2)}) collective-permute-start(f32[2,128]{1,0:T(2,128)S(1)} %fusion.4), channel_id=1, source_target_pairs={{0,192},{1,193},{2,194},{3,195},{4,196},{5,197},{6,198},{7,199},{8... | collective-permute-start | bytes 3080 | tf_op jit(solution)/shard_map/ppermute | solution.py:55
  (110 shorter events, 36.3 us)
Async XLA Ops:
  7.2 63.8 %all-gather.5.cloned.1.call-start = ((), (), s32[]{:S(2)}) async-start(), calls=%async_computation | async-start | bytes 5013504 | tf_op jit(solution)/shard_map/all_gather | solution.py:207
  9.2 90.8 %all-gather.7.cloned.1.call-start = ((), (), s32[]{:S(2)}) async-start(), calls=%async_computation.1 | async-start | bytes 5013504 | tf_op jit(solution)/shard_map/all_gather | solution.py:207
  10.0 8.3 %collective-permute-start = (bf16[384,384]{1,0:T(8,128)(2,1)S(1)}, bf16[384,384]{1,0:T(8,128)(2,1)S(1)}, u32[]{:S(2)}, u32[]{:S(2)}) collective-permute-start(bf16[384,384]{1,0:T(8,128)(2,1)S(1)} %get-tuple-element.13.own_ref), channel_id=1, source_target_pairs={{0,1},{1,2},{2,3},{3,0},{4,5},{5,6},{6,7},{7,4},{8,9},{9,10},{10,1... | collective-permute-start | bytes 884744 | tf_op jit(solution)/shard_map/ppermute | solution.py:55
  12.2 10.7 %collective-permute-start.1 = (bf16[384,384]{1,0:T(8,128)(2,1)S(1)}, bf16[384,384]{1,0:T(8,128)(2,1)S(1)}, u32[]{:S(2)}, u32[]{:S(2)}) collective-permute-start(bf16[384,384]{1,0:T(8,128)(2,1)S(1)} %get-tuple-element.13.own_ref), channel_id=1, source_target_pairs={{0,3},{1,0},{2,1},{3,2},{4,7},{5,4},{6,5},{7,6},{8,11},{9,8},{10,9... | collective-permute-start | bytes 884744 | tf_op jit(solution)/shard_map/ppermute | solution.py:55
  13.7 13.8 %collective-permute-start.2 = (bf16[384,384]{1,0:T(8,128)(2,1)S(1)}, bf16[384,384]{1,0:T(8,128)(2,1)S(1)}, u32[]{:S(2)}, u32[]{:S(2)}) collective-permute-start(bf16[384,384]{1,0:T(8,128)(2,1)S(1)} %get-tuple-element.13.own_ref), channel_id=1, source_target_pairs={{0,2},{1,3},{2,0},{3,1},{4,6},{5,7},{6,4},{7,5},{8,10},{9,11},{10,... | collective-permute-start | bytes 884744 | tf_op jit(solution)/shard_map/ppermute | solution.py:55
  15.3 16.2 %collective-permute-start.7 = (bf16[384,384]{1,0:T(8,128)(2,1)S(1)}, bf16[384,384]{1,0:T(8,128)(2,1)S(1)}, u32[]{:S(2)}, u32[]{:S(2)}) collective-permute-start(bf16[384,384]{1,0:T(8,128)(2,1)S(1)} %get-tuple-element.14.own_ref), channel_id=1, source_target_pairs={{0,4},{1,5},{2,6},{3,7},{4,8},{5,9},{6,10},{7,11},{8,12},{9,13},{1... | collective-permute-start | bytes 884744 | tf_op jit(solution)/shard_map/ppermute | solution.py:55
  16.5 15.0 %collective-permute-start.8 = (bf16[384,384]{1,0:T(8,128)(2,1)S(1)}, bf16[384,384]{1,0:T(8,128)(2,1)S(1)}, u32[]{:S(2)}, u32[]{:S(2)}) collective-permute-start(bf16[384,384]{1,0:T(8,128)(2,1)S(1)} %get-tuple-element.14.own_ref), channel_id=1, source_target_pairs={{0,12},{1,13},{2,14},{3,15},{4,0},{5,1},{6,2},{7,3},{8,4},{9,5},{1... | collective-permute-start | bytes 884744 | tf_op jit(solution)/shard_map/ppermute | solution.py:55
  18.3 13.2 %collective-permute-start.9 = (bf16[384,384]{1,0:T(8,128)(2,1)S(1)}, bf16[384,384]{1,0:T(8,128)(2,1)S(1)}, u32[]{:S(2)}, u32[]{:S(2)}) collective-permute-start(bf16[384,384]{1,0:T(8,128)(2,1)S(1)} %get-tuple-element.14.own_ref), channel_id=1, source_target_pairs={{0,8},{1,9},{2,10},{3,11},{4,12},{5,13},{6,14},{7,15},{8,0},{9,1},... | collective-permute-start | bytes 884744 | tf_op jit(solution)/shard_map/ppermute | solution.py:55
  28.8 27.3 %collective-permute-start.3 = (bf16[4,384,384]{2,1,0:T(8,128)(2,1)S(1)}, bf16[4,384,384]{2,1,0:T(8,128)(2,1)S(1)}, u32[]{:S(2)}, u32[]{:S(2)}) collective-permute-start(bf16[4,384,384]{2,1,0:T(8,128)(2,1)S(1)} %pad_maximum_fusion.rest_0_), channel_id=1, source_target_pairs={{0,4},{1,5},{2,6},{3,7},{4,8},{5,9},{6,10},{7,11},{8,12},{9,13},{1... | collective-permute-start | bytes 3538952 | tf_op jit(solution)/shard_map/ppermute | solution.py:55
  30.0 27.0 %collective-permute-start.4 = (bf16[4,384,384]{2,1,0:T(8,128)(2,1)S(1)}, bf16[4,384,384]{2,1,0:T(8,128)(2,1)S(1)}, u32[]{:S(2)}, u32[]{:S(2)}) collective-permute-start(bf16[4,384,384]{2,1,0:T(8,128)(2,1)S(1)} %pad_maximum_fusion.rest_0_), channel_id=1, source_target_pairs={{0,12},{1,13},{2,14},{3,15},{4,0},{5,1},{6,2},{7,3},{8,4},{9,5},{1... | collective-permute-start | bytes 3538952 | tf_op jit(solution)/shard_map/ppermute | solution.py:55
  31.7 29.0 %collective-permute-start.10 = (bf16[4,384,384]{2,1,0:T(8,128)(2,1)S(1)}, bf16[4,384,384]{2,1,0:T(8,128)(2,1)S(1)}, u32[]{:S(2)}, u32[]{:S(2)}) collective-permute-start(bf16[4,384,384]{2,1,0:T(8,128)(2,1)S(1)} %pad_maximum_fusion.1.rest_0_), channel_id=1, source_target_pairs={{0,1},{1,2},{2,3},{3,0},{4,5},{5,6},{6,7},{7,4},{8,9},{9,10},{10,1... | collective-permute-start | bytes 3538952 | tf_op jit(solution)/shard_map/ppermute | solution.py:55
  32.3 29.4 %collective-permute-start.11 = (bf16[4,384,384]{2,1,0:T(8,128)(2,1)S(1)}, bf16[4,384,384]{2,1,0:T(8,128)(2,1)S(1)}, u32[]{:S(2)}, u32[]{:S(2)}) collective-permute-start(bf16[4,384,384]{2,1,0:T(8,128)(2,1)S(1)} %pad_maximum_fusion.1.rest_0_), channel_id=1, source_target_pairs={{0,3},{1,0},{2,1},{3,2},{4,7},{5,4},{6,5},{7,6},{8,11},{9,8},{10,9... | collective-permute-start | bytes 3538952 | tf_op jit(solution)/shard_map/ppermute | solution.py:55
  57.1 13.9 %collective-permute-start.5 = (bf16[2,384,384]{2,1,0:T(8,128)(2,1)}, bf16[2,384,384]{2,1,0:T(8,128)(2,1)}, u32[]{:S(2)}, u32[]{:S(2)}) collective-permute-start(bf16[2,384,384]{2,1,0:T(8,128)(2,1)} %slice.40), channel_id=1, source_target_pairs={{0,4},{1,5},{2,6},{3,7},{4,8},{5,9},{6,10},{7,11},{8,12},{9,13},{1... | collective-permute-start | bytes 1769480 | tf_op jit(solution)/shard_map/ppermute | solution.py:55
  58.0 13.0 %collective-permute-start.6 = (bf16[2,384,384]{2,1,0:T(8,128)(2,1)}, bf16[2,384,384]{2,1,0:T(8,128)(2,1)}, u32[]{:S(2)}, u32[]{:S(2)}) collective-permute-start(bf16[2,384,384]{2,1,0:T(8,128)(2,1)} %slice.41), channel_id=1, source_target_pairs={{0,12},{1,13},{2,14},{3,15},{4,0},{5,1},{6,2},{7,3},{8,4},{9,5},{1... | collective-permute-start | bytes 1769480 | tf_op jit(solution)/shard_map/ppermute | solution.py:55
  61.6 22.0 %collective-permute-start.12 = (bf16[2,384,384]{2,1,0:T(8,128)(2,1)}, bf16[2,384,384]{2,1,0:T(8,128)(2,1)}, u32[]{:S(2)}, u32[]{:S(2)}) collective-permute-start(bf16[2,384,384]{2,1,0:T(8,128)(2,1)} %slice.42), channel_id=1, source_target_pairs={{0,1},{1,2},{2,3},{3,0},{4,5},{5,6},{6,7},{7,4},{8,9},{9,10},{10,1... | collective-permute-start | bytes 1769480 | tf_op jit(solution)/shard_map/ppermute | solution.py:55
  63.7 19.9 %collective-permute-start.13 = (bf16[2,384,384]{2,1,0:T(8,128)(2,1)}, bf16[2,384,384]{2,1,0:T(8,128)(2,1)}, u32[]{:S(2)}, u32[]{:S(2)}) collective-permute-start(bf16[2,384,384]{2,1,0:T(8,128)(2,1)} %slice.43), channel_id=1, source_target_pairs={{0,3},{1,0},{2,1},{3,2},{4,7},{5,4},{6,5},{7,6},{8,11},{9,8},{10,9... | collective-permute-start | bytes 1769480 | tf_op jit(solution)/shard_map/ppermute | solution.py:55
  113.3 5.5 %collective-permute-start.14 = (f32[8,128]{1,0:T(8,128)S(1)}, f32[8,128]{1,0:T(8,128)S(1)}, u32[]{:S(2)}, u32[]{:S(2)}) collective-permute-start(f32[8,128]{1,0:T(8,128)S(1)} %get-tuple-element.7), channel_id=1, source_target_pairs={{0,8},{1,9},{2,10},{3,11},{4,12},{5,13},{6,14},{7,15},{8,0},{9,1},... | collective-permute-start | bytes 12296 | tf_op jit(solution)/shard_map/ppermute | solution.py:55
  116.1 3.7 %collective-permute-start.15 = (f32[8,128]{1,0:T(8,128)S(1)}, f32[8,128]{1,0:T(8,128)S(1)}, u32[]{:S(2)}, u32[]{:S(2)}) collective-permute-start(f32[8,128]{1,0:T(8,128)S(1)} %get-tuple-element.7), channel_id=1, source_target_pairs={{0,4},{1,5},{2,6},{3,7},{4,8},{5,9},{6,10},{7,11},{8,12},{9,13},{1... | collective-permute-start | bytes 12296 | tf_op jit(solution)/shard_map/ppermute | solution.py:55
  119.8 6.1 %collective-permute-start.17 = (f32[8,128]{1,0:T(8,128)S(1)}, f32[8,128]{1,0:T(8,128)S(1)}, u32[]{:S(2)}, u32[]{:S(2)}) collective-permute-start(f32[8,128]{1,0:T(8,128)S(1)} %add_add_fusion.1), channel_id=1, source_target_pairs={{0,2},{1,3},{2,0},{3,1},{4,6},{5,7},{6,4},{7,5},{8,10},{9,11},{10,... | collective-permute-start | bytes 12296 | tf_op jit(solution)/shard_map/ppermute | solution.py:55
  122.5 3.7 %collective-permute-start.18 = (f32[8,128]{1,0:T(8,128)S(1)}, f32[8,128]{1,0:T(8,128)S(1)}, u32[]{:S(2)}, u32[]{:S(2)}) collective-permute-start(f32[8,128]{1,0:T(8,128)S(1)} %add_add_fusion.1), channel_id=1, source_target_pairs={{0,1},{1,2},{2,3},{3,0},{4,5},{5,6},{6,7},{7,4},{8,9},{9,10},{10,1... | collective-permute-start | bytes 12296 | tf_op jit(solution)/shard_map/ppermute | solution.py:55
  128.3 3.9 %collective-permute-start.20 = (f32[2,128]{1,0:T(2,128)S(1)}, f32[2,128]{1,0:T(2,128)S(1)}, u32[]{:S(2)}, u32[]{:S(2)}) collective-permute-start(f32[2,128]{1,0:T(2,128)S(1)} %broadcast_in_dim.2), channel_id=1, source_target_pairs={{0,16},{1,17},{2,18},{3,19},{4,20},{5,21},{6,22},{7,23},{8,24},{9,... | collective-permute-start | bytes 3080 | tf_op jit(solution)/shard_map/ppermute | solution.py:55
  134.8 7.2 %collective-permute-start.22 = (f32[2,128]{1,0:T(2,128)S(1)}, f32[2,128]{1,0:T(2,128)S(1)}, u32[]{:S(2)}, u32[]{:S(2)}) collective-permute-start(f32[2,128]{1,0:T(2,128)S(1)} %fusion.4), channel_id=1, source_target_pairs={{0,128},{1,129},{2,130},{3,131},{4,132},{5,133},{6,134},{7,135},{8... | collective-permute-start | bytes 3080 | tf_op jit(solution)/shard_map/ppermute | solution.py:55
  137.5 4.5 %collective-permute-start.23 = (f32[2,128]{1,0:T(2,128)S(1)}, f32[2,128]{1,0:T(2,128)S(1)}, u32[]{:S(2)}, u32[]{:S(2)}) collective-permute-start(f32[2,128]{1,0:T(2,128)S(1)} %fusion.4), channel_id=1, source_target_pairs={{0,64},{1,65},{2,66},{3,67},{4,68},{5,69},{6,70},{7,71},{8,72},{9,... | collective-permute-start | bytes 3080 | tf_op jit(solution)/shard_map/ppermute | solution.py:55
  138.8 3.6 %collective-permute-start.24 = (f32[2,128]{1,0:T(2,128)S(1)}, f32[2,128]{1,0:T(2,128)S(1)}, u32[]{:S(2)}, u32[]{:S(2)}) collective-permute-start(f32[2,128]{1,0:T(2,128)S(1)} %fusion.4), channel_id=1, source_target_pairs={{0,192},{1,193},{2,194},{3,195},{4,196},{5,197},{6,198},{7,199},{8... | collective-permute-start | bytes 3080 | tf_op jit(solution)/shard_map/ppermute | solution.py:55
  (29 other events, 209.6 us)
Sparse Core Ops, SparseCore 0:
  9.8 46.9 all-gather.4
  58.7 41.3 all-gather.6

commit v2 on v0

v2 whole, which is shorter than its diff:
```python
import jax
import jax.numpy as jnp
from jax import lax
from jax.experimental import pallas as pl
from jax.experimental.pallas import tpu as pltpu
from jax.sharding import PartitionSpec as P

TILE = 128
ROWS = 384
SLABS = 16
LANES = 128

mixing = 0.25
time_step = 0.1
epsilon = 1e-06

AXES = ("row", "col")


def place(z, core, x, y):
    return (z % 8 * 2 + core) * 16 + x % 4 * 4 + y % 4


def pairs(move):
    out = []
    for z in range(8):
        for core in range(2):
            for x in range(4):
                for y in range(4):
                    out.append((place(z, core, x, y), place(*move(z, core, x, y))))
    return out


def x_by(k):
    return pairs(lambda z, core, x, y: (z, core, x + k, y))


def y_by(k):
    return pairs(lambda z, core, x, y: (z, core, x, y + k))


def x_swap(bit):
    return pairs(lambda z, core, x, y: (z, core, x ^ bit, y))


def y_swap(bit):
    return pairs(lambda z, core, x, y: (z, core, x, y ^ bit))


def z_swap(bit):
    return pairs(lambda z, core, x, y: (z ^ bit, core, x, y))


def core_swap():
    return pairs(lambda z, core, x, y: (z, 1 - core, x, y))


def send(value, table):
    return lax.ppermute(value, AXES, table)


def gather_plane(block, first, second):
    one = send(block, first(1))
    two = send(block, first(-1))
    three = send(block, first(2))
    near = jnp.stack([block, one])
    ahead_near = send(near, second(1))
    behind_near = send(near, second(-1))
    rest = jnp.stack([two, three])
    ahead_rest = send(rest, second(1))
    behind_rest = send(rest, second(-1))
    far_near = send(ahead_near, second(1))
    far_rest = send(behind_rest, second(-1))
    return (near, ahead_near, behind_near, far_near, rest, ahead_rest, behind_rest, far_rest)


def slots(first_at, second_at):
    order = [(a, b) for line in ((0, -1), (1, 2)) for b in (0, -1, 1, 2) for a in line]
    return [((first_at + a) & 3, (second_at + b) & 3) for a, b in order]


def terms_of(matrix, deriv_ref, one_hot):
    rows = []
    for x in range(3):
        column = jnp.sum(matrix * deriv_ref[x].astype(jnp.float32), axis=1, keepdims=True)
        rows.append(jnp.sum(column * one_hot, axis=0, keepdims=True))
    return rows


def one_hot_of(atom_ref):
    lanes = lax.broadcasted_iota(jnp.int32, (ROWS, LANES), 1)
    return (atom_ref[...] == lanes).astype(jnp.float32)


def overlap_kernel(atom_ref, weighted_ref, ovl_ref, out_ref):
    rows = terms_of(weighted_ref[...].astype(jnp.float32), ovl_ref, one_hot_of(atom_ref))
    out_ref[...] = jnp.zeros_like(out_ref)
    for x in range(3):
        out_ref[x : x + 1, :] = 2.0 * rows[x]


PIECES = 8
GROUPS = 4


def b_copies(facts_ref, tall_ref, b_buf, sems):
    copies = []
    for spin in range(2):
        for t in range(SLABS):
            start = pl.multiple_of(facts_ref[spin * SLABS + t] * ROWS, ROWS)
            copies.append(
                pltpu.make_async_copy(
                    tall_ref.at[spin, pl.ds(start, ROWS), :],
                    b_buf.at[spin, pl.ds(t * ROWS, ROWS), :],
                    sems.at[spin, t],
                )
            )
    return copies


def purify_kernel(facts_ref, *rest):
    wide = (rest[:PIECES], rest[PIECES : 2 * PIECES])
    tall_ref, density_ref, deriv_ref, atom_ref, overlap_ref = rest[2 * PIECES : 2 * PIECES + 5]
    out_ref, sums_ref, b_buf, sems, total, own_ref, ham_ref, own_sems = rest[2 * PIECES + 5 :]
    copies = b_copies(facts_ref, tall_ref, b_buf, sems)
    own_copy = pltpu.make_async_copy(density_ref, own_ref, own_sems.at[0])
    ham_copy = pltpu.make_async_copy(deriv_ref, ham_ref, own_sems.at[1])
    for copy in copies[:SLABS]:
        copy.start()
    own_copy.start()
    for copy in copies[SLABS:]:
        copy.start()
    ham_copy.start()
    each = SLABS // GROUPS
    for spin in range(2):
        for group in range(GROUPS):
            for copy in copies[spin * SLABS + group * each : spin * SLABS + (group + 1) * each]:
                copy.wait()
            slabs = [wide[spin][group * each // 2 + i][j] for i in range(each // 2) for j in range(2)]
            product = jnp.dot(
                jnp.concatenate(slabs, axis=1),
                b_buf[spin, pl.ds(group * each * ROWS, each * ROWS), :],
                preferred_element_type=jnp.float32,
            )
            if group == 0:
                total[...] = product
            else:
                total[...] += product
        square = total[...]
        if spin == 0:
            own_copy.wait()
        flip = facts_ref[2 * SLABS + spin] == 1
        raw = jnp.where(flip, 2.0 * own_ref[spin].astype(jnp.float32) - square, square)
        for i in range(3):
            for j in range(3):
                weight = facts_ref[2 * SLABS + 2 + 3 * i + j].astype(jnp.float32)
                at = (slice(i * TILE, (i + 1) * TILE), slice(j * TILE, (j + 1) * TILE))
                out_ref[(spin,) + at] = (raw[at] * weight).astype(jnp.bfloat16)
    both = out_ref[0].astype(jnp.float32) + out_ref[1].astype(jnp.float32)
    ham_copy.wait()
    rows = terms_of(both, ham_ref, one_hot_of(atom_ref))
    sums_ref[...] = overlap_ref[...]
    for x in range(3):
        sums_ref[x : x + 1, :] += -2.0 * rows[x]


def norm_kernel(one_ref, two_ref, velocities_ref, masses_ref, forces_ref, sums_ref, norms_ref):
    sums = one_ref[...] + two_ref[...]
    forces = sums[:3, : forces_ref.shape[1]]
    forces_ref[...] = forces
    sums_ref[...] = sums
    scaled = forces / jnp.sqrt(masses_ref[...])
    speeds = velocities_ref[...]
    rows = lax.broadcasted_iota(jnp.int32, norms_ref.shape, 0)
    norms_ref[...] = jnp.where(rows == 0, jnp.sum(scaled * scaled), jnp.sum(speeds * speeds))


def update_kernel(
    one_ref, two_ref, sums_ref, positions_ref, velocities_ref, masses_ref, speeds_ref, places_ref
):
    norms = one_ref[...] + two_ref[...]
    force_norm, speed_norm = norms[0:1, 0:1], norms[1:2, 0:1]
    root_mass = jnp.sqrt(masses_ref[...])
    scaled = sums_ref[:3, : speeds_ref.shape[1]] / root_mass
    speeds = (
        (1.0 - mixing) * velocities_ref[...]
        + mixing * jnp.sqrt(speed_norm) * scaled / jnp.sqrt(force_norm + epsilon)
        + time_step * scaled
    )
    speeds_ref[...] = speeds
    places_ref[...] = positions_ref[...] + time_step * speeds / root_mass


SMEM = pl.BlockSpec(memory_space=pltpu.SMEM)
VMEM = pl.BlockSpec(memory_space=pltpu.VMEM)
HBM = pl.BlockSpec(memory_space=pltpu.HBM)

COST = pl.CostEstimate(
    flops=4 * ROWS * ROWS * ROWS * SLABS,
    bytes_accessed=8 * ROWS * ROWS * SLABS,
    transcendentals=0,
)
PARAMS = pltpu.CompilerParams(vmem_limit_bytes=45 * 1024 * 1024)


def small(shape):
    return jax.ShapeDtypeStruct(shape, jnp.float32)


def local(
    density,
    weighted,
    ham_deriv,
    ovl_deriv,
    tile_pattern,
    branch,
    orbital_atom,
    positions,
    velocities,
    masses,
):
    column = lax.axis_index("col")
    at_x, at_y = column >> 2, column & 3
    slabs = jnp.stack(
        [
            jnp.stack([a + b * 4 for a, b in slots(at_y, at_x)]),
            jnp.stack([a * 4 + b for a, b in slots(at_x, at_y)]),
        ]
    ).astype(jnp.int32)
    facts = jnp.concatenate([slabs.reshape(-1), branch, tile_pattern.reshape(-1)])

    tall = lax.all_gather(density, "row", axis=1, tiled=True)
    low, high = lax.optimization_barrier((density[0], density[1]))
    wide_zero = gather_plane(low, y_by, x_by)
    wide_one = gather_plane(high, x_by, y_by)

    atom_column = orbital_atom.reshape(ROWS, 1)
    overlap = pl.pallas_call(
        overlap_kernel,
        out_shape=small((8, LANES)),
        in_specs=[VMEM] * 3,
        out_specs=VMEM,
    )(atom_column, weighted, ovl_deriv)

    purified, sums = pl.pallas_call(
        purify_kernel,
        out_shape=(
            jax.ShapeDtypeStruct((2, ROWS, ROWS), jnp.bfloat16),
            small((8, LANES)),
        ),
        in_specs=[SMEM] + [VMEM] * (2 * PIECES) + [HBM] * 3 + [VMEM] * 2,
        out_specs=(VMEM, VMEM),
        scratch_shapes=[
            pltpu.VMEM((2, SLABS * ROWS, ROWS), jnp.bfloat16),
            pltpu.SemaphoreType.DMA((2, SLABS)),
            pltpu.VMEM((ROWS, ROWS), jnp.float32),
            pltpu.VMEM((2, ROWS, ROWS), jnp.bfloat16),
            pltpu.VMEM((3, ROWS, ROWS), jnp.bfloat16),
            pltpu.SemaphoreType.DMA((2,)),
        ],
        compiler_params=PARAMS,
        cost_estimate=COST,
    )(
        facts,
        *wide_zero,
        *wide_one,
        tall,
        density,
        ham_deriv,
        atom_column,
        overlap,
    )

    for swap in (x_swap(1), x_swap(2), y_swap(1)):
        sums = sums + send(sums, swap)
    mass_row = masses[None, :]
    forces, sums, norms = pl.pallas_call(
        norm_kernel,
        out_shape=(small(positions.shape), small((8, LANES)), small((8, LANES))),
        in_specs=[VMEM] * 4,
        out_specs=(VMEM, VMEM, VMEM),
    )(sums, send(sums, y_swap(2)), velocities, mass_row)
    for swap in (core_swap(), z_swap(1), z_swap(2)):
        norms = norms + send(norms, swap)
    new_velocities, new_positions = pl.pallas_call(
        update_kernel,
        out_shape=(small(positions.shape), small(positions.shape)),
        in_specs=[VMEM] * 6,
        out_specs=(VMEM, VMEM),
    )(norms, send(norms, z_swap(4)), sums, positions, velocities, mass_row)
    return (purified, forces, new_velocities, new_positions)


def solution(mesh):
    in_specs = (
        P(None, "row", "col"),
        P("row", "col"),
        P(None, "row", "col"),
        P(None, "row", "col"),
        P("row", "col"),
        P(),
        P("row", None),
        P(None, "row"),
        P(None, "row"),
        P("row"),
    )
    out_specs = (P(None, "row", "col"), P(None, "row"), P(None, "row"), P(None, "row"))
    return jax.shard_map(local, mesh=mesh, in_specs=in_specs, out_specs=out_specs, check_vma=False)
```

time: 252 us -> 151 us (0.60)
  waiting for transfers between devices: 155 us -> 61.9 us
  blocking collectives: 64.1 us -> 0 us
  starting transfers between devices: 0.08 us -> 46.3 us
  Pallas kernels: 0 us -> 15.5 us
  matrix products: 14.6 us -> 0 us
  local copies, waits for them, and re-layouts: 0.66 us -> 10.2 us
    all_gather x2 -> x1, waiting for transfers between devices: 154 us -> 0.01 us  [local(): tall = lax.all_gather(density, 'row', axis=1, tiled=True)]
    psum x2 -> x0, blocking collectives: 64.1 us -> none  [the longest x1 33.2 us: local(): forces = lax.psum(local_forces, 'col')]
    ppermute x0 -> x26, waiting for transfers between devices: none -> 61.2 us  [send(): return lax.ppermute(value, AXES, table)]
    ppermute x0 -> x26, starting transfers between devices: none -> 46.2 us  [send(): return lax.ppermute(value, AXES, table)]
    pallas_call x0 -> x4, Pallas kernels: none -> 15.5 us  [the longest x1 10.5 us: local(): pl.pallas_call(purify_kernel, out_shape=(jax.ShapeDtypeStruct((2, ROWS, R...]
    dot_general x4 -> x0, matrix products: 14.6 us -> none  [the longest x1 11.3 us: local(): jnp.einsum('smk,skn->smn', gathered, lax.all_gather(density, 'row', axis=...]
    unnamed x23 -> x20, local copies, waits for them, and re-layouts: 0.49 us -> 6.55 us
  transfers between devices with their start and end apart: 2 -> 27, of which waited for: 2 -> 16; matrix products, arithmetic and copies ran while one was open for 1% -> 3% of each run, Pallas kernels for 0% -> 2%
where the time goes in v2:
time: 151 us; the launch traced here: 150 us
  waiting for transfers between devices  61.9 us (41%)
  starting transfers between devices  46.3 us (31%)
  Pallas kernels  15.5 us (10%)
  between operations  14.1 us (9%)
  local copies, waits for them, and re-layouts  10.2 us (7%)
  other arithmetic  1.69 us (1%)
    ppermute x26, waiting for transfers between devices, send(): return lax.ppermute(value, AXES, table)  61.2 us
    ppermute x26, starting transfers between devices, send(): return lax.ppermute(value, AXES, table)  46.2 us
    pallas_call x1, Pallas kernels, local(): pl.pallas_call(purify_kernel, out_shape=(jax.ShapeDtypeStruct((2, ROWS, R...  10.5 us
    unnamed x20, local copies, waits for them, and re-layouts  6.55 us
  transfers between devices with their start and end apart: 27, of which 16 were waited for; matrix products, arithmetic and copies ran while one was open for 3% of the time, Pallas kernels for 2%

profile of v2, /device:TPU:1, one launch (start us, length us, event | category | flops | bytes accessed | tf_op | source)
XLA Modules:
  0.0 149.8 jit_solution(2087446140277581970)
XLA Ops:
  9.0 2.1 %collective-permute-start.9 = (bf16[384,384]{1,0:T(8,128)(2,1)S(1)}, bf16[384,384]{1,0:T(8,128)(2,1)S(1)}, u32[]{:S(2)}, u32[]{:S(2)}) collective-permute-start(bf16[384,384]{1,0:T(8,128)(2,1)S(1)} %get-tuple-element.14), channel_id=1, source_target_pairs={{0,4},{1,5},{2,6},{3,7},{4,8},{5,9},{6,10},{7,11},{8,12},{9,13},{1... | collective-permute-start | bytes 884744 | tf_op jit(solution)/shard_map/ppermute | solution.py:59
  11.1 2.5 %collective-permute-start.14 = (bf16[384,384]{1,0:T(8,128)(2,1)S(1)}, bf16[384,384]{1,0:T(8,128)(2,1)S(1)}, u32[]{:S(2)}, u32[]{:S(2)}) collective-permute-start(bf16[384,384]{1,0:T(8,128)(2,1)S(1)} %get-tuple-element.14), channel_id=1, source_target_pairs={{0,8},{1,9},{2,10},{3,11},{4,12},{5,13},{6,14},{7,15},{8,0},{9,1},... | collective-permute-start | bytes 884744 | tf_op jit(solution)/shard_map/ppermute | solution.py:59
  14.7 2.1 %collective-permute-done.9 = bf16[384,384]{1,0:T(8,128)(2,1)S(1)} collective-permute-done((bf16[384,384]{1,0:T(8,128)(2,1)S(1)}, bf16[384,384]{1,0:T(8,128)(2,1)S(1)}, u32[]{:S(2)}, u32[]{:S(2)}) %collective-permute-start.9) | collective-permute-done | bytes 294944 | tf_op jit(solution)/shard_map/ppermute | solution.py:59
  16.9 5.0 %collective-permute-start.11 = (bf16[2,384,384]{2,1,0:T(8,128)(2,1)S(1)}, bf16[2,384,384]{2,1,0:T(8,128)(2,1)S(1)}, u32[]{:S(2)}, u32[]{:S(2)}) collective-permute-start(bf16[2,384,384]{2,1,0:T(8,128)(2,1)S(1)} %pad_maximum_fusion.2.rest_8_), channel_id=1, source_target_pairs={{0,3},{1,0},{2,1},{3,2},{4,7},{5,4},{6,5},{7,6},{8,11},{9,8},{10,9... | collective-permute-start | bytes 1769480 | tf_op jit(solution)/shard_map/ppermute | solution.py:59
  21.9 4.4 %collective-permute-done.14 = bf16[384,384]{1,0:T(8,128)(2,1)S(1)} collective-permute-done((bf16[384,384]{1,0:T(8,128)(2,1)S(1)}, bf16[384,384]{1,0:T(8,128)(2,1)S(1)}, u32[]{:S(2)}, u32[]{:S(2)}) %collective-permute-start.14) | collective-permute-done | bytes 294944 | tf_op jit(solution)/shard_map/ppermute | solution.py:59
  26.3 2.9 %collective-permute-start.5 = (bf16[384,384]{1,0:T(8,128)(2,1)S(1)}, bf16[384,384]{1,0:T(8,128)(2,1)S(1)}, u32[]{:S(2)}, u32[]{:S(2)}) collective-permute-start(bf16[384,384]{1,0:T(8,128)(2,1)S(1)} %get-tuple-element.13), channel_id=1, source_target_pairs={{0,2},{1,3},{2,0},{3,1},{4,6},{5,7},{6,4},{7,5},{8,10},{9,11},{10,... | collective-permute-start | bytes 884744 | tf_op jit(solution)/shard_map/ppermute | solution.py:59
  30.1 13.3 %collective-permute-done = bf16[384,384]{1,0:T(8,128)(2,1)S(1)} collective-permute-done((bf16[384,384]{1,0:T(8,128)(2,1)S(1)}, bf16[384,384]{1,0:T(8,128)(2,1)S(1)}, u32[]{:S(2)}, u32[]{:S(2)}) %collective-permute-start) | collective-permute-done | bytes 294944 | tf_op jit(solution)/shard_map/ppermute | solution.py:59
  43.5 4.1 %collective-permute-done.5 = bf16[384,384]{1,0:T(8,128)(2,1)S(1)} collective-permute-done((bf16[384,384]{1,0:T(8,128)(2,1)S(1)}, bf16[384,384]{1,0:T(8,128)(2,1)S(1)}, u32[]{:S(2)}, u32[]{:S(2)}) %collective-permute-start.5) | collective-permute-done | bytes 294944 | tf_op jit(solution)/shard_map/ppermute | solution.py:59
  50.5 5.3 %collective-permute-done.16.rest_14_ = bf16[2,384,384]{2,1,0:T(8,128)(2,1)} collective-permute-done((bf16[2,384,384]{2,1,0:T(8,128)(2,1)S(1)}, bf16[2,384,384]{2,1,0:T(8,128)(2,1)}, u32[]{:S(2)}, u32[]{:S(2)}) %collective-permute-start.16) | collective-permute-done | bytes 589856 | tf_op jit(solution)/shard_map/ppermute | solution.py:59
  55.8 3.9 %collective-permute-done.15.rest_13_ = bf16[2,384,384]{2,1,0:T(8,128)(2,1)S(1)} collective-permute-done((bf16[2,384,384]{2,1,0:T(8,128)(2,1)S(1)}, bf16[2,384,384]{2,1,0:T(8,128)(2,1)S(1)}, u32[]{:S(2)}, u32[]{:S(2)}) %collective-permute-start.15) | collective-permute-done | bytes 589856 | tf_op jit(solution)/shard_map/ppermute | solution.py:59
  61.3 2.7 %collective-permute-start.17 = (bf16[2,384,384]{2,1,0:T(8,128)(2,1)}, bf16[2,384,384]{2,1,0:T(8,128)(2,1)}, u32[]{:S(2)}, u32[]{:S(2)}) collective-permute-start(bf16[2,384,384]{2,1,0:T(8,128)(2,1)} %collective-permute-done.16.rest_14_), channel_id=1, source_target_pairs={{0,3},{1,0},{2,1},{3,2},{4,7},{5,4},{6,5},{7,6},{8,11},{9,8},{10,9... | collective-permute-start | bytes 1769480 | tf_op jit(solution)/shard_map/ppermute | solution.py:59
  64.0 5.1 %collective-permute-done.7.rest_6_ = bf16[2,384,384]{2,1,0:T(8,128)(2,1)} collective-permute-done((bf16[2,384,384]{2,1,0:T(8,128)(2,1)S(1)}, bf16[2,384,384]{2,1,0:T(8,128)(2,1)}, u32[]{:S(2)}, u32[]{:S(2)}) %collective-permute-start.7) | collective-permute-done | bytes 589856 | tf_op jit(solution)/shard_map/ppermute | solution.py:59
  71.7 2.3 %shard_map.129.rest_20_ = f32[8,128]{1,0:T(8,128)} custom-call(s32[384,1]{1,0:T(8,128)} %copy.15.atom_ref.rest_19_, bf16[384,384]{1,0:T(8,128)(2,1)} %weighted_ref.1, bf16[3,384,384]{2,1,0:T(8,128)(2,1)} %ovl_ref.1), custom_call_target="tpu_custom_call" | custom-call | tf_op jit(solution)/shard_map/pallas_call | solution.py:238
  74.7 9.7 %collective-permute-done.3.rest_3_ = bf16[2,384,384]{2,1,0:T(8,128)(2,1)} collective-permute-done((bf16[2,384,384]{2,1,0:T(8,128)(2,1)}, bf16[2,384,384]{2,1,0:T(8,128)(2,1)}, u32[]{:S(2)}, u32[]{:S(2)}) %collective-permute-start.3) | collective-permute-done | bytes 589856 | tf_op jit(solution)/shard_map/ppermute | solution.py:59
  88.2 10.5 %shard_map.130 = (bf16[2,384,384]{2,1,0:T(8,128)(2,1)}, f32[8,128]{1,0:T(8,128)S(1)}) custom-call(s32[43]{0:T(128)S(1)} %pad_add_fusion.1.facts_ref, bf16[2,384,384]{2,1,0:T(8,128)(2,1)S(1)} %pad_maximum_fusion.rest_0_, bf16[2,384,384]{2,1,0:T(8,128)(2,1)} %collective-permute-done.1.rest_1_, bf16[2,384,384]{2,1,0:T(8,128)(2,1)S(1)} %copy-done.4, ...), custom_call_target="tpu_custom_call" | custom-call | flops 3623878656 | bytes 18874368 | tf_op jit(solution)/shard_map/pallas_call | solution.py:245
  98.7 2.4 %collective-permute-done.18 = f32[8,128]{1,0:T(8,128)S(1)} collective-permute-done((f32[8,128]{1,0:T(8,128)S(1)}, f32[8,128]{1,0:T(8,128)S(1)}, u32[]{:S(2)}, u32[]{:S(2)}) %collective-permute-start.18) | collective-permute-done | bytes 4128 | tf_op jit(solution)/shard_map/ppermute | solution.py:59
  101.3 3.8 %collective-permute-done.19 = f32[8,128]{1,0:T(8,128)S(1)} collective-permute-done((f32[8,128]{1,0:T(8,128)S(1)}, f32[8,128]{1,0:T(8,128)S(1)}, u32[]{:S(2)}, u32[]{:S(2)}) %collective-permute-start.19) | collective-permute-done | bytes 4128 | tf_op jit(solution)/shard_map/ppermute | solution.py:59
  105.2 3.9 %collective-permute-start.20 = (f32[8,128]{1,0:T(8,128)S(1)}, f32[8,128]{1,0:T(8,128)S(1)}, u32[]{:S(2)}, u32[]{:S(2)}) collective-permute-start(f32[8,128]{1,0:T(8,128)S(1)} %add.79), channel_id=1, source_target_pairs={{0,1},{1,0},{2,3},{3,2},{4,5},{5,4},{6,7},{7,6},{8,9},{9,8},{10,11... | collective-permute-start | bytes 12296 | tf_op jit(solution)/shard_map/ppermute | solution.py:59
  110.0 2.0 %collective-permute-start.21 = (f32[8,128]{1,0:T(8,128)S(1)}, f32[8,128]{1,0:T(8,128)S(1)}, u32[]{:S(2)}, u32[]{:S(2)}) collective-permute-start(f32[8,128]{1,0:T(8,128)S(1)} %add.80.one_ref), channel_id=1, source_target_pairs={{0,2},{1,3},{2,0},{3,1},{4,6},{5,7},{6,4},{7,5},{8,10},{9,11},{10,... | collective-permute-start | bytes 12296 | tf_op jit(solution)/shard_map/ppermute | solution.py:59
  112.1 2.0 %collective-permute-done.21.two_ref = f32[8,128]{1,0:T(8,128)S(1)} collective-permute-done((f32[8,128]{1,0:T(8,128)S(1)}, f32[8,128]{1,0:T(8,128)S(1)}, u32[]{:S(2)}, u32[]{:S(2)}) %collective-permute-start.21) | collective-permute-done | bytes 4128 | tf_op jit(solution)/shard_map/ppermute | solution.py:59
  116.0 9.5 %collective-permute-start.22 = (f32[8,128]{1,0:T(8,128)}, f32[8,128]{1,0:T(8,128)S(1)}, u32[]{:S(2)}, u32[]{:S(2)}) collective-permute-start(f32[8,128]{1,0:T(8,128)} %get-tuple-element.18), channel_id=1, source_target_pairs={{0,16},{1,17},{2,18},{3,19},{4,20},{5,21},{6,22},{7,23},{8,24},{9,... | collective-permute-start | bytes 12296 | tf_op jit(solution)/shard_map/ppermute | solution.py:59
  127.2 1.6 %collective-permute-start.23 = (f32[8,128]{1,0:T(8,128)S(1)}, f32[8,128]{1,0:T(8,128)S(1)}, u32[]{:S(2)}, u32[]{:S(2)}) collective-permute-start(f32[8,128]{1,0:T(8,128)S(1)} %add.81), channel_id=1, source_target_pairs={{0,32},{1,33},{2,34},{3,35},{4,36},{5,37},{6,38},{7,39},{8,40},{9,... | collective-permute-start | bytes 12296 | tf_op jit(solution)/shard_map/ppermute | solution.py:59
  129.9 3.0 %collective-permute-start.24 = (f32[8,128]{1,0:T(8,128)S(1)}, f32[8,128]{1,0:T(8,128)S(1)}, u32[]{:S(2)}, u32[]{:S(2)}) collective-permute-start(f32[8,128]{1,0:T(8,128)S(1)} %add.82), channel_id=1, source_target_pairs={{0,64},{1,65},{2,66},{3,67},{4,68},{5,69},{6,70},{7,71},{8,72},{9,... | collective-permute-start | bytes 12296 | tf_op jit(solution)/shard_map/ppermute | solution.py:59
  133.9 6.1 %collective-permute-start.25 = (f32[8,128]{1,0:T(8,128)S(1)}, f32[8,128]{1,0:T(8,128)S(1)}, u32[]{:S(2)}, u32[]{:S(2)}) collective-permute-start(f32[8,128]{1,0:T(8,128)S(1)} %add.83.one_ref), channel_id=1, source_target_pairs={{0,128},{1,129},{2,130},{3,131},{4,132},{5,133},{6,134},{7,135},{8... | collective-permute-start | bytes 12296 | tf_op jit(solution)/shard_map/ppermute | solution.py:59
  (73 shorter events, 25.4 us)
Async XLA Ops:
  7.2 77.3 %all-gather.2.cloned.1.call-start = ((), (), s32[]{:S(2)}) async-start(), calls=%async_computation | async-start | bytes 10027008 | tf_op jit(solution)/shard_map/all_gather | solution.py:232
  9.0 7.8 %collective-permute-start.9 = (bf16[384,384]{1,0:T(8,128)(2,1)S(1)}, bf16[384,384]{1,0:T(8,128)(2,1)S(1)}, u32[]{:S(2)}, u32[]{:S(2)}) collective-permute-start(bf16[384,384]{1,0:T(8,128)(2,1)S(1)} %get-tuple-element.14), channel_id=1, source_target_pairs={{0,4},{1,5},{2,6},{3,7},{4,8},{5,9},{6,10},{7,11},{8,12},{9,13},{1... | collective-permute-start | bytes 884744 | tf_op jit(solution)/shard_map/ppermute | solution.py:59
  11.1 15.2 %collective-permute-start.14 = (bf16[384,384]{1,0:T(8,128)(2,1)S(1)}, bf16[384,384]{1,0:T(8,128)(2,1)S(1)}, u32[]{:S(2)}, u32[]{:S(2)}) collective-permute-start(bf16[384,384]{1,0:T(8,128)(2,1)S(1)} %get-tuple-element.14), channel_id=1, source_target_pairs={{0,8},{1,9},{2,10},{3,11},{4,12},{5,13},{6,14},{7,15},{8,0},{9,1},... | collective-permute-start | bytes 884744 | tf_op jit(solution)/shard_map/ppermute | solution.py:59
  13.6 15.6 %collective-permute-start.13 = (bf16[384,384]{1,0:T(8,128)(2,1)S(1)}, bf16[384,384]{1,0:T(8,128)(2,1)S(1)}, u32[]{:S(2)}, u32[]{:S(2)}) collective-permute-start(bf16[384,384]{1,0:T(8,128)(2,1)S(1)} %get-tuple-element.14), channel_id=1, source_target_pairs={{0,12},{1,13},{2,14},{3,15},{4,0},{5,1},{6,2},{7,3},{8,4},{9,5},{1... | collective-permute-start | bytes 884744 | tf_op jit(solution)/shard_map/ppermute | solution.py:59
  16.9 30.8 %collective-permute-start.11 = (bf16[2,384,384]{2,1,0:T(8,128)(2,1)S(1)}, bf16[2,384,384]{2,1,0:T(8,128)(2,1)S(1)}, u32[]{:S(2)}, u32[]{:S(2)}) collective-permute-start(bf16[2,384,384]{2,1,0:T(8,128)(2,1)S(1)} %pad_maximum_fusion.2.rest_8_), channel_id=1, source_target_pairs={{0,3},{1,0},{2,1},{3,2},{4,7},{5,4},{6,5},{7,6},{8,11},{9,8},{10,9... | collective-permute-start | bytes 1769480 | tf_op jit(solution)/shard_map/ppermute | solution.py:59
  21.9 27.3 %collective-permute-start.10 = (bf16[2,384,384]{2,1,0:T(8,128)(2,1)S(1)}, bf16[2,384,384]{2,1,0:T(8,128)(2,1)S(1)}, u32[]{:S(2)}, u32[]{:S(2)}) collective-permute-start(bf16[2,384,384]{2,1,0:T(8,128)(2,1)S(1)} %pad_maximum_fusion.2.rest_8_), channel_id=1, source_target_pairs={{0,1},{1,2},{2,3},{3,0},{4,5},{5,6},{6,7},{7,4},{8,9},{9,10},{10,1... | collective-permute-start | bytes 1769480 | tf_op jit(solution)/shard_map/ppermute | solution.py:59
  21.9 21.5 %collective-permute-start = (bf16[384,384]{1,0:T(8,128)(2,1)S(1)}, bf16[384,384]{1,0:T(8,128)(2,1)S(1)}, u32[]{:S(2)}, u32[]{:S(2)}) collective-permute-start(bf16[384,384]{1,0:T(8,128)(2,1)S(1)} %get-tuple-element.13), channel_id=1, source_target_pairs={{0,1},{1,2},{2,3},{3,0},{4,5},{5,6},{6,7},{7,4},{8,9},{9,10},{10,1... | collective-permute-start | bytes 884744 | tf_op jit(solution)/shard_map/ppermute | solution.py:59
  26.3 21.3 %collective-permute-start.5 = (bf16[384,384]{1,0:T(8,128)(2,1)S(1)}, bf16[384,384]{1,0:T(8,128)(2,1)S(1)}, u32[]{:S(2)}, u32[]{:S(2)}) collective-permute-start(bf16[384,384]{1,0:T(8,128)(2,1)S(1)} %get-tuple-element.13), channel_id=1, source_target_pairs={{0,2},{1,3},{2,0},{3,1},{4,6},{5,7},{6,4},{7,5},{8,10},{9,11},{10,... | collective-permute-start | bytes 884744 | tf_op jit(solution)/shard_map/ppermute | solution.py:59
  29.2 18.4 %collective-permute-start.4 = (bf16[384,384]{1,0:T(8,128)(2,1)S(1)}, bf16[384,384]{1,0:T(8,128)(2,1)S(1)}, u32[]{:S(2)}, u32[]{:S(2)}) collective-permute-start(bf16[384,384]{1,0:T(8,128)(2,1)S(1)} %get-tuple-element.13), channel_id=1, source_target_pairs={{0,3},{1,0},{2,1},{3,2},{4,7},{5,4},{6,5},{7,6},{8,11},{9,8},{10,9... | collective-permute-start | bytes 884744 | tf_op jit(solution)/shard_map/ppermute | solution.py:59
  43.4 12.4 %collective-permute-start.16 = (bf16[2,384,384]{2,1,0:T(8,128)(2,1)S(1)}, bf16[2,384,384]{2,1,0:T(8,128)(2,1)}, u32[]{:S(2)}, u32[]{:S(2)}) collective-permute-start(bf16[2,384,384]{2,1,0:T(8,128)(2,1)S(1)} %pad_maximum_fusion.3.rest_12_), channel_id=1, source_target_pairs={{0,3},{1,0},{2,1},{3,2},{4,7},{5,4},{6,5},{7,6},{8,11},{9,8},{10,9... | collective-permute-start | bytes 1769480 | tf_op jit(solution)/shard_map/ppermute | solution.py:59
  47.6 12.1 %collective-permute-start.15 = (bf16[2,384,384]{2,1,0:T(8,128)(2,1)S(1)}, bf16[2,384,384]{2,1,0:T(8,128)(2,1)S(1)}, u32[]{:S(2)}, u32[]{:S(2)}) collective-permute-start(bf16[2,384,384]{2,1,0:T(8,128)(2,1)S(1)} %pad_maximum_fusion.3.rest_12_), channel_id=1, source_target_pairs={{0,1},{1,2},{2,3},{3,0},{4,5},{5,6},{6,7},{7,4},{8,9},{9,10},{10,1... | collective-permute-start | bytes 1769480 | tf_op jit(solution)/shard_map/ppermute | solution.py:59
  47.6 12.9 %collective-permute-start.2 = (bf16[2,384,384]{2,1,0:T(8,128)(2,1)S(1)}, bf16[2,384,384]{2,1,0:T(8,128)(2,1)S(1)}, u32[]{:S(2)}, u32[]{:S(2)}) collective-permute-start(bf16[2,384,384]{2,1,0:T(8,128)(2,1)S(1)} %pad_maximum_fusion.rest_0_), channel_id=1, source_target_pairs={{0,12},{1,13},{2,14},{3,15},{4,0},{5,1},{6,2},{7,3},{8,4},{9,5},{1... | collective-permute-start | bytes 1769480 | tf_op jit(solution)/shard_map/ppermute | solution.py:59
  47.7 16.3 %collective-permute-start.1 = (bf16[2,384,384]{2,1,0:T(8,128)(2,1)S(1)}, bf16[2,384,384]{2,1,0:T(8,128)(2,1)}, u32[]{:S(2)}, u32[]{:S(2)}) collective-permute-start(bf16[2,384,384]{2,1,0:T(8,128)(2,1)S(1)} %pad_maximum_fusion.rest_0_), channel_id=1, source_target_pairs={{0,4},{1,5},{2,6},{3,7},{4,8},{5,9},{6,10},{7,11},{8,12},{9,13},{1... | collective-permute-start | bytes 1769480 | tf_op jit(solution)/shard_map/ppermute | solution.py:59
  49.2 19.9 %collective-permute-start.7 = (bf16[2,384,384]{2,1,0:T(8,128)(2,1)S(1)}, bf16[2,384,384]{2,1,0:T(8,128)(2,1)}, u32[]{:S(2)}, u32[]{:S(2)}) collective-permute-start(bf16[2,384,384]{2,1,0:T(8,128)(2,1)S(1)} %pad_maximum_fusion.1.rest_4_), channel_id=1, source_target_pairs={{0,12},{1,13},{2,14},{3,15},{4,0},{5,1},{6,2},{7,3},{8,4},{9,5},{1... | collective-permute-start | bytes 1769480 | tf_op jit(solution)/shard_map/ppermute | solution.py:59
  55.8 18.9 %collective-permute-start.6 = (bf16[2,384,384]{2,1,0:T(8,128)(2,1)S(1)}, bf16[2,384,384]{2,1,0:T(8,128)(2,1)}, u32[]{:S(2)}, u32[]{:S(2)}) collective-permute-start(bf16[2,384,384]{2,1,0:T(8,128)(2,1)S(1)} %pad_maximum_fusion.1.rest_4_), channel_id=1, source_target_pairs={{0,4},{1,5},{2,6},{3,7},{4,8},{5,9},{6,10},{7,11},{8,12},{9,13},{1... | collective-permute-start | bytes 1769480 | tf_op jit(solution)/shard_map/ppermute | solution.py:59
  60.5 14.2 %collective-permute-start.12 = (bf16[2,384,384]{2,1,0:T(8,128)(2,1)S(1)}, bf16[2,384,384]{2,1,0:T(8,128)(2,1)}, u32[]{:S(2)}, u32[]{:S(2)}) collective-permute-start(bf16[2,384,384]{2,1,0:T(8,128)(2,1)S(1)} %collective-permute-done.10.rest_9_), channel_id=1, source_target_pairs={{0,1},{1,2},{2,3},{3,0},{4,5},{5,6},{6,7},{7,4},{8,9},{9,10},{10,1... | collective-permute-start | bytes 1769480 | tf_op jit(solution)/shard_map/ppermute | solution.py:59
  61.3 13.4 %collective-permute-start.17 = (bf16[2,384,384]{2,1,0:T(8,128)(2,1)}, bf16[2,384,384]{2,1,0:T(8,128)(2,1)}, u32[]{:S(2)}, u32[]{:S(2)}) collective-permute-start(bf16[2,384,384]{2,1,0:T(8,128)(2,1)} %collective-permute-done.16.rest_14_), channel_id=1, source_target_pairs={{0,3},{1,0},{2,1},{3,2},{4,7},{5,4},{6,5},{7,6},{8,11},{9,8},{10,9... | collective-permute-start | bytes 1769480 | tf_op jit(solution)/shard_map/ppermute | solution.py:59
  64.0 20.4 %collective-permute-start.3 = (bf16[2,384,384]{2,1,0:T(8,128)(2,1)}, bf16[2,384,384]{2,1,0:T(8,128)(2,1)}, u32[]{:S(2)}, u32[]{:S(2)}) collective-permute-start(bf16[2,384,384]{2,1,0:T(8,128)(2,1)} %collective-permute-done.1.rest_1_), channel_id=1, source_target_pairs={{0,4},{1,5},{2,6},{3,7},{4,8},{5,9},{6,10},{7,11},{8,12},{9,13},{1... | collective-permute-start | bytes 1769480 | tf_op jit(solution)/shard_map/ppermute | solution.py:59
  69.1 15.3 %collective-permute-start.8 = (bf16[2,384,384]{2,1,0:T(8,128)(2,1)}, bf16[2,384,384]{2,1,0:T(8,128)(2,1)}, u32[]{:S(2)}, u32[]{:S(2)}) collective-permute-start(bf16[2,384,384]{2,1,0:T(8,128)(2,1)} %collective-permute-done.7.rest_6_), channel_id=1, source_target_pairs={{0,12},{1,13},{2,14},{3,15},{4,0},{5,1},{6,2},{7,3},{8,4},{9,5},{1... | collective-permute-start | bytes 1769480 | tf_op jit(solution)/shard_map/ppermute | solution.py:59
  101.2 4.0 %collective-permute-start.19 = (f32[8,128]{1,0:T(8,128)S(1)}, f32[8,128]{1,0:T(8,128)S(1)}, u32[]{:S(2)}, u32[]{:S(2)}) collective-permute-start(f32[8,128]{1,0:T(8,128)S(1)} %add.78), channel_id=1, source_target_pairs={{0,8},{1,9},{2,10},{3,11},{4,12},{5,13},{6,14},{7,15},{8,0},{9,1},... | collective-permute-start | bytes 12296 | tf_op jit(solution)/shard_map/ppermute | solution.py:59
  105.2 4.9 %collective-permute-start.20 = (f32[8,128]{1,0:T(8,128)S(1)}, f32[8,128]{1,0:T(8,128)S(1)}, u32[]{:S(2)}, u32[]{:S(2)}) collective-permute-start(f32[8,128]{1,0:T(8,128)S(1)} %add.79), channel_id=1, source_target_pairs={{0,1},{1,0},{2,3},{3,2},{4,5},{5,4},{6,7},{7,6},{8,9},{9,8},{10,11... | collective-permute-start | bytes 12296 | tf_op jit(solution)/shard_map/ppermute | solution.py:59
  116.0 10.5 %collective-permute-start.22 = (f32[8,128]{1,0:T(8,128)}, f32[8,128]{1,0:T(8,128)S(1)}, u32[]{:S(2)}, u32[]{:S(2)}) collective-permute-start(f32[8,128]{1,0:T(8,128)} %get-tuple-element.18), channel_id=1, source_target_pairs={{0,16},{1,17},{2,18},{3,19},{4,20},{5,21},{6,22},{7,23},{8,24},{9,... | collective-permute-start | bytes 12296 | tf_op jit(solution)/shard_map/ppermute | solution.py:59
  129.9 4.0 %collective-permute-start.24 = (f32[8,128]{1,0:T(8,128)S(1)}, f32[8,128]{1,0:T(8,128)S(1)}, u32[]{:S(2)}, u32[]{:S(2)}) collective-permute-start(f32[8,128]{1,0:T(8,128)S(1)} %add.82), channel_id=1, source_target_pairs={{0,64},{1,65},{2,66},{3,67},{4,68},{5,69},{6,70},{7,71},{8,72},{9,... | collective-permute-start | bytes 12296 | tf_op jit(solution)/shard_map/ppermute | solution.py:59
  133.9 7.1 %collective-permute-start.25 = (f32[8,128]{1,0:T(8,128)S(1)}, f32[8,128]{1,0:T(8,128)S(1)}, u32[]{:S(2)}, u32[]{:S(2)}) collective-permute-start(f32[8,128]{1,0:T(8,128)S(1)} %add.83.one_ref), channel_id=1, source_target_pairs={{0,128},{1,129},{2,130},{3,131},{4,132},{5,133},{6,134},{7,135},{8... | collective-permute-start | bytes 12296 | tf_op jit(solution)/shard_map/ppermute | solution.py:59
  (13 other events, 26.8 us)
Sparse Core Ops, SparseCore 0:
  9.8 65.0 all-gather.1

commit v3 on v2

--- a/solution.py
+++ b/solution.py
@@ -39,22 +39,6 @@
     return pairs(lambda z, core, x, y: (z, core, x, y + k))
 
 
-def x_swap(bit):
-    return pairs(lambda z, core, x, y: (z, core, x ^ bit, y))
-
-
-def y_swap(bit):
-    return pairs(lambda z, core, x, y: (z, core, x, y ^ bit))
-
-
-def z_swap(bit):
-    return pairs(lambda z, core, x, y: (z ^ bit, core, x, y))
-
-
-def core_swap():
-    return pairs(lambda z, core, x, y: (z, 1 - core, x, y))
-
-
 def send(value, table):
     return lax.ppermute(value, AXES, table)
 
@@ -63,19 +47,16 @@
     one = send(block, first(1))
     two = send(block, first(-1))
     three = send(block, first(2))
-    near = jnp.stack([block, one])
-    ahead_near = send(near, second(1))
-    behind_near = send(near, second(-1))
-    rest = jnp.stack([two, three])
-    ahead_rest = send(rest, second(1))
-    behind_rest = send(rest, second(-1))
-    far_near = send(ahead_near, second(1))
-    far_rest = send(behind_rest, second(-1))
-    return (near, ahead_near, behind_near, far_near, rest, ahead_rest, behind_rest, far_rest)
+    line = jnp.stack([block, one, two, three])
+    ahead = send(line, second(1))
+    behind = send(line, second(-1))
+    far_low = send(ahead[:2], second(1))
+    far_high = send(behind[2:], second(-1))
+    return (line, ahead, behind, far_low, far_high)
 
 
 def slots(first_at, second_at):
-    order = [(a, b) for line in ((0, -1), (1, 2)) for b in (0, -1, 1, 2) for a in line]
+    order = [(a, b) for b in (0, -1, 1, 2) for a in (0, -1, 1, 2)]
     return [((first_at + a) & 3, (second_at + b) & 3) for a, b in order]
 
 
@@ -99,7 +80,7 @@
         out_ref[x : x + 1, :] = 2.0 * rows[x]
 
 
-PIECES = 8
+PIECES = 5
 GROUPS = 4
 
 
@@ -136,7 +117,10 @@
         for group in range(GROUPS):
             for copy in copies[spin * SLABS + group * each : spin * SLABS + (group + 1) * each]:
                 copy.wait()
-            slabs = [wide[spin][group * each // 2 + i][j] for i in range(each // 2) for j in range(2)]
+            if group < 3:
+                slabs = [wide[spin][group][i] for i in range(4)]
+            else:
+                slabs = [wide[spin][3][0], wide[spin][3][1], wide[spin][4][0], wide[spin][4][1]]
             product = jnp.dot(
                 jnp.concatenate(slabs, axis=1),
                 b_buf[spin, pl.ds(group * each * ROWS, each * ROWS), :],
@@ -159,26 +143,33 @@
     both = out_ref[0].astype(jnp.float32) + out_ref[1].astype(jnp.float32)
     ham_copy.wait()
     rows = terms_of(both, ham_ref, one_hot_of(atom_ref))
-    sums_ref[...] = overlap_ref[...]
+    terms = overlap_ref[...]
+    lines = lax.broadcasted_iota(jnp.int32, (8, LANES), 0)
     for x in range(3):
-        sums_ref[x : x + 1, :] += -2.0 * rows[x]
-
-
-def norm_kernel(one_ref, two_ref, velocities_ref, masses_ref, forces_ref, sums_ref, norms_ref):
-    sums = one_ref[...] + two_ref[...]
+        terms = jnp.where(lines == x, terms - 2.0 * rows[x], terms)
+    for part in range(SLABS):
+        sums_ref[part] = terms
+
+
+def norm_kernel(parts_ref, velocities_ref, masses_ref, forces_ref, sums_ref, norms_ref):
+    sums = parts_ref[0]
+    for part in range(1, parts_ref.shape[0]):
+        sums = sums + parts_ref[part]
     forces = sums[:3, : forces_ref.shape[1]]
     forces_ref[...] = forces
     sums_ref[...] = sums
     scaled = forces / jnp.sqrt(masses_ref[...])
     speeds = velocities_ref[...]
-    rows = lax.broadcasted_iota(jnp.int32, norms_ref.shape, 0)
+    rows = lax.broadcasted_iota(jnp.int32, norms_ref.shape, 1)
     norms_ref[...] = jnp.where(rows == 0, jnp.sum(scaled * scaled), jnp.sum(speeds * speeds))
 
 
 def update_kernel(
-    one_ref, two_ref, sums_ref, positions_ref, velocities_ref, masses_ref, speeds_ref, places_ref
+    parts_ref, sums_ref, positions_ref, velocities_ref, masses_ref, speeds_ref, places_ref
 ):
-    norms = one_ref[...] + two_ref[...]
+    norms = parts_ref[0]
+    for part in range(1, parts_ref.shape[0]):
+        norms = norms + parts_ref[part]
     force_norm, speed_norm = norms[0:1, 0:1], norms[1:2, 0:1]
     root_mass = jnp.sqrt(masses_ref[...])
     scaled = sums_ref[:3, : speeds_ref.shape[1]] / root_mass
@@ -201,6 +192,9 @@
     transcendentals=0,
 )
 PARAMS = pltpu.CompilerParams(vmem_limit_bytes=45 * 1024 * 1024)
+
+
+LITTLE = pltpu.CompilerParams(vmem_limit_bytes=2 * 1024 * 1024)
 
 
 def small(shape):
@@ -240,13 +234,14 @@
         out_shape=small((8, LANES)),
         in_specs=[VMEM] * 3,
         out_specs=VMEM,
+        compiler_params=pltpu.CompilerParams(vmem_limit_bytes=4 * 1024 * 1024),
     )(atom_column, weighted, ovl_deriv)
 
     purified, sums = pl.pallas_call(
         purify_kernel,
         out_shape=(
             jax.ShapeDtypeStruct((2, ROWS, ROWS), jnp.bfloat16),
-            small((8, LANES)),
+            small((SLABS, 8, LANES)),
         ),
         in_specs=[SMEM] + [VMEM] * (2 * PIECES) + [HBM] * 3 + [VMEM] * 2,
         out_specs=(VMEM, VMEM),
@@ -271,23 +266,23 @@
         overlap,
     )
 
-    for swap in (x_swap(1), x_swap(2), y_swap(1)):
-        sums = sums + send(sums, swap)
+    parts = lax.all_to_all(sums, "col", 0, 0)
     mass_row = masses[None, :]
     forces, sums, norms = pl.pallas_call(
         norm_kernel,
-        out_shape=(small(positions.shape), small((8, LANES)), small((8, LANES))),
-        in_specs=[VMEM] * 4,
+        out_shape=(small(positions.shape), small((8, LANES)), small((SLABS, 8, LANES))),
+        in_specs=[VMEM] * 3,
         out_specs=(VMEM, VMEM, VMEM),
-    )(sums, send(sums, y_swap(2)), velocities, mass_row)
-    for swap in (core_swap(), z_swap(1), z_swap(2)):
-        norms = norms + send(norms, swap)
+        compiler_params=LITTLE,
+    )(parts, velocities, mass_row)
+    parts = lax.all_to_all(norms, "row", 0, 0)
     new_velocities, new_positions = pl.pallas_call(
         update_kernel,
         out_shape=(small(positions.shape), small(positions.shape)),
-        in_specs=[VMEM] * 6,
+        in_specs=[VMEM] * 5,
         out_specs=(VMEM, VMEM),
-    )(norms, send(norms, z_swap(4)), sums, positions, velocities, mass_row)
+        compiler_params=LITTLE,
+    )(parts, sums, positions, velocities, mass_row)
     return (purified, forces, new_velocities, new_positions)
 
 

time: 151 us -> 133 us (0.88)
  blocking collectives: 0 us -> 30.8 us
  starting transfers between devices: 46.3 us -> 22.6 us
  waiting for transfers between devices: 61.9 us -> 41.4 us
  Pallas kernels: 15.5 us -> 12.1 us
    all_to_all x0 -> x2, blocking collectives: none -> 30.8 us  [the longest x1 20.7 us: local(): parts = lax.all_to_all(norms, 'row', 0, 0)]
    ppermute x26 -> x14, starting transfers between devices: 46.2 us -> 22.6 us  [send(): return lax.ppermute(value, AXES, table)]
    ppermute x26 -> x14, waiting for transfers between devices: 61.2 us -> 40.7 us  [send(): return lax.ppermute(value, AXES, table)]
    slice x0 -> x4, local copies, waits for them, and re-layouts: none -> 3.79 us  [the longest x2 1.94 us: gather_plane(): far_low = send(ahead[:2], second(1))]
    pallas_call x1, Pallas kernels: 2.28 us -> 0.3 us  [local(): pl.pallas_call(overlap_kernel, out_shape=small((8, LANES)), in_specs=[VME...]
    unnamed x20 -> x32, local copies, waits for them, and re-layouts: 6.55 us -> 5.29 us
  transfers between devices with their start and end apart: 27 -> 15, of which waited for: 16 -> 8; matrix products, arithmetic and copies ran while one was open for 3% -> 4% of each run, Pallas kernels for 2% -> 0%
where the time goes in v3:
time: 133 us; the launch traced here: 132 us
  waiting for transfers between devices  41.4 us (31%)
  blocking collectives  30.8 us (23%)
  starting transfers between devices  22.6 us (17%)
  between operations  14.2 us (11%)
  Pallas kernels  12.1 us (9%)
  local copies, waits for them, and re-layouts  10.7 us (8%)
    ppermute x14, waiting for transfers between devices, send(): return lax.ppermute(value, AXES, table)  40.7 us
    ppermute x14, starting transfers between devices, send(): return lax.ppermute(value, AXES, table)  22.6 us
    all_to_all x1, blocking collectives, local(): parts = lax.all_to_all(norms, 'row', 0, 0)  20.7 us
    pallas_call x1, Pallas kernels, local(): pl.pallas_call(purify_kernel, out_shape=(jax.ShapeDtypeStruct((2, ROWS, R...  10.5 us
    all_to_all x1, blocking collectives, local(): parts = lax.all_to_all(sums, 'col', 0, 0)  10.1 us
    unnamed x32, local copies, waits for them, and re-layouts  5.29 us
  transfers between devices with their start and end apart: 15, of which 8 were waited for; matrix products, arithmetic and copies ran while one was open for 4% of the time, Pallas kernels for 0%

profile of v3, /device:TPU:1, one launch (start us, length us, event | category | flops | bytes accessed | tf_op | source)
XLA Modules:
  0.0 132.2 jit_solution(919450370088599265)
XLA Ops:
  7.9 1.1 slice_bitcast_fusion
  9.0 3.7 %collective-permute-start.9 = (bf16[384,384]{1,0:T(8,128)(2,1)S(1)}, bf16[384,384]{1,0:T(8,128)(2,1)S(1)}, u32[]{:S(2)}, u32[]{:S(2)}) collective-permute-start(bf16[384,384]{1,0:T(8,128)(2,1)S(1)} %get-tuple-element.14), channel_id=1, source_target_pairs={{0,8},{1,9},{2,10},{3,11},{4,12},{5,13},{6,14},{7,15},{8,0},{9,1},... | collective-permute-start | bytes 884744 | tf_op jit(solution)/shard_map/ppermute | solution.py:43
  14.1 2.9 %collective-permute-start.2 = (bf16[384,384]{1,0:T(8,128)(2,1)S(1)}, bf16[384,384]{1,0:T(8,128)(2,1)S(1)}, u32[]{:S(2)}, u32[]{:S(2)}) collective-permute-start(bf16[384,384]{1,0:T(8,128)(2,1)S(1)} %get-tuple-element.13), channel_id=1, source_target_pairs={{0,2},{1,3},{2,0},{3,1},{4,6},{5,7},{6,4},{7,5},{8,10},{9,11},{10,... | collective-permute-start | bytes 884744 | tf_op jit(solution)/shard_map/ppermute | solution.py:43
  18.4 2.3 %collective-permute-start = (bf16[384,384]{1,0:T(8,128)(2,1)S(1)}, bf16[384,384]{1,0:T(8,128)(2,1)S(1)}, u32[]{:S(2)}, u32[]{:S(2)}) collective-permute-start(bf16[384,384]{1,0:T(8,128)(2,1)S(1)} %get-tuple-element.13), channel_id=1, source_target_pairs={{0,1},{1,2},{2,3},{3,0},{4,5},{5,6},{6,7},{7,4},{8,9},{9,10},{10,1... | collective-permute-start | bytes 884744 | tf_op jit(solution)/shard_map/ppermute | solution.py:43
  20.7 5.1 %collective-permute-done.8 = bf16[384,384]{1,0:T(8,128)(2,1)S(1)} collective-permute-done((bf16[384,384]{1,0:T(8,128)(2,1)S(1)}, bf16[384,384]{1,0:T(8,128)(2,1)S(1)}, u32[]{:S(2)}, u32[]{:S(2)}) %collective-permute-start.8) | collective-permute-done | bytes 294944 | tf_op jit(solution)/shard_map/ppermute | solution.py:43
  26.0 3.7 %collective-permute-start.11 = (bf16[4,384,384]{2,1,0:T(8,128)(2,1)S(1)}, bf16[4,384,384]{2,1,0:T(8,128)(2,1)S(1)}, u32[]{:S(2)}, u32[]{:S(2)}) collective-permute-start(bf16[4,384,384]{2,1,0:T(8,128)(2,1)S(1)} %pad_maximum_fusion.1.rest_5_), channel_id=1, source_target_pairs={{0,3},{1,0},{2,1},{3,2},{4,7},{5,4},{6,5},{7,6},{8,11},{9,8},{10,9... | collective-permute-start | bytes 3538952 | tf_op jit(solution)/shard_map/ppermute | solution.py:43
  30.4 2.1 %collective-permute-start.4 = (bf16[4,384,384]{2,1,0:T(8,128)(2,1)S(1)}, bf16[4,384,384]{2,1,0:T(8,128)(2,1)S(1)}, u32[]{:S(2)}, u32[]{:S(2)}) collective-permute-start(bf16[4,384,384]{2,1,0:T(8,128)(2,1)S(1)} %pad_maximum_fusion.rest_0_), channel_id=1, source_target_pairs={{0,12},{1,13},{2,14},{3,15},{4,0},{5,1},{6,2},{7,3},{8,4},{9,5},{1... | collective-permute-start | bytes 3538952 | tf_op jit(solution)/shard_map/ppermute | solution.py:43
  32.6 22.4 %collective-permute-done.11.rest_7_ = bf16[4,384,384]{2,1,0:T(8,128)(2,1)S(1)} collective-permute-done((bf16[4,384,384]{2,1,0:T(8,128)(2,1)S(1)}, bf16[4,384,384]{2,1,0:T(8,128)(2,1)S(1)}, u32[]{:S(2)}, u32[]{:S(2)}) %collective-permute-start.11) | collective-permute-done | bytes 1179680 | tf_op jit(solution)/shard_map/ppermute | solution.py:43
  54.9 1.0 slice.27
  55.9 3.1 %collective-permute-start.13 = (bf16[2,384,384]{2,1,0:T(8,128)(2,1)}, bf16[2,384,384]{2,1,0:T(8,128)(2,1)}, u32[]{:S(2)}, u32[]{:S(2)}) collective-permute-start(bf16[2,384,384]{2,1,0:T(8,128)(2,1)} %slice.27), channel_id=1, source_target_pairs={{0,3},{1,0},{2,1},{3,2},{4,7},{5,4},{6,5},{7,6},{8,11},{9,8},{10,9... | collective-permute-start | bytes 1769480 | tf_op jit(solution)/shard_map/ppermute | solution.py:43
  59.1 1.0 slice.26
  60.2 0.9 slice.25
  61.1 2.4 %collective-permute-start.6 = (bf16[2,384,384]{2,1,0:T(8,128)(2,1)}, bf16[2,384,384]{2,1,0:T(8,128)(2,1)}, u32[]{:S(2)}, u32[]{:S(2)}) collective-permute-start(bf16[2,384,384]{2,1,0:T(8,128)(2,1)} %slice.25), channel_id=1, source_target_pairs={{0,12},{1,13},{2,14},{3,15},{4,0},{5,1},{6,2},{7,3},{8,4},{9,5},{1... | collective-permute-start | bytes 1769480 | tf_op jit(solution)/shard_map/ppermute | solution.py:43
  63.5 0.9 slice.24
  65.3 1.2 copy-done.5
  67.0 4.3 %collective-permute-done.13.rest_9_ = bf16[2,384,384]{2,1,0:T(8,128)(2,1)} collective-permute-done((bf16[2,384,384]{2,1,0:T(8,128)(2,1)}, bf16[2,384,384]{2,1,0:T(8,128)(2,1)}, u32[]{:S(2)}, u32[]{:S(2)}) %collective-permute-start.13) | collective-permute-done | bytes 589856 | tf_op jit(solution)/shard_map/ppermute | solution.py:43
  71.3 3.6 %collective-permute-done.12.rest_8_ = bf16[2,384,384]{2,1,0:T(8,128)(2,1)} collective-permute-done((bf16[2,384,384]{2,1,0:T(8,128)(2,1)}, bf16[2,384,384]{2,1,0:T(8,128)(2,1)}, u32[]{:S(2)}, u32[]{:S(2)}) %collective-permute-start.12) | collective-permute-done | bytes 589856 | tf_op jit(solution)/shard_map/ppermute | solution.py:43
  75.0 4.1 %collective-permute-done.5.rest_3_ = bf16[2,384,384]{2,1,0:T(8,128)(2,1)} collective-permute-done((bf16[2,384,384]{2,1,0:T(8,128)(2,1)}, bf16[2,384,384]{2,1,0:T(8,128)(2,1)}, u32[]{:S(2)}, u32[]{:S(2)}) %collective-permute-start.5) | collective-permute-done | bytes 589856 | tf_op jit(solution)/shard_map/ppermute | solution.py:43
  79.0 1.3 copy-done.2
  80.3 1.3 copy-done.4
  81.6 1.2 copy-done.6
  82.7 10.5 %shard_map.130 = (bf16[2,384,384]{2,1,0:T(8,128)(2,1)}, f32[16,8,128]{2,1,0:T(8,128)S(1)}) custom-call(s32[43]{0:T(128)S(1)} %pad_add_fusion.1.facts_ref, bf16[4,384,384]{2,1,0:T(8,128)(2,1)S(1)} %pad_maximum_fusion.rest_0_, bf16[4,384,384]{2,1,0:T(8,128)(2,1)S(1)} %copy-done.4, bf16[4,384,384]{2,1,0:T(8,128)(2,1)S(1)} %copy-done.2, ...), custom_call_target="tpu_custom_call" | custom-call | flops 3623878656 | bytes 18874368 | tf_op jit(solution)/shard_map/pallas_call | solution.py:240
  93.3 10.1 %all_to_all.10.parts_ref = f32[16,8,128]{2,1,0:T(8,128)S(1)} all-to-all(f32[16,8,128]{2,1,0:T(8,128)S(1)} %get-tuple-element.16), channel_id=1, replica_groups=mesh['row'=16,'col'=16] {'col'}, dimensions={0} | all-to-all | bytes 131072 | tf_op jit(solution)/shard_map/all_to_all | solution.py:269
  104.0 20.7 %all_to_all.11.parts_ref = f32[16,8,128]{2,1,0:T(8,128)S(1)} all-to-all(f32[16,8,128]{2,1,0:T(8,128)S(1)} %get-tuple-element.18), channel_id=1, replica_groups=mesh['row'=16,'col'=16] {'row'}, dimensions={0} | all-to-all | bytes 131072 | tf_op jit(solution)/shard_map/all_to_all | solution.py:278
  (59 shorter events, 7.1 us)
Async XLA Ops:
  7.2 71.9 %all-gather.2.cloned.1.call-start = ((), (), s32[]{:S(2)}) async-start(), calls=%async_computation.2 | async-start | bytes 10027008 | tf_op jit(solution)/shard_map/all_gather | solution.py:226
  9.0 9.4 %collective-permute-start.9 = (bf16[384,384]{1,0:T(8,128)(2,1)S(1)}, bf16[384,384]{1,0:T(8,128)(2,1)S(1)}, u32[]{:S(2)}, u32[]{:S(2)}) collective-permute-start(bf16[384,384]{1,0:T(8,128)(2,1)S(1)} %get-tuple-element.14), channel_id=1, source_target_pairs={{0,8},{1,9},{2,10},{3,11},{4,12},{5,13},{6,14},{7,15},{8,0},{9,1},... | collective-permute-start | bytes 884744 | tf_op jit(solution)/shard_map/ppermute | solution.py:43
  12.7 13.1 %collective-permute-start.8 = (bf16[384,384]{1,0:T(8,128)(2,1)S(1)}, bf16[384,384]{1,0:T(8,128)(2,1)S(1)}, u32[]{:S(2)}, u32[]{:S(2)}) collective-permute-start(bf16[384,384]{1,0:T(8,128)(2,1)S(1)} %get-tuple-element.14), channel_id=1, source_target_pairs={{0,12},{1,13},{2,14},{3,15},{4,0},{5,1},{6,2},{7,3},{8,4},{9,5},{1... | collective-permute-start | bytes 884744 | tf_op jit(solution)/shard_map/ppermute | solution.py:43
  13.5 12.3 %collective-permute-start.7 = (bf16[384,384]{1,0:T(8,128)(2,1)S(1)}, bf16[384,384]{1,0:T(8,128)(2,1)S(1)}, u32[]{:S(2)}, u32[]{:S(2)}) collective-permute-start(bf16[384,384]{1,0:T(8,128)(2,1)S(1)} %get-tuple-element.14), channel_id=1, source_target_pairs={{0,4},{1,5},{2,6},{3,7},{4,8},{5,9},{6,10},{7,11},{8,12},{9,13},{1... | collective-permute-start | bytes 884744 | tf_op jit(solution)/shard_map/ppermute | solution.py:43
  14.1 15.5 %collective-permute-start.2 = (bf16[384,384]{1,0:T(8,128)(2,1)S(1)}, bf16[384,384]{1,0:T(8,128)(2,1)S(1)}, u32[]{:S(2)}, u32[]{:S(2)}) collective-permute-start(bf16[384,384]{1,0:T(8,128)(2,1)S(1)} %get-tuple-element.13), channel_id=1, source_target_pairs={{0,2},{1,3},{2,0},{3,1},{4,6},{5,7},{6,4},{7,5},{8,10},{9,11},{10,... | collective-permute-start | bytes 884744 | tf_op jit(solution)/shard_map/ppermute | solution.py:43
  17.1 13.2 %collective-permute-start.1 = (bf16[384,384]{1,0:T(8,128)(2,1)S(1)}, bf16[384,384]{1,0:T(8,128)(2,1)S(1)}, u32[]{:S(2)}, u32[]{:S(2)}) collective-permute-start(bf16[384,384]{1,0:T(8,128)(2,1)S(1)} %get-tuple-element.13), channel_id=1, source_target_pairs={{0,3},{1,0},{2,1},{3,2},{4,7},{5,4},{6,5},{7,6},{8,11},{9,8},{10,9... | collective-permute-start | bytes 884744 | tf_op jit(solution)/shard_map/ppermute | solution.py:43
  18.4 11.8 %collective-permute-start = (bf16[384,384]{1,0:T(8,128)(2,1)S(1)}, bf16[384,384]{1,0:T(8,128)(2,1)S(1)}, u32[]{:S(2)}, u32[]{:S(2)}) collective-permute-start(bf16[384,384]{1,0:T(8,128)(2,1)S(1)} %get-tuple-element.13), channel_id=1, source_target_pairs={{0,1},{1,2},{2,3},{3,0},{4,5},{5,6},{6,7},{7,4},{8,9},{9,10},{10,1... | collective-permute-start | bytes 884744 | tf_op jit(solution)/shard_map/ppermute | solution.py:43
  26.0 28.9 %collective-permute-start.11 = (bf16[4,384,384]{2,1,0:T(8,128)(2,1)S(1)}, bf16[4,384,384]{2,1,0:T(8,128)(2,1)S(1)}, u32[]{:S(2)}, u32[]{:S(2)}) collective-permute-start(bf16[4,384,384]{2,1,0:T(8,128)(2,1)S(1)} %pad_maximum_fusion.1.rest_5_), channel_id=1, source_target_pairs={{0,3},{1,0},{2,1},{3,2},{4,7},{5,4},{6,5},{7,6},{8,11},{9,8},{10,9... | collective-permute-start | bytes 3538952 | tf_op jit(solution)/shard_map/ppermute | solution.py:43
  29.7 29.4 %collective-permute-start.10 = (bf16[4,384,384]{2,1,0:T(8,128)(2,1)S(1)}, bf16[4,384,384]{2,1,0:T(8,128)(2,1)S(1)}, u32[]{:S(2)}, u32[]{:S(2)}) collective-permute-start(bf16[4,384,384]{2,1,0:T(8,128)(2,1)S(1)} %pad_maximum_fusion.1.rest_5_), channel_id=1, source_target_pairs={{0,1},{1,2},{2,3},{3,0},{4,5},{5,6},{6,7},{7,4},{8,9},{9,10},{10,1... | collective-permute-start | bytes 3538952 | tf_op jit(solution)/shard_map/ppermute | solution.py:43
  30.4 29.8 %collective-permute-start.4 = (bf16[4,384,384]{2,1,0:T(8,128)(2,1)S(1)}, bf16[4,384,384]{2,1,0:T(8,128)(2,1)S(1)}, u32[]{:S(2)}, u32[]{:S(2)}) collective-permute-start(bf16[4,384,384]{2,1,0:T(8,128)(2,1)S(1)} %pad_maximum_fusion.rest_0_), channel_id=1, source_target_pairs={{0,12},{1,13},{2,14},{3,15},{4,0},{5,1},{6,2},{7,3},{8,4},{9,5},{1... | collective-permute-start | bytes 3538952 | tf_op jit(solution)/shard_map/ppermute | solution.py:43
  32.6 31.0 %collective-permute-start.3 = (bf16[4,384,384]{2,1,0:T(8,128)(2,1)S(1)}, bf16[4,384,384]{2,1,0:T(8,128)(2,1)S(1)}, u32[]{:S(2)}, u32[]{:S(2)}) collective-permute-start(bf16[4,384,384]{2,1,0:T(8,128)(2,1)S(1)} %pad_maximum_fusion.rest_0_), channel_id=1, source_target_pairs={{0,4},{1,5},{2,6},{3,7},{4,8},{5,9},{6,10},{7,11},{8,12},{9,13},{1... | collective-permute-start | bytes 3538952 | tf_op jit(solution)/shard_map/ppermute | solution.py:43
  54.9 5.1 %copy-start.11 = (bf16[4,384,384]{2,1,0:T(8,128)(2,1)}, bf16[4,384,384]{2,1,0:T(8,128)(2,1)S(1)}, u32[]{:S(2)}) copy-start(bf16[4,384,384]{2,1,0:T(8,128)(2,1)S(1)} %collective-permute-done.11.rest_7_) | copy-start | bytes 3538948
  55.9 15.4 %collective-permute-start.13 = (bf16[2,384,384]{2,1,0:T(8,128)(2,1)}, bf16[2,384,384]{2,1,0:T(8,128)(2,1)}, u32[]{:S(2)}, u32[]{:S(2)}) collective-permute-start(bf16[2,384,384]{2,1,0:T(8,128)(2,1)} %slice.27), channel_id=1, source_target_pairs={{0,3},{1,0},{2,1},{3,2},{4,7},{5,4},{6,5},{7,6},{8,11},{9,8},{10,9... | collective-permute-start | bytes 1769480 | tf_op jit(solution)/shard_map/ppermute | solution.py:43
  60.1 4.9 %copy-start.13 = (s32[3,3]{1,0:T(4,128)S(1)}, s32[3,3]{1,0:T(4,128)}, u32[]{:S(2)}) copy-start(s32[3,3]{1,0:T(4,128)} %param.14) | copy-start | bytes 112
  60.1 5.1 %copy-start.14 = (s32[1,384]{1,0:T(1,128)S(1)}, s32[1,384]{1,0:T(1,128)}, u32[]{:S(2)}) copy-start(s32[1,384]{1,0:T(1,128)} %param.16) | copy-start | bytes 4612
  60.1 5.2 %copy-start.7 = (bf16[384,384]{1,0:T(8,128)(2,1)S(1)}, bf16[384,384]{1,0:T(8,128)(2,1)}, u32[]{:S(2)}) copy-start(bf16[384,384]{1,0:T(8,128)(2,1)} %weighted_ref.1) | copy-start | bytes 884740
  60.1 14.8 %collective-permute-start.12 = (bf16[2,384,384]{2,1,0:T(8,128)(2,1)}, bf16[2,384,384]{2,1,0:T(8,128)(2,1)}, u32[]{:S(2)}, u32[]{:S(2)}) collective-permute-start(bf16[2,384,384]{2,1,0:T(8,128)(2,1)} %slice.26), channel_id=1, source_target_pairs={{0,1},{1,2},{2,3},{3,0},{4,5},{5,6},{6,7},{7,4},{8,9},{9,10},{10,1... | collective-permute-start | bytes 1769480 | tf_op jit(solution)/shard_map/ppermute | solution.py:43
  61.1 5.8 %copy-start.15 = (s32[2]{0:T(128)S(1)}, s32[2]{0:T(128)}, u32[]{:S(2)}) copy-start(s32[2]{0:T(128)} %param.15) | copy-start | bytes 28
  61.1 17.9 %copy-start = (bf16[2,384,384]{2,1,0:T(8,128)(2,1)S(1)}, bf16[2,384,384]{2,1,0:T(8,128)(2,1)}, u32[]{:S(2)}) copy-start(bf16[2,384,384]{2,1,0:T(8,128)(2,1)} %rest_11_.1) | copy-start | bytes 1769476
  61.1 13.9 %collective-permute-start.6 = (bf16[2,384,384]{2,1,0:T(8,128)(2,1)}, bf16[2,384,384]{2,1,0:T(8,128)(2,1)}, u32[]{:S(2)}, u32[]{:S(2)}) collective-permute-start(bf16[2,384,384]{2,1,0:T(8,128)(2,1)} %slice.25), channel_id=1, source_target_pairs={{0,12},{1,13},{2,14},{3,15},{4,0},{5,1},{6,2},{7,3},{8,4},{9,5},{1... | collective-permute-start | bytes 1769480 | tf_op jit(solution)/shard_map/ppermute | solution.py:43
  64.5 14.6 %collective-permute-start.5 = (bf16[2,384,384]{2,1,0:T(8,128)(2,1)}, bf16[2,384,384]{2,1,0:T(8,128)(2,1)}, u32[]{:S(2)}, u32[]{:S(2)}) collective-permute-start(bf16[2,384,384]{2,1,0:T(8,128)(2,1)} %slice.24), channel_id=1, source_target_pairs={{0,4},{1,5},{2,6},{3,7},{4,8},{5,9},{6,10},{7,11},{8,12},{9,13},{1... | collective-permute-start | bytes 1769480 | tf_op jit(solution)/shard_map/ppermute | solution.py:43
  66.6 36.8 %copy-start.9 = (f32[96]{0:T(128)S(1)}, f32[96]{0:T(128)}, u32[]{:S(2)}) copy-start(f32[96]{0:T(128)} %param.19) | copy-start | bytes 1156
  66.6 58.1 %copy-start.10 = (f32[3,96]{1,0:T(4,128)S(1)}, f32[3,96]{1,0:T(4,128)}, u32[]{:S(2)}) copy-start(f32[3,96]{1,0:T(4,128)} %positions_ref.1) | copy-start | bytes 3460
  66.9 36.5 %copy-start.8 = (f32[3,96]{1,0:T(4,128)S(1)}, f32[3,96]{1,0:T(4,128)}, u32[]{:S(2)}) copy-start(f32[3,96]{1,0:T(4,128)} %velocities_ref.3) | copy-start | bytes 3460
  (7 other events, 12.5 us)
Sparse Core Ops, SparseCore 0:
  9.8 65.0 all-gather.1

commit v4 on v3

v4 whole, which is shorter than its diff:
```python
import jax
import jax.numpy as jnp
from jax import lax
from jax.experimental import pallas as pl
from jax.experimental.pallas import tpu as pltpu
from jax.sharding import PartitionSpec as P

TILE = 128
ROWS = 384
SLABS = 16
HALVES = 2
LANES = 128

mixing = 0.25
time_step = 0.1
epsilon = 1e-06

AXES = ("row", "col")


def place(z, core, x, y):
    return (z % 8 * 2 + core) * 16 + x % 4 * 4 + y % 4


def pairs(move):
    out = []
    for z in range(8):
        for core in range(2):
            for x in range(4):
                for y in range(4):
                    out.append((place(z, core, x, y), place(*move(z, core, x, y))))
    return out


def first_by(k):
    return pairs(lambda z, core, x, y: (z, core, x + k * core, y + k * (1 - core)))


def second_by(k):
    return pairs(lambda z, core, x, y: (z, core, x + k * (1 - core), y + k * core))


def z_by(k):
    return pairs(lambda z, core, x, y: (z + k, core, x, y))


def core_swap():
    return pairs(lambda z, core, x, y: (z, 1 - core, x, y))


def send(value, table):
    return lax.ppermute(value, AXES, table)


def gather_plane(block):
    back = send(block, first_by(1))
    fore = send(block, first_by(-1))
    line = jnp.stack([block, back, fore])
    far = jnp.stack([send(back[0], first_by(1)), send(fore[1], first_by(-1))])
    line_back = send(line, second_by(1))
    line_fore = send(line, second_by(-1))
    far_back = send(far, second_by(1))
    far_fore = send(far, second_by(-1))
    line_low = send(line_back[:, 0], second_by(1))
    line_high = send(line_fore[:, 1], second_by(-1))
    far_low = send(far_back[0], second_by(1))
    far_high = send(far_fore[1], second_by(-1))
    return (
        line,
        far,
        line_back,
        far_back,
        line_fore,
        far_fore,
        line_low,
        line_high,
        far_low,
        far_high,
    )


def rank(difference):
    return jnp.where(difference == 0, 0, jnp.where(difference == 3, 1, jnp.where(difference == 1, 2, 3)))


def gather_column(block):
    back = send(block, z_by(1))
    fore = send(block, z_by(-1))
    back_two = send(back, z_by(1))
    fore_two = send(fore, z_by(-1))
    back_three = send(back_two, z_by(1))
    fore_three = send(fore_two, z_by(-1))
    low = send(back_three[0], z_by(1))
    high = send(fore_three[1], z_by(-1))
    return (block, back, back_two, back_three, fore_three, fore_two, fore, low, high)


LEVELS = (0, -1, -2, -3, 3, 2, 1)


def terms_of(matrix, deriv_ref, one_hot):
    rows = []
    for x in range(3):
        column = jnp.sum(matrix * deriv_ref[x].astype(jnp.float32), axis=1, keepdims=True)
        rows.append(jnp.sum(column * one_hot, axis=0, keepdims=True))
    return rows


def one_hot_of(atom_ref):
    lanes = lax.broadcasted_iota(jnp.int32, (ROWS, LANES), 1)
    return (atom_ref[...] == lanes).astype(jnp.float32)


def by_line(rows, scale):
    lines = lax.broadcasted_iota(jnp.int32, (8, LANES), 0)
    out = jnp.zeros((8, LANES), jnp.float32)
    for x in range(3):
        out = jnp.where(lines == x, scale * rows[x], out)
    return out


def overlap_kernel(atom_ref, weighted_ref, ovl_ref, out_ref):
    rows = terms_of(weighted_ref[...].astype(jnp.float32), ovl_ref, one_hot_of(atom_ref))
    out_ref[...] = by_line(rows, 2.0)


FACT_CORE = SLABS
FACT_BRANCH = SLABS + 1
FACT_PATTERN = SLABS + 2
FACT_Z = SLABS + 20


def purify_kernel(facts_ref, *rest):
    wide, tall, rest = rest[:10], rest[10:19], rest[19:]
    atom_ref, other_atom_ref, ham_ref, other_ham_ref, overlap_ref = rest[:5]
    keep_ref, give_ref, sums_ref, give_sums_ref, b_buf, total, done = rest[5:]
    line, far, line_back, far_back, line_fore, far_fore, line_low, line_high, far_low, far_high = wide
    core, z = facts_ref[FACT_CORE], facts_ref[FACT_Z]
    for half in range(HALVES):
        for level, offset in enumerate(LEVELS):
            slab = ((z + offset) & 7) * 2 + half
            b_buf[facts_ref[slab]] = tall[level][half]
        slab = ((z + 4) & 7) * 2 + half
        b_buf[facts_ref[slab]] = tall[7 + half][...]
    for half in range(HALVES):
        groups = [
            [line[0, half], line[1, half], line[2, half], far[half]],
            [line_back[0, half], line_back[1, half], line_back[2, half], far_back[half]],
            [line_fore[0, half], line_fore[1, half], line_fore[2, half], far_fore[half]],
        ]
        last, corner = ((line_low, far_low), (line_high, far_high))[half]
        groups.append([last[0], last[1], last[2], corner[...]])
        for i, group in enumerate(groups):
            product = jnp.dot(
                jnp.concatenate(group, axis=1),
                b_buf[4 * i : 4 * i + 4].reshape(4 * ROWS, ROWS),
                preferred_element_type=jnp.float32,
            )
            if i == 0:
                total[...] = product
            else:
                total[...] += product
        square = total[...]
        flip = facts_ref[FACT_BRANCH] == 1
        raw = jnp.where(flip, 2.0 * line[0, half].astype(jnp.float32) - square, square)
        for i in range(3):
            for j in range(3):
                weight = facts_ref[FACT_PATTERN + 9 * half + 3 * i + j].astype(jnp.float32)
                at = (slice(i * TILE, (i + 1) * TILE), slice(j * TILE, (j + 1) * TILE))
                done[(half,) + at] = (raw[at] * weight).astype(jnp.bfloat16)
    mine = done[core]
    keep_ref[...] = mine
    rows = terms_of(mine.astype(jnp.float32), ham_ref, one_hot_of(atom_ref))
    sums_ref[...] = overlap_ref[...] + by_line(rows, -2.0)
    theirs = done[1 - core]
    give_ref[...] = theirs
    rows = terms_of(theirs.astype(jnp.float32), other_ham_ref, one_hot_of(other_atom_ref))
    give_sums_ref[...] = by_line(rows, -2.0)


def norm_kernel(parts_ref, velocities_ref, masses_ref, forces_ref, sums_ref, norms_ref):
    sums = parts_ref[0]
    for part in range(1, parts_ref.shape[0]):
        sums = sums + parts_ref[part]
    forces = sums[:3, : forces_ref.shape[1]]
    forces_ref[...] = forces
    sums_ref[...] = sums
    scaled = forces / jnp.sqrt(masses_ref[...])
    speeds = velocities_ref[...]
    rows = lax.broadcasted_iota(jnp.int32, norms_ref.shape, 1)
    norms_ref[...] = jnp.where(rows == 0, jnp.sum(scaled * scaled), jnp.sum(speeds * speeds))


def update_kernel(
    parts_ref, sums_ref, positions_ref, velocities_ref, masses_ref, speeds_ref, places_ref
):
    norms = parts_ref[0]
    for part in range(1, parts_ref.shape[0]):
        norms = norms + parts_ref[part]
    force_norm, speed_norm = norms[0:1, 0:1], norms[1:2, 0:1]
    root_mass = jnp.sqrt(masses_ref[...])
    scaled = sums_ref[:3, : speeds_ref.shape[1]] / root_mass
    speeds = (
        (1.0 - mixing) * velocities_ref[...]
        + mixing * jnp.sqrt(speed_norm) * scaled / jnp.sqrt(force_norm + epsilon)
        + time_step * scaled
    )
    speeds_ref[...] = speeds
    places_ref[...] = positions_ref[...] + time_step * speeds / root_mass


SMEM = pl.BlockSpec(memory_space=pltpu.SMEM)
VMEM = pl.BlockSpec(memory_space=pltpu.VMEM)

COST = pl.CostEstimate(
    flops=4 * ROWS * ROWS * ROWS * SLABS,
    bytes_accessed=8 * ROWS * ROWS * SLABS,
    transcendentals=0,
)
PARAMS = pltpu.CompilerParams(vmem_limit_bytes=16 * 1024 * 1024)
LITTLE = pltpu.CompilerParams(vmem_limit_bytes=2 * 1024 * 1024)


def small(shape):
    return jax.ShapeDtypeStruct(shape, jnp.float32)


def half_block():
    return jax.ShapeDtypeStruct((ROWS, ROWS), jnp.bfloat16)


def local(
    density,
    weighted,
    ham_deriv,
    ovl_deriv,
    tile_pattern,
    branch,
    orbital_atom,
    positions,
    velocities,
    masses,
):
    row, column = lax.axis_index("row"), lax.axis_index("col")
    z, core = row >> 1, row & 1
    on_zero = core == 0
    at_x, at_y = column >> 2, column & 3

    mine = jnp.where(on_zero, density[0], density[1])
    theirs = send(jnp.where(on_zero, density[1], density[0]), core_swap())
    block = jnp.stack([jnp.where(on_zero, mine, theirs), jnp.where(on_zero, theirs, mine)])
    wide = gather_plane(block)
    tall = gather_column(block)

    other_ham = send(ham_deriv, core_swap())
    notes = jnp.concatenate(
        [orbital_atom.reshape(-1), tile_pattern.reshape(-1), jnp.zeros((119,), jnp.int32)]
    ).astype(jnp.float32)
    other_notes = send(notes.reshape(4, LANES), core_swap()).reshape(-1).astype(jnp.int32)
    other_atom, other_pattern = other_notes[:ROWS], other_notes[ROWS : ROWS + 9]
    own_pattern = tile_pattern.reshape(-1)

    slab = jnp.arange(SLABS, dtype=jnp.int32)
    by_x, by_y = ((slab >> 2) - at_x) & 3, ((slab & 3) - at_y) & 3
    first, second = jnp.where(on_zero, by_y, by_x), jnp.where(on_zero, by_x, by_y)
    facts = jnp.concatenate(
        [
            rank(second) * 4 + rank(first),
            jnp.stack([core, jnp.where(on_zero, branch[0], branch[1])]),
            jnp.where(on_zero, own_pattern, other_pattern),
            jnp.where(on_zero, other_pattern, own_pattern),
            jnp.stack([z]),
        ]
    ).astype(jnp.int32)

    atom_column = orbital_atom.reshape(ROWS, 1)
    overlap = pl.pallas_call(
        overlap_kernel,
        out_shape=small((8, LANES)),
        in_specs=[VMEM] * 3,
        out_specs=VMEM,
        compiler_params=pltpu.CompilerParams(vmem_limit_bytes=4 * 1024 * 1024),
    )(atom_column, weighted, ovl_deriv)

    keep, give, sums, give_sums = pl.pallas_call(
        purify_kernel,
        out_shape=(half_block(), half_block(), small((8, LANES)), small((8, LANES))),
        in_specs=[SMEM] + [VMEM] * 24,
        out_specs=(VMEM,) * 4,
        scratch_shapes=[
            pltpu.VMEM((SLABS, ROWS, ROWS), jnp.bfloat16),
            pltpu.VMEM((ROWS, ROWS), jnp.float32),
            pltpu.VMEM((HALVES, ROWS, ROWS), jnp.bfloat16),
        ],
        compiler_params=PARAMS,
        cost_estimate=COST,
    )(
        facts,
        *wide,
        *tall,
        atom_column,
        other_atom.reshape(ROWS, 1),
        ham_deriv,
        other_ham,
        overlap,
    )

    sums = sums + send(give_sums, core_swap())
    got = send(give, core_swap())
    parts = lax.all_to_all(jnp.broadcast_to(sums, (SLABS, 8, LANES)), "col", 0, 0)
    mass_row = masses[None, :]
    forces, sums, norms = pl.pallas_call(
        norm_kernel,
        out_shape=(small(positions.shape), small((8, LANES)), small((SLABS, 8, LANES))),
        in_specs=[VMEM] * 3,
        out_specs=(VMEM, VMEM, VMEM),
        compiler_params=LITTLE,
    )(parts, velocities, mass_row)
    parts = lax.all_to_all(norms, "row", 0, 0)
    new_velocities, new_positions = pl.pallas_call(
        update_kernel,
        out_shape=(small(positions.shape), small(positions.shape)),
        in_specs=[VMEM] * 5,
        out_specs=(VMEM, VMEM),
        compiler_params=LITTLE,
    )(parts, sums, positions, velocities, mass_row)
    purified = jnp.stack([jnp.where(on_zero, keep, got), jnp.where(on_zero, got, keep)])
    return (purified, forces, new_velocities, new_positions)


def solution(mesh):
    in_specs = (
        P(None, "row", "col"),
        P("row", "col"),
        P(None, "row", "col"),
        P(None, "row", "col"),
        P("row", "col"),
        P(),
        P("row", None),
        P(None, "row"),
        P(None, "row"),
        P("row"),
    )
    out_specs = (P(None, "row", "col"), P(None, "row"), P(None, "row"), P(None, "row"))
    return jax.shard_map(local, mesh=mesh, in_specs=in_specs, out_specs=out_specs, check_vma=False)
```

time: 133 us -> 146 us (1.098)
  local copies, waits for them, and re-layouts: 10.7 us -> 27.7 us
  between operations: 14.2 us -> 2.1 us
  starting transfers between devices: 22.6 us -> 32.8 us
  blocking collectives: 30.8 us -> 24.6 us
  other arithmetic: 0.45 us -> 6.56 us
    unnamed x32 -> x47, local copies, waits for them, and re-layouts: 5.29 us -> 15.8 us
    ppermute x14 -> x25, starting transfers between devices: 22.6 us -> 32.8 us  [send(): return lax.ppermute(value, AXES, table)]
    squeeze x1 -> x8, local copies, waits for them, and re-layouts: 1.11 us -> 8.92 us  [the longest x1 2.2 us: gather_plane(): line_high = send(line_fore[:, 1], second_by(-1))]
    all_to_all x1, blocking collectives: 20.7 us -> 15 us  [local(): parts = lax.all_to_all(norms, 'row', 0, 0)]
    another operation x3 -> x6, other arithmetic: 0.37 us -> 4.34 us  [the longest x1 1.93 us: gather_plane(): far = jnp.stack([send(back[0], first_by(1)), send(fore[1], first_by(-1))])]
    slice x4 -> x1, local copies, waits for them, and re-layouts: 3.79 us -> 1.31 us  [local(): branch[1]]
    select_n x0 -> x2, other arithmetic: none -> 1.59 us  [the longest x1 1.09 us: local(): theirs = send(jnp.where(on_zero, density[1], density[0]), core_swap())]
    ppermute x14 -> x25, waiting for transfers between devices: 40.7 us -> 40.4 us  [send(): return lax.ppermute(value, AXES, table)]
  transfers between devices with their start and end apart: 15 -> 25, of which waited for: 8 -> 8; matrix products, arithmetic and copies ran while one was open for 4% -> 11% of each run, Pallas kernels for 0% -> 1%
where the time goes in v4:
time: 146 us; the launch traced here: 145 us
  waiting for transfers between devices  40.4 us (28%)
  starting transfers between devices  32.8 us (22%)
  local copies, waits for them, and re-layouts  27.7 us (19%)
  blocking collectives  24.6 us (17%)
  Pallas kernels  10.9 us (7%)
  other arithmetic  6.56 us (4%)
  between operations  2.1 us (1%)
    ppermute x25, waiting for transfers between devices, send(): return lax.ppermute(value, AXES, table)  40.4 us
    ppermute x25, starting transfers between devices, send(): return lax.ppermute(value, AXES, table)  32.8 us
    unnamed x47, local copies, waits for them, and re-layouts  15.8 us
    all_to_all x1, blocking collectives, local(): parts = lax.all_to_all(norms, 'row', 0, 0)  15 us
    all_to_all x1, blocking collectives, local(): lax.all_to_all(jnp.broadcast_to(sums, (SLABS, 8, LANES)), 'col', 0, 0)  9.66 us
    pallas_call x1, Pallas kernels, local(): pl.pallas_call(purify_kernel, out_shape=(half_block(), half_block(), smal...  9.4 us
  transfers between devices with their start and end apart: 25, of which 8 were waited for; matrix products, arithmetic and copies ran while one was open for 11% of the time, Pallas kernels for 1%

profile of v4, /device:TPU:1, one launch (start us, length us, event | category | flops | bytes accessed | tf_op | source)
XLA Modules:
  0.0 145.1 jit_solution(11452158613817162356)
XLA Ops:
  1.7 3.3 %collective-permute-start.1 = (bf16[384,384]{1,0:T(8,128)(2,1)S(1)}, bf16[384,384]{1,0:T(8,128)(2,1)S(1)}, u32[]{:S(2)}, u32[]{:S(2)}) collective-permute-start(bf16[384,384]{1,0:T(8,128)(2,1)S(1)} %select_bitcast_fusion.2), channel_id=1, source_target_pairs={{0,16},{1,17},{2,18},{3,19},{4,20},{5,21},{6,22},{7,23},{8,24},{9,... | collective-permute-start | bytes 884744 | tf_op jit(solution)/shard_map/ppermute | solution.py:52
  7.6 2.7 %collective-permute-start.3 = (bf16[2,384,384]{2,1,0:T(8,128)(2,1)S(1)}, bf16[2,384,384]{2,1,0:T(8,128)(2,1)S(1)}, u32[]{:S(2)}, u32[]{:S(2)}) collective-permute-start(bf16[2,384,384]{2,1,0:T(8,128)(2,1)S(1)} %get-tuple-element.27.rest_10_), channel_id=1, source_target_pairs={{0,3},{1,0},{2,1},{3,2},{4,7},{5,4},{6,5},{7,6},{8,11},{9,8},{10,9... | collective-permute-start | bytes 1769480 | tf_op jit(solution)/shard_map/ppermute | solution.py:52
  10.3 7.6 %collective-permute-done.2 = bf16[2,384,384]{2,1,0:T(8,128)(2,1)S(1)} collective-permute-done((bf16[2,384,384]{2,1,0:T(8,128)(2,1)S(1)}, bf16[2,384,384]{2,1,0:T(8,128)(2,1)S(1)}, u32[]{:S(2)}, u32[]{:S(2)}) %collective-permute-start.2) | collective-permute-done | bytes 589856 | tf_op jit(solution)/shard_map/ppermute | solution.py:52
  19.4 2.7 %collective-permute-start.5 = (bf16[384,384]{1,0:T(8,128)(2,1)}, bf16[384,384]{1,0:T(8,128)(2,1)}, u32[]{:S(2)}, u32[]{:S(2)}) collective-permute-start(bf16[384,384]{1,0:T(8,128)(2,1)} %slice_bitcast_fusion.6), channel_id=1, source_target_pairs={{0,3},{1,0},{2,1},{3,2},{4,7},{5,4},{6,5},{7,6},{8,11},{9,8},{10,9... | collective-permute-start | bytes 884744 | tf_op jit(solution)/shard_map/ppermute | solution.py:52
  23.4 4.0 %collective-permute-start.17 = (bf16[2,384,384]{2,1,0:T(8,128)(2,1)}, bf16[2,384,384]{2,1,0:T(8,128)(2,1)}, u32[]{:S(2)}, u32[]{:S(2)}) collective-permute-start(bf16[2,384,384]{2,1,0:T(8,128)(2,1)} %copy-done), channel_id=1, source_target_pairs={{0,224},{1,225},{2,226},{3,227},{4,228},{5,229},{6,230},{7,231},{8... | collective-permute-start | bytes 1769480 | tf_op jit(solution)/shard_map/ppermute | solution.py:52
  27.5 1.9 %pad_maximum_fusion.2.rest_1_ = bf16[2,384,384]{2,1,0:T(8,128)(2,1)} fusion(bf16[1,384,384]{2,1,0:T(8,128)(2,1)} %bitcast.17, bf16[1,384,384]{2,1,0:T(8,128)(2,1)} %bitcast.15), kind=kLoop, calls=%fused_computation.4 | loop fusion | flops 294912 | bytes 1179648 | tf_op jit(solution)/shard_map/stack | solution.py:59
  29.4 1.3 collective-permute-start.7
  30.8 2.8 %collective-permute-start = (f32[4,128]{1,0:T(4,128)S(1)}, f32[4,128]{1,0:T(4,128)S(1)}, u32[]{:S(2)}, u32[]{:S(2)}) collective-permute-start(f32[4,128]{1,0:T(4,128)S(1)} %fusion.2), channel_id=1, source_target_pairs={{0,16},{1,17},{2,18},{3,19},{4,20},{5,21},{6,22},{7,23},{8,24},{9,... | collective-permute-start | bytes 6152 | tf_op jit(solution)/shard_map/ppermute | solution.py:52
  34.7 4.4 %collective-permute-done.14.rest_11_ = bf16[2,384,384]{2,1,0:T(8,128)(2,1)} collective-permute-done((bf16[2,384,384]{2,1,0:T(8,128)(2,1)}, bf16[2,384,384]{2,1,0:T(8,128)(2,1)}, u32[]{:S(2)}, u32[]{:S(2)}) %collective-permute-start.14) | collective-permute-done | bytes 589856 | tf_op jit(solution)/shard_map/ppermute | solution.py:52
  39.1 2.7 %collective-permute-start.18 = (bf16[2,384,384]{2,1,0:T(8,128)(2,1)}, bf16[2,384,384]{2,1,0:T(8,128)(2,1)}, u32[]{:S(2)}, u32[]{:S(2)}) collective-permute-start(bf16[2,384,384]{2,1,0:T(8,128)(2,1)} %collective-permute-done.17.rest_16_), channel_id=1, source_target_pairs={{0,224},{1,225},{2,226},{3,227},{4,228},{5,229},{6,230},{7,231},{8... | collective-permute-start | bytes 1769480 | tf_op jit(solution)/shard_map/ppermute | solution.py:52
  41.7 11.2 %collective-permute-done.7.rest_3_ = bf16[2,384,384]{2,1,0:T(8,128)(2,1)} collective-permute-done((bf16[2,384,384]{2,1,0:T(8,128)(2,1)}, bf16[2,384,384]{2,1,0:T(8,128)(2,1)}, u32[]{:S(2)}, u32[]{:S(2)}) %collective-permute-start.7) | collective-permute-done | bytes 589856 | tf_op jit(solution)/shard_map/ppermute | solution.py:52
  53.0 1.3 fusion.7
  61.3 1.4 collective-permute-start.22
  62.8 1.4 collective-permute-start.16
  64.2 4.0 %collective-permute-start.19 = (bf16[2,384,384]{2,1,0:T(8,128)(2,1)}, bf16[2,384,384]{2,1,0:T(8,128)(2,1)S(1)}, u32[]{:S(2)}, u32[]{:S(2)}) collective-permute-start(bf16[2,384,384]{2,1,0:T(8,128)(2,1)} %collective-permute-done.18.rest_15_), channel_id=1, source_target_pairs={{0,224},{1,225},{2,226},{3,227},{4,228},{5,229},{6,230},{7,231},{8... | collective-permute-start | bytes 1769480 | tf_op jit(solution)/shard_map/ppermute | solution.py:52
  68.2 1.7 %slice_bitcast_fusion.4 = bf16[384,384]{1,0:T(8,128)(2,1)} fusion(bf16[2,384,384]{2,1,0:T(8,128)(2,1)} %collective-permute-done.9.rest_5_), kind=kLoop, calls=%fused_computation.8 | loop fusion | bytes 589824 | tf_op jit(solution)/shard_map/squeeze | solution.py:67
  71.1 2.2 %slice_bitcast_fusion = bf16[3,384,384]{2,1,0:T(8,128)(2,1)} fusion(bf16[3,2,384,384]{3,2,1,0:T(8,128)(2,1)} %collective-permute-done.8.rest_4_), kind=kLoop, calls=%fused_computation.1 | loop fusion | bytes 1769472 | tf_op jit(solution)/shard_map/squeeze | solution.py:65
  73.3 8.6 %collective-permute-done.16.rest_13_ = bf16[2,384,384]{2,1,0:T(8,128)(2,1)S(1)} collective-permute-done((bf16[2,384,384]{2,1,0:T(8,128)(2,1)}, bf16[2,384,384]{2,1,0:T(8,128)(2,1)S(1)}, u32[]{:S(2)}, u32[]{:S(2)}) %collective-permute-start.16) | collective-permute-done | bytes 589856 | tf_op jit(solution)/shard_map/ppermute | solution.py:52
  87.5 2.7 %collective-permute-start.21 = (bf16[384,384]{1,0:T(8,128)(2,1)}, bf16[384,384]{1,0:T(8,128)(2,1)}, u32[]{:S(2)}, u32[]{:S(2)}) collective-permute-start(bf16[384,384]{1,0:T(8,128)(2,1)} %slice_bitcast_fusion.2), channel_id=1, source_target_pairs={{0,224},{1,225},{2,226},{3,227},{4,228},{5,229},{6,230},{7,231},{8... | collective-permute-start | bytes 884744 | tf_op jit(solution)/shard_map/ppermute | solution.py:52
  92.2 5.4 %collective-permute-done.13.rest_9_ = bf16[384,384]{1,0:T(8,128)(2,1)} collective-permute-done((bf16[384,384]{1,0:T(8,128)(2,1)}, bf16[384,384]{1,0:T(8,128)(2,1)}, u32[]{:S(2)}, u32[]{:S(2)}) %collective-permute-start.13) | collective-permute-done | bytes 294944 | tf_op jit(solution)/shard_map/ppermute | solution.py:52
  106.0 9.4 %shard_map.130 = (bf16[384,384]{1,0:T(8,128)(2,1)S(1)}, bf16[384,384]{1,0:T(8,128)(2,1)S(1)}, f32[8,128]{1,0:T(8,128)S(1)}, f32[8,128]{1,0:T(8,128)S(1)}) custom-call(s32[37]{0:T(128)S(1)} %concatenate.7.facts_ref, bf16[3,2,384,384]{3,2,1,0:T(8,128)(2,1)S(1)} %pad_maximum_fusion.rest_0_, bf16[2,384,384]{2,1,0:T(8,128)(2,1)} %pad_maximum_fusion.2.rest_1_, ...), custom_call_target="tpu_custom_call" | custom-call | flops 3623878656 | bytes 18874368 | tf_op jit(solution)/shard_map/pallas_call | solution.py:285
  115.4 1.6 %collective-permute-start.23 = (bf16[384,384]{1,0:T(8,128)(2,1)S(1)}, bf16[384,384]{1,0:T(8,128)(2,1)S(1)}, u32[]{:S(2)}, u32[]{:S(2)}) collective-permute-start(bf16[384,384]{1,0:T(8,128)(2,1)S(1)} %get-tuple-element.14), channel_id=1, source_target_pairs={{0,16},{1,17},{2,18},{3,19},{4,20},{5,21},{6,22},{7,23},{8,24},{9,... | collective-permute-start | bytes 884744 | tf_op jit(solution)/shard_map/ppermute | solution.py:52
  118.3 9.7 %all_to_all.10.parts_ref = f32[16,8,128]{2,1,0:T(8,128)S(1)} all-to-all(f32[16,8,128]{2,1,0:T(8,128)S(1)} %broadcast_in_dim.24), channel_id=1, replica_groups=mesh['row'=16,'col'=16] {'col'}, dimensions={0} | all-to-all | bytes 131072 | tf_op jit(solution)/shard_map/all_to_all | solution.py:310
  128.5 15.0 %all_to_all.11.parts_ref = f32[16,8,128]{2,1,0:T(8,128)S(1)} all-to-all(f32[16,8,128]{2,1,0:T(8,128)S(1)} %get-tuple-element.18), channel_id=1, replica_groups=mesh['row'=16,'col'=16] {'row'}, dimensions={0} | all-to-all | bytes 131072 | tf_op jit(solution)/shard_map/all_to_all | solution.py:319
  (106 shorter events, 34.0 us)
Async XLA Ops:
  1.7 4.5 %collective-permute-start.1 = (bf16[384,384]{1,0:T(8,128)(2,1)S(1)}, bf16[384,384]{1,0:T(8,128)(2,1)S(1)}, u32[]{:S(2)}, u32[]{:S(2)}) collective-permute-start(bf16[384,384]{1,0:T(8,128)(2,1)S(1)} %select_bitcast_fusion.2), channel_id=1, source_target_pairs={{0,16},{1,17},{2,18},{3,19},{4,20},{5,21},{6,22},{7,23},{8,24},{9,... | collective-permute-start | bytes 884744 | tf_op jit(solution)/shard_map/ppermute | solution.py:52
  7.5 10.3 %collective-permute-start.2 = (bf16[2,384,384]{2,1,0:T(8,128)(2,1)S(1)}, bf16[2,384,384]{2,1,0:T(8,128)(2,1)S(1)}, u32[]{:S(2)}, u32[]{:S(2)}) collective-permute-start(bf16[2,384,384]{2,1,0:T(8,128)(2,1)S(1)} %get-tuple-element.27.rest_10_), channel_id=1, source_target_pairs={{0,1},{1,2},{2,3},{3,0},{4,5},{5,6},{6,7},{7,4},{8,9},{9,10},{10,1... | collective-permute-start | bytes 1769480 | tf_op jit(solution)/shard_map/ppermute | solution.py:52
  7.6 11.0 %collective-permute-start.3 = (bf16[2,384,384]{2,1,0:T(8,128)(2,1)S(1)}, bf16[2,384,384]{2,1,0:T(8,128)(2,1)S(1)}, u32[]{:S(2)}, u32[]{:S(2)}) collective-permute-start(bf16[2,384,384]{2,1,0:T(8,128)(2,1)S(1)} %get-tuple-element.27.rest_10_), channel_id=1, source_target_pairs={{0,3},{1,0},{2,1},{3,2},{4,7},{5,4},{6,5},{7,6},{8,11},{9,8},{10,9... | collective-permute-start | bytes 1769480 | tf_op jit(solution)/shard_map/ppermute | solution.py:52
  18.6 8.9 %collective-permute-start.4 = (bf16[384,384]{1,0:T(8,128)(2,1)}, bf16[384,384]{1,0:T(8,128)(2,1)}, u32[]{:S(2)}, u32[]{:S(2)}) collective-permute-start(bf16[384,384]{1,0:T(8,128)(2,1)} %slice_bitcast_fusion.7), channel_id=1, source_target_pairs={{0,1},{1,2},{2,3},{3,0},{4,5},{5,6},{6,7},{7,4},{8,9},{9,10},{10,1... | collective-permute-start | bytes 884744 | tf_op jit(solution)/shard_map/ppermute | solution.py:52
  19.4 8.1 %collective-permute-start.5 = (bf16[384,384]{1,0:T(8,128)(2,1)}, bf16[384,384]{1,0:T(8,128)(2,1)}, u32[]{:S(2)}, u32[]{:S(2)}) collective-permute-start(bf16[384,384]{1,0:T(8,128)(2,1)} %slice_bitcast_fusion.6), channel_id=1, source_target_pairs={{0,3},{1,0},{2,1},{3,2},{4,7},{5,4},{6,5},{7,6},{8,11},{9,8},{10,9... | collective-permute-start | bytes 884744 | tf_op jit(solution)/shard_map/ppermute | solution.py:52
  22.3 47.7 %collective-permute-start.6 = (bf16[3,2,384,384]{3,2,1,0:T(8,128)(2,1)S(1)}, bf16[3,2,384,384]{3,2,1,0:T(8,128)(2,1)S(1)}, u32[]{:S(2)}, u32[]{:S(2)}) collective-permute-start(bf16[3,2,384,384]{3,2,1,0:T(8,128)(2,1)S(1)} %pad_maximum_fusion.rest_0_), channel_id=1, source_target_pairs={{0,4},{1,5},{2,6},{3,7},{4,8},{5,9},{6,10},{7,11},{8,12},{9,13},{1... | collective-permute-start | bytes 5308424 | tf_op jit(solution)/shard_map/ppermute | solution.py:52
  22.8 16.2 %collective-permute-start.14 = (bf16[2,384,384]{2,1,0:T(8,128)(2,1)}, bf16[2,384,384]{2,1,0:T(8,128)(2,1)}, u32[]{:S(2)}, u32[]{:S(2)}) collective-permute-start(bf16[2,384,384]{2,1,0:T(8,128)(2,1)} %copy-done), channel_id=1, source_target_pairs={{0,32},{1,33},{2,34},{3,35},{4,36},{5,37},{6,38},{7,39},{8,40},{9,... | collective-permute-start | bytes 1769480 | tf_op jit(solution)/shard_map/ppermute | solution.py:52
  23.4 15.6 %collective-permute-start.17 = (bf16[2,384,384]{2,1,0:T(8,128)(2,1)}, bf16[2,384,384]{2,1,0:T(8,128)(2,1)}, u32[]{:S(2)}, u32[]{:S(2)}) collective-permute-start(bf16[2,384,384]{2,1,0:T(8,128)(2,1)} %copy-done), channel_id=1, source_target_pairs={{0,224},{1,225},{2,226},{3,227},{4,228},{5,229},{6,230},{7,231},{8... | collective-permute-start | bytes 1769480 | tf_op jit(solution)/shard_map/ppermute | solution.py:52
  29.4 23.6 %collective-permute-start.7 = (bf16[2,384,384]{2,1,0:T(8,128)(2,1)}, bf16[2,384,384]{2,1,0:T(8,128)(2,1)}, u32[]{:S(2)}, u32[]{:S(2)}) collective-permute-start(bf16[2,384,384]{2,1,0:T(8,128)(2,1)} %pad_maximum_fusion.2.rest_1_), channel_id=1, source_target_pairs={{0,4},{1,5},{2,6},{3,7},{4,8},{5,9},{6,10},{7,11},{8,12},{9,13},{1... | collective-permute-start | bytes 1769480 | tf_op jit(solution)/shard_map/ppermute | solution.py:52
  30.8 3.6 %collective-permute-start = (f32[4,128]{1,0:T(4,128)S(1)}, f32[4,128]{1,0:T(4,128)S(1)}, u32[]{:S(2)}, u32[]{:S(2)}) collective-permute-start(f32[4,128]{1,0:T(4,128)S(1)} %fusion.2), channel_id=1, source_target_pairs={{0,16},{1,17},{2,18},{3,19},{4,20},{5,21},{6,22},{7,23},{8,24},{9,... | collective-permute-start | bytes 6152 | tf_op jit(solution)/shard_map/ppermute | solution.py:52
  34.4 36.6 %collective-permute-start.8 = (bf16[3,2,384,384]{3,2,1,0:T(8,128)(2,1)S(1)}, bf16[3,2,384,384]{3,2,1,0:T(8,128)(2,1)}, u32[]{:S(2)}, u32[]{:S(2)}) collective-permute-start(bf16[3,2,384,384]{3,2,1,0:T(8,128)(2,1)S(1)} %pad_maximum_fusion.rest_0_), channel_id=1, source_target_pairs={{0,12},{1,13},{2,14},{3,15},{4,0},{5,1},{6,2},{7,3},{8,4},{9,5},{1... | collective-permute-start | bytes 5308424 | tf_op jit(solution)/shard_map/ppermute | solution.py:52
  39.1 22.3 %collective-permute-start.15 = (bf16[2,384,384]{2,1,0:T(8,128)(2,1)}, bf16[2,384,384]{2,1,0:T(8,128)(2,1)}, u32[]{:S(2)}, u32[]{:S(2)}) collective-permute-start(bf16[2,384,384]{2,1,0:T(8,128)(2,1)} %collective-permute-done.14.rest_11_), channel_id=1, source_target_pairs={{0,32},{1,33},{2,34},{3,35},{4,36},{5,37},{6,38},{7,39},{8,40},{9,... | collective-permute-start | bytes 1769480 | tf_op jit(solution)/shard_map/ppermute | solution.py:52
  39.1 23.7 %collective-permute-start.18 = (bf16[2,384,384]{2,1,0:T(8,128)(2,1)}, bf16[2,384,384]{2,1,0:T(8,128)(2,1)}, u32[]{:S(2)}, u32[]{:S(2)}) collective-permute-start(bf16[2,384,384]{2,1,0:T(8,128)(2,1)} %collective-permute-done.17.rest_16_), channel_id=1, source_target_pairs={{0,224},{1,225},{2,226},{3,227},{4,228},{5,229},{6,230},{7,231},{8... | collective-permute-start | bytes 1769480 | tf_op jit(solution)/shard_map/ppermute | solution.py:52
  53.0 11.2 %collective-permute-start.9 = (bf16[2,384,384]{2,1,0:T(8,128)(2,1)}, bf16[2,384,384]{2,1,0:T(8,128)(2,1)}, u32[]{:S(2)}, u32[]{:S(2)}) collective-permute-start(bf16[2,384,384]{2,1,0:T(8,128)(2,1)} %pad_maximum_fusion.2.rest_1_), channel_id=1, source_target_pairs={{0,12},{1,13},{2,14},{3,15},{4,0},{5,1},{6,2},{7,3},{8,4},{9,5},{1... | collective-permute-start | bytes 1769480 | tf_op jit(solution)/shard_map/ppermute | solution.py:52
  61.3 24.5 %collective-permute-start.22 = (bf16[3,384,384]{2,1,0:T(8,128)(2,1)S(1)}, bf16[3,384,384]{2,1,0:T(8,128)(2,1)S(1)}, u32[]{:S(2)}, u32[]{:S(2)}) collective-permute-start(bf16[3,384,384]{2,1,0:T(8,128)(2,1)S(1)} %copy-done.9), channel_id=1, source_target_pairs={{0,16},{1,17},{2,18},{3,19},{4,20},{5,21},{6,22},{7,23},{8,24},{9,... | collective-permute-start | bytes 2654216 | tf_op jit(solution)/shard_map/ppermute | solution.py:52
  62.8 19.2 %collective-permute-start.16 = (bf16[2,384,384]{2,1,0:T(8,128)(2,1)}, bf16[2,384,384]{2,1,0:T(8,128)(2,1)S(1)}, u32[]{:S(2)}, u32[]{:S(2)}) collective-permute-start(bf16[2,384,384]{2,1,0:T(8,128)(2,1)} %collective-permute-done.15.rest_12_), channel_id=1, source_target_pairs={{0,32},{1,33},{2,34},{3,35},{4,36},{5,37},{6,38},{7,39},{8,40},{9,... | collective-permute-start | bytes 1769480 | tf_op jit(solution)/shard_map/ppermute | solution.py:52
  64.2 19.6 %collective-permute-start.19 = (bf16[2,384,384]{2,1,0:T(8,128)(2,1)}, bf16[2,384,384]{2,1,0:T(8,128)(2,1)S(1)}, u32[]{:S(2)}, u32[]{:S(2)}) collective-permute-start(bf16[2,384,384]{2,1,0:T(8,128)(2,1)} %collective-permute-done.18.rest_15_), channel_id=1, source_target_pairs={{0,224},{1,225},{2,226},{3,227},{4,228},{5,229},{6,230},{7,231},{8... | collective-permute-start | bytes 1769480 | tf_op jit(solution)/shard_map/ppermute | solution.py:52
  69.9 16.8 %collective-permute-start.12 = (bf16[384,384]{1,0:T(8,128)(2,1)S(1)}, bf16[384,384]{1,0:T(8,128)(2,1)S(1)}, u32[]{:S(2)}, u32[]{:S(2)}) collective-permute-start(bf16[384,384]{1,0:T(8,128)(2,1)S(1)} %slice_bitcast_fusion.5), channel_id=1, source_target_pairs={{0,4},{1,5},{2,6},{3,7},{4,8},{5,9},{6,10},{7,11},{8,12},{9,13},{1... | collective-permute-start | bytes 884744 | tf_op jit(solution)/shard_map/ppermute | solution.py:52
  71.0 26.7 %collective-permute-start.10 = (bf16[3,384,384]{2,1,0:T(8,128)(2,1)}, bf16[3,384,384]{2,1,0:T(8,128)(2,1)}, u32[]{:S(2)}, u32[]{:S(2)}) collective-permute-start(bf16[3,384,384]{2,1,0:T(8,128)(2,1)} %slice_bitcast_fusion.1), channel_id=1, source_target_pairs={{0,4},{1,5},{2,6},{3,7},{4,8},{5,9},{6,10},{7,11},{8,12},{9,13},{1... | collective-permute-start | bytes 2654216 | tf_op jit(solution)/shard_map/ppermute | solution.py:52
  82.0 15.7 %collective-permute-start.11 = (bf16[3,384,384]{2,1,0:T(8,128)(2,1)}, bf16[3,384,384]{2,1,0:T(8,128)(2,1)}, u32[]{:S(2)}, u32[]{:S(2)}) collective-permute-start(bf16[3,384,384]{2,1,0:T(8,128)(2,1)} %slice_bitcast_fusion), channel_id=1, source_target_pairs={{0,12},{1,13},{2,14},{3,15},{4,0},{5,1},{6,2},{7,3},{8,4},{9,5},{1... | collective-permute-start | bytes 2654216 | tf_op jit(solution)/shard_map/ppermute | solution.py:52
  83.8 13.8 %collective-permute-start.13 = (bf16[384,384]{1,0:T(8,128)(2,1)}, bf16[384,384]{1,0:T(8,128)(2,1)}, u32[]{:S(2)}, u32[]{:S(2)}) collective-permute-start(bf16[384,384]{1,0:T(8,128)(2,1)} %slice_bitcast_fusion.4), channel_id=1, source_target_pairs={{0,12},{1,13},{2,14},{3,15},{4,0},{5,1},{6,2},{7,3},{8,4},{9,5},{1... | collective-permute-start | bytes 884744 | tf_op jit(solution)/shard_map/ppermute | solution.py:52
  86.8 10.9 %collective-permute-start.20 = (bf16[384,384]{1,0:T(8,128)(2,1)}, bf16[384,384]{1,0:T(8,128)(2,1)}, u32[]{:S(2)}, u32[]{:S(2)}) collective-permute-start(bf16[384,384]{1,0:T(8,128)(2,1)} %slice_bitcast_fusion.3), channel_id=1, source_target_pairs={{0,32},{1,33},{2,34},{3,35},{4,36},{5,37},{6,38},{7,39},{8,40},{9,... | collective-permute-start | bytes 884744 | tf_op jit(solution)/shard_map/ppermute | solution.py:52
  87.5 10.1 %collective-permute-start.21 = (bf16[384,384]{1,0:T(8,128)(2,1)}, bf16[384,384]{1,0:T(8,128)(2,1)}, u32[]{:S(2)}, u32[]{:S(2)}) collective-permute-start(bf16[384,384]{1,0:T(8,128)(2,1)} %slice_bitcast_fusion.2), channel_id=1, source_target_pairs={{0,224},{1,225},{2,226},{3,227},{4,228},{5,229},{6,230},{7,231},{8... | collective-permute-start | bytes 884744 | tf_op jit(solution)/shard_map/ppermute | solution.py:52
  115.4 28.7 %collective-permute-start.23 = (bf16[384,384]{1,0:T(8,128)(2,1)S(1)}, bf16[384,384]{1,0:T(8,128)(2,1)S(1)}, u32[]{:S(2)}, u32[]{:S(2)}) collective-permute-start(bf16[384,384]{1,0:T(8,128)(2,1)S(1)} %get-tuple-element.14), channel_id=1, source_target_pairs={{0,16},{1,17},{2,18},{3,19},{4,20},{5,21},{6,22},{7,23},{8,24},{9,... | collective-permute-start | bytes 884744 | tf_op jit(solution)/shard_map/ppermute | solution.py:52
  (23 other events, 115.0 us)

commit v5 on v4

v5 whole, which is shorter than its diff:
```python
import jax
import jax.numpy as jnp
from jax import lax
from jax.experimental import pallas as pl
from jax.experimental.pallas import tpu as pltpu
from jax.sharding import PartitionSpec as P

TILE = 128
ROWS = 384
SLABS = 16
HALVES = 2
LANES = 128

mixing = 0.25
time_step = 0.1
epsilon = 1e-06

AXES = ("row", "col")


def place(z, core, x, y):
    return (z % 8 * 2 + core) * 16 + x % 4 * 4 + y % 4


def pairs(move):
    out = []
    for z in range(8):
        for core in range(2):
            for x in range(4):
                for y in range(4):
                    out.append((place(z, core, x, y), place(*move(z, core, x, y))))
    return out


def first_by(k):
    return pairs(lambda z, core, x, y: (z, core, x + k * core, y + k * (1 - core)))


def second_by(k):
    return pairs(lambda z, core, x, y: (z, core, x + k * (1 - core), y + k * core))


def z_by(k):
    return pairs(lambda z, core, x, y: (z + k, core, x, y))


def core_swap():
    return pairs(lambda z, core, x, y: (z, 1 - core, x, y))


def send(value, table):
    return lax.ppermute(value, AXES, table)


def after(value, *others):
    return lax.optimization_barrier((value,) + others)[0]


def gather(block):
    z_back = send(block, z_by(1))
    z_fore = send(block, z_by(-1))
    back = send(block, first_by(1))
    fore = send(block, first_by(-1))
    far = send(block, first_by(2))
    back, fore, far = after((back, fore, far), z_back, z_fore)
    line = jnp.stack([block, back, fore, far])
    line_back = send(line, second_by(1))
    line_fore = send(line, second_by(-1))
    z_back_two = send(z_back, z_by(1))
    z_fore_two = send(z_fore, z_by(-1))
    z_back_three = send(z_back_two, z_by(1))
    z_fore_three = send(z_fore_two, z_by(-1))
    low, high = after((line_back[:, 0], line_fore[:, 1]), z_back_three, z_fore_three)
    line_low = send(low, second_by(1))
    line_high = send(high, second_by(-1))
    z_low = send(z_back_three[0], z_by(1))
    z_high = send(z_fore_three[1], z_by(-1))
    wide = (line, line_back, line_fore, line_low, line_high)
    tall = (
        block,
        z_back,
        z_back_two,
        z_back_three,
        z_fore_three,
        z_fore_two,
        z_fore,
        z_low,
        z_high,
    )
    return wide, tall


LEVELS = (0, -1, -2, -3, 3, 2, 1)


def position():
    row, column = lax.axis_index("row"), lax.axis_index("col")
    return row >> 1, row & 1, column >> 2, column & 3


def terms_of(matrix, deriv_ref, one_hot):
    rows = []
    for x in range(3):
        column = jnp.sum(matrix * deriv_ref[x].astype(jnp.float32), axis=1, keepdims=True)
        rows.append(jnp.sum(column * one_hot, axis=0, keepdims=True))
    return rows


def one_hot_of(atom_ref):
    atoms = jnp.broadcast_to(atom_ref[...].astype(jnp.float32), (LANES, ROWS))
    lanes = lax.broadcasted_iota(jnp.int32, (ROWS, LANES), 1).astype(jnp.float32)
    return (jnp.transpose(atoms) == lanes).astype(jnp.float32)


def by_line(rows, scale):
    lines = lax.broadcasted_iota(jnp.int32, (8, LANES), 0)
    out = jnp.zeros((8, LANES), jnp.float32)
    for x in range(3):
        out = jnp.where(lines == x, scale * rows[x], out)
    return out


def overlap_kernel(atom_ref, weighted_ref, ovl_ref, out_ref):
    rows = terms_of(weighted_ref[...].astype(jnp.float32), ovl_ref, one_hot_of(atom_ref))
    out_ref[...] = by_line(rows, 2.0)


def give_kernel(density_ref, give_ref, sem):
    core = position()[1]
    copy = pltpu.make_async_copy(density_ref.at[1 - core], give_ref, sem)
    copy.start()
    copy.wait()


def block_kernel(density_ref, got_ref, block_ref, sems):
    core = position()[1]
    mine = pltpu.make_async_copy(density_ref.at[core], block_ref.at[core], sems.at[0])
    theirs = pltpu.make_async_copy(got_ref, block_ref.at[1 - core], sems.at[1])
    mine.start()
    theirs.start()
    mine.wait()
    theirs.wait()


def purify_kernel(branch_ref, pattern_ref, other_pattern_ref, *rest):
    wide, tall, rest = rest[:5], rest[5:14], rest[14:]
    ham_ref, other_ham_ref, atom_ref, other_atom_ref, overlap_ref = rest[:5]
    out_ref, give_ref, sums_ref, b_buf, total, done, out_sem = rest[5:]
    line = wide[0]
    z, core, at_x, at_y = position()
    for half in range(HALVES):
        for level, offset in enumerate(LEVELS + (4,)):
            slab = ((z + offset) & 7) * 2 + half
            by_x, by_y = ((slab >> 2) - at_x) & 3, ((slab & 3) - at_y) & 3
            first = jnp.where(core == 0, by_y, by_x)
            second = jnp.where(core == 0, by_x, by_y)
            first = jnp.where(first == 3, 1, first + jnp.minimum(first, 1))
            second = jnp.where(second == 3, 1, second + jnp.minimum(second, 1))
            slot = second * 4 + first
            b_buf[slot] = tall[level][half] if level < 7 else tall[7 + half][...]
    for group in range(4):
        rows = b_buf[4 * group : 4 * group + 4].reshape(4 * ROWS, ROWS)
        for half in range(HALVES):
            if group < 3:
                slabs = [wide[group][i, half] for i in range(4)]
            else:
                slabs = [wide[3 + half][i] for i in range(4)]
            product = jnp.dot(
                jnp.concatenate(slabs, axis=1),
                rows,
                preferred_element_type=jnp.float32,
            )
            if group == 0:
                total[half] = product
            else:
                total[half] += product
    for half in range(HALVES):
        square = total[half]
        flip = branch_ref[core] == 1
        raw = jnp.where(flip, 2.0 * line[0, half].astype(jnp.float32) - square, square)
        for i in range(3):
            for j in range(3):
                weight = jnp.where(core == half, pattern_ref[i, j], other_pattern_ref[i, j])
                at = (slice(i * TILE, (i + 1) * TILE), slice(j * TILE, (j + 1) * TILE))
                done[(half,) + at] = (raw[at] * weight.astype(jnp.float32)).astype(jnp.bfloat16)
    out_copy = pltpu.make_async_copy(done.at[core], out_ref.at[core], out_sem)
    out_copy.start()
    mine = terms_of(done[core].astype(jnp.float32), ham_ref, one_hot_of(atom_ref))
    mine = overlap_ref[...] + by_line(mine, -2.0)
    theirs = done[1 - core]
    give_ref[...] = theirs
    theirs = terms_of(theirs.astype(jnp.float32), other_ham_ref, one_hot_of(other_atom_ref))
    theirs = by_line(theirs, -2.0)
    zero, one = jnp.where(core == 0, mine, theirs), jnp.where(core == 0, theirs, mine)
    for part in range(SLABS):
        sums_ref[part] = zero
        sums_ref[SLABS + part] = one
    out_copy.wait()


def norm_kernel(parts_ref, velocities_ref, masses_ref, forces_ref, sums_ref, norms_ref):
    sums = parts_ref[0]
    for part in range(1, parts_ref.shape[0]):
        sums = sums + parts_ref[part]
    forces = sums[:3, : forces_ref.shape[1]]
    forces_ref[...] = forces
    sums_ref[...] = sums
    scaled = forces / jnp.sqrt(masses_ref[...])
    speeds = velocities_ref[...]
    rows = lax.broadcasted_iota(jnp.int32, norms_ref.shape, 1)
    norms_ref[...] = jnp.where(rows == 0, jnp.sum(scaled * scaled), jnp.sum(speeds * speeds))


def update_kernel(
    got_ref,
    half_ref,
    parts_ref,
    sums_ref,
    positions_ref,
    velocities_ref,
    masses_ref,
    out_ref,
    speeds_ref,
    places_ref,
    out_sem,
):
    del half_ref
    out_copy = pltpu.make_async_copy(got_ref, out_ref.at[1 - position()[1]], out_sem)
    out_copy.start()
    norms = parts_ref[0]
    for part in range(1, parts_ref.shape[0]):
        norms = norms + parts_ref[part]
    force_norm, speed_norm = norms[0:1, 0:1], norms[1:2, 0:1]
    root_mass = jnp.sqrt(masses_ref[...])
    scaled = sums_ref[:3, : speeds_ref.shape[1]] / root_mass
    speeds = (
        (1.0 - mixing) * velocities_ref[...]
        + mixing * jnp.sqrt(speed_norm) * scaled / jnp.sqrt(force_norm + epsilon)
        + time_step * scaled
    )
    speeds_ref[...] = speeds
    places_ref[...] = positions_ref[...] + time_step * speeds / root_mass
    out_copy.wait()


SMEM = pl.BlockSpec(memory_space=pltpu.SMEM)
VMEM = pl.BlockSpec(memory_space=pltpu.VMEM)
HBM = pl.BlockSpec(memory_space=pltpu.HBM)

COST = pl.CostEstimate(
    flops=4 * ROWS * ROWS * ROWS * SLABS,
    bytes_accessed=8 * ROWS * ROWS * SLABS,
    transcendentals=0,
)
PARAMS = pltpu.CompilerParams(vmem_limit_bytes=28 * 1024 * 1024)
LITTLE = pltpu.CompilerParams(vmem_limit_bytes=2 * 1024 * 1024)


def small(shape):
    return jax.ShapeDtypeStruct(shape, jnp.float32)


def local(
    density,
    weighted,
    ham_deriv,
    ovl_deriv,
    tile_pattern,
    branch,
    orbital_atom,
    positions,
    velocities,
    masses,
):
    block_type = jax.ShapeDtypeStruct((ROWS, ROWS), jnp.bfloat16)
    give = pl.pallas_call(
        give_kernel,
        out_shape=block_type,
        in_specs=[HBM],
        out_specs=VMEM,
        scratch_shapes=[pltpu.SemaphoreType.DMA],
        compiler_params=LITTLE,
    )(density)
    block = pl.pallas_call(
        block_kernel,
        out_shape=jax.ShapeDtypeStruct((HALVES, ROWS, ROWS), jnp.bfloat16),
        in_specs=[HBM, VMEM],
        out_specs=VMEM,
        scratch_shapes=[pltpu.SemaphoreType.DMA((2,))],
        compiler_params=LITTLE,
    )(density, send(give, core_swap()))
    wide, tall = gather(block)

    other_ham = send(ham_deriv, core_swap())
    other_atom = send(orbital_atom, core_swap())
    other_pattern = send(tile_pattern, core_swap())

    overlap = pl.pallas_call(
        overlap_kernel,
        out_shape=small((8, LANES)),
        in_specs=[VMEM] * 3,
        out_specs=VMEM,
        compiler_params=pltpu.CompilerParams(vmem_limit_bytes=4 * 1024 * 1024),
    )(orbital_atom, weighted, ovl_deriv)

    half, give, sums = pl.pallas_call(
        purify_kernel,
        out_shape=(
            jax.ShapeDtypeStruct((2, ROWS, ROWS), jnp.bfloat16),
            block_type,
            small((2 * SLABS, 8, LANES)),
        ),
        in_specs=[SMEM] * 3 + [VMEM] * 19,
        out_specs=(HBM, VMEM, VMEM),
        scratch_shapes=[
            pltpu.VMEM((SLABS, ROWS, ROWS), jnp.bfloat16),
            pltpu.VMEM((HALVES, ROWS, ROWS), jnp.float32),
            pltpu.VMEM((HALVES, ROWS, ROWS), jnp.bfloat16),
            pltpu.SemaphoreType.DMA,
        ],
        compiler_params=PARAMS,
        cost_estimate=COST,
    )(
        branch,
        tile_pattern,
        other_pattern,
        *wide,
        *tall,
        ham_deriv,
        other_ham,
        orbital_atom,
        other_atom,
        overlap,
    )
    got = send(give, core_swap())

    planes = [[(2 * z + c) * SLABS + i for c in range(2) for i in range(SLABS)] for z in range(8)]
    parts = lax.all_to_all(sums, AXES, 0, 0, axis_index_groups=planes)
    mass_row = masses[None, :]
    forces, sums, norms = pl.pallas_call(
        norm_kernel,
        out_shape=(small(positions.shape), small((8, LANES)), small((SLABS, 8, LANES))),
        in_specs=[VMEM] * 3,
        out_specs=(VMEM, VMEM, VMEM),
        compiler_params=LITTLE,
    )(parts, velocities, mass_row)
    parts = lax.all_to_all(norms, "row", 0, 0)
    purified, new_velocities, new_positions = pl.pallas_call(
        update_kernel,
        out_shape=(
            jax.ShapeDtypeStruct((2, ROWS, ROWS), jnp.bfloat16),
            small(positions.shape),
            small(positions.shape),
        ),
        in_specs=[HBM, HBM] + [VMEM] * 5,
        out_specs=(HBM, VMEM, VMEM),
        scratch_shapes=[pltpu.SemaphoreType.DMA],
        input_output_aliases={1: 0},
        compiler_params=LITTLE,
    )(got, half, parts, sums, positions, velocities, mass_row)
    return (purified, forces, new_velocities, new_positions)


def solution(mesh):
    in_specs = (
        P(None, "row", "col"),
        P("row", "col"),
        P(None, "row", "col"),
        P(None, "row", "col"),
        P("row", "col"),
        P(),
        P("row", None),
        P(None, "row"),
        P(None, "row"),
        P("row"),
    )
    out_specs = (P(None, "row", "col"), P(None, "row"), P(None, "row"), P(None, "row"))
    return jax.shard_map(local, mesh=mesh, in_specs=in_specs, out_specs=out_specs, check_vma=False)
```

time: 146 us -> 119 us (0.82)
  local copies, waits for them, and re-layouts: 27.7 us -> 2.13 us
  other arithmetic: 6.56 us -> 0.36 us
  waiting for transfers between devices: 40.4 us -> 45.4 us
  blocking collectives: 24.6 us -> 28.3 us
    unnamed x47 -> x20, local copies, waits for them, and re-layouts: 15.8 us -> 1.11 us
    squeeze x8 -> x4, local copies, waits for them, and re-layouts: 8.92 us -> 0.3 us  [the longest x1 0.12 us: gather(): line_fore[:, 1]]
    ppermute x25 -> x20, waiting for transfers between devices: 40.4 us -> 45.4 us  [send(): return lax.ppermute(value, AXES, table)]
    all_to_all x1, blocking collectives: 9.66 us -> 14.6 us  [local(): parts = lax.all_to_all(sums, AXES, 0, 0, axis_index_groups=planes)]
    another operation x6 -> x1, other arithmetic: 4.34 us -> 0.36 us  [gather(): line = jnp.stack([block, back, fore, far])]
    select_n x2 -> x0, other arithmetic: 1.59 us -> none  [the longest x1 1.09 us: local(): theirs = send(jnp.where(on_zero, density[1], density[0]), core_swap())]
    ppermute x25 -> x20, starting transfers between devices: 32.8 us -> 31.6 us  [send(): return lax.ppermute(value, AXES, table)]
    pallas_call x2 -> x4, Pallas kernels: 10.1 us -> 8.92 us  [the longest x1 7.4 us: local(): pl.pallas_call(purify_kernel, out_shape=(jax.ShapeDtypeStruct((2, ROWS, R...]
  transfers between devices with their start and end apart: 25 -> 20, of which waited for: 8 -> 8; matrix products, arithmetic and copies ran while one was open for 11% -> 1% of each run, Pallas kernels for 1% -> 1%
where the time goes in v5:
time: 119 us
  waiting for transfers between devices  45.4 us (38%)
  starting transfers between devices  31.6 us (27%)
  blocking collectives  28.3 us (24%)
  Pallas kernels  9.85 us (8%)
  local copies, waits for them, and re-layouts  2.13 us (2%)
    ppermute x20, waiting for transfers between devices, send(): return lax.ppermute(value, AXES, table)  45.4 us
    ppermute x20, starting transfers between devices, send(): return lax.ppermute(value, AXES, table)  31.6 us
    all_to_all x1, blocking collectives, local(): parts = lax.all_to_all(sums, AXES, 0, 0, axis_index_groups=planes)  14.6 us
    all_to_all x1, blocking collectives, local(): parts = lax.all_to_all(norms, 'row', 0, 0)  13.6 us
    pallas_call x1, Pallas kernels, local(): pl.pallas_call(purify_kernel, out_shape=(jax.ShapeDtypeStruct((2, ROWS, R...  7.4 us
  transfers between devices with their start and end apart: 20, of which 8 were waited for; matrix products, arithmetic and copies ran while one was open for 1% of the time, Pallas kernels for 1%

profile of v5, /device:TPU:1, one launch (start us, length us, event | category | flops | bytes accessed | tf_op | source)
XLA Modules:
  0.0 118.6 jit_solution(16735632376387713803)
XLA Ops:
  1.8 3.3 %collective-permute-start.1 = (bf16[384,384]{1,0:T(8,128)(2,1)S(1)}, bf16[384,384]{1,0:T(8,128)(2,1)S(1)}, u32[]{:S(2)}, u32[]{:S(2)}) collective-permute-start(bf16[384,384]{1,0:T(8,128)(2,1)S(1)} %shard_map.129), channel_id=1, source_target_pairs={{0,16},{1,17},{2,18},{3,19},{4,20},{5,21},{6,22},{7,23},{8,24},{9,... | collective-permute-start | bytes 884744 | tf_op jit(solution)/shard_map/ppermute | solution.py:52
  5.1 1.2 %collective-permute-done.1.got_ref = bf16[384,384]{1,0:T(8,128)(2,1)S(1)} collective-permute-done((bf16[384,384]{1,0:T(8,128)(2,1)S(1)}, bf16[384,384]{1,0:T(8,128)(2,1)S(1)}, u32[]{:S(2)}, u32[]{:S(2)}) %collective-permute-start.1) | collective-permute-done | bytes 294944 | tf_op jit(solution)/shard_map/ppermute | solution.py:52
  6.5 3.9 %collective-permute-start.6 = (bf16[2,384,384]{2,1,0:T(8,128)(2,1)S(1)}, bf16[2,384,384]{2,1,0:T(8,128)(2,1)S(1)}, u32[]{:S(2)}, u32[]{:S(2)}) collective-permute-start(bf16[2,384,384]{2,1,0:T(8,128)(2,1)S(1)} %shard_map.130.rest_5_), channel_id=1, source_target_pairs={{0,224},{1,225},{2,226},{3,227},{4,228},{5,229},{6,230},{7,231},{8... | collective-permute-start | bytes 1769480 | tf_op jit(solution)/shard_map/ppermute | solution.py:52
  10.5 1.2 %collective-permute-start.2 = (bf16[2,384,384]{2,1,0:T(8,128)(2,1)S(1)}, bf16[2,384,384]{2,1,0:T(8,128)(2,1)S(1)}, u32[]{:S(2)}, u32[]{:S(2)}) collective-permute-start(bf16[2,384,384]{2,1,0:T(8,128)(2,1)S(1)} %shard_map.130.rest_5_), channel_id=1, source_target_pairs={{0,1},{1,2},{2,3},{3,0},{4,5},{5,6},{6,7},{7,4},{8,9},{9,10},{10,1... | collective-permute-start | bytes 1769480 | tf_op jit(solution)/shard_map/ppermute | solution.py:52
  11.7 1.5 %collective-permute-start.3 = (bf16[2,384,384]{2,1,0:T(8,128)(2,1)S(1)}, bf16[2,384,384]{2,1,0:T(8,128)(2,1)S(1)}, u32[]{:S(2)}, u32[]{:S(2)}) collective-permute-start(bf16[2,384,384]{2,1,0:T(8,128)(2,1)S(1)} %shard_map.130.rest_5_), channel_id=1, source_target_pairs={{0,3},{1,0},{2,1},{3,2},{4,7},{5,4},{6,5},{7,6},{8,11},{9,8},{10,9... | collective-permute-start | bytes 1769480 | tf_op jit(solution)/shard_map/ppermute | solution.py:52
  13.1 1.5 %collective-permute-start.4 = (bf16[2,384,384]{2,1,0:T(8,128)(2,1)S(1)}, bf16[2,384,384]{2,1,0:T(8,128)(2,1)S(1)}, u32[]{:S(2)}, u32[]{:S(2)}) collective-permute-start(bf16[2,384,384]{2,1,0:T(8,128)(2,1)S(1)} %shard_map.130.rest_5_), channel_id=1, source_target_pairs={{0,2},{1,3},{2,0},{3,1},{4,6},{5,7},{6,4},{7,5},{8,10},{9,11},{10,... | collective-permute-start | bytes 1769480 | tf_op jit(solution)/shard_map/ppermute | solution.py:52
  14.7 9.1 %collective-permute-done.5.rest_6_ = bf16[2,384,384]{2,1,0:T(8,128)(2,1)S(1)} collective-permute-done((bf16[2,384,384]{2,1,0:T(8,128)(2,1)S(1)}, bf16[2,384,384]{2,1,0:T(8,128)(2,1)S(1)}, u32[]{:S(2)}, u32[]{:S(2)}) %collective-permute-start.5) | collective-permute-done | bytes 589856 | tf_op jit(solution)/shard_map/ppermute | solution.py:52
  23.8 4.2 %collective-permute-done.4 = bf16[2,384,384]{2,1,0:T(8,128)(2,1)S(1)} collective-permute-done((bf16[2,384,384]{2,1,0:T(8,128)(2,1)S(1)}, bf16[2,384,384]{2,1,0:T(8,128)(2,1)S(1)}, u32[]{:S(2)}, u32[]{:S(2)}) %collective-permute-start.4) | collective-permute-done | bytes 589856 | tf_op jit(solution)/shard_map/ppermute | solution.py:52
  28.4 2.8 %collective-permute-start.8 = (bf16[4,2,384,384]{3,2,0,1:T(8,128)(2,1)S(1)}, bf16[4,2,384,384]{3,2,0,1:T(8,128)(2,1)S(1)}, u32[]{:S(2)}, u32[]{:S(2)}) collective-permute-start(bf16[4,2,384,384]{3,2,0,1:T(8,128)(2,1)S(1)} %pad_maximum_fusion), channel_id=1, source_target_pairs={{0,12},{1,13},{2,14},{3,15},{4,0},{5,1},{6,2},{7,3},{8,4},{9,5},{1... | collective-permute-start | bytes 7077896 | tf_op jit(solution)/shard_map/ppermute | solution.py:52
  31.2 2.7 %collective-permute-start.11 = (bf16[2,384,384]{2,1,0:T(8,128)(2,1)S(1)}, bf16[2,384,384]{2,1,0:T(8,128)(2,1)S(1)}, u32[]{:S(2)}, u32[]{:S(2)}) collective-permute-start(bf16[2,384,384]{2,1,0:T(8,128)(2,1)S(1)} %collective-permute-done.6.rest_11_), channel_id=1, source_target_pairs={{0,224},{1,225},{2,226},{3,227},{4,228},{5,229},{6,230},{7,231},{8... | collective-permute-start | bytes 1769480 | tf_op jit(solution)/shard_map/ppermute | solution.py:52
  33.9 11.6 %collective-permute-done.9.rest_7_ = bf16[2,384,384]{2,1,0:T(8,128)(2,1)S(1)} collective-permute-done((bf16[2,384,384]{2,1,0:T(8,128)(2,1)S(1)}, bf16[2,384,384]{2,1,0:T(8,128)(2,1)S(1)}, u32[]{:S(2)}, u32[]{:S(2)}) %collective-permute-start.9) | collective-permute-done | bytes 589856 | tf_op jit(solution)/shard_map/ppermute | solution.py:52
  45.5 2.7 %collective-permute-start.12 = (bf16[2,384,384]{2,1,0:T(8,128)(2,1)S(1)}, bf16[2,384,384]{2,1,0:T(8,128)(2,1)S(1)}, u32[]{:S(2)}, u32[]{:S(2)}) collective-permute-start(bf16[2,384,384]{2,1,0:T(8,128)(2,1)S(1)} %collective-permute-done.11.rest_10_), channel_id=1, source_target_pairs={{0,224},{1,225},{2,226},{3,227},{4,228},{5,229},{6,230},{7,231},{8... | collective-permute-start | bytes 1769480 | tf_op jit(solution)/shard_map/ppermute | solution.py:52
  48.2 8.9 %collective-permute-done.8 = bf16[4,2,384,384]{3,2,0,1:T(8,128)(2,1)S(1)} collective-permute-done((bf16[4,2,384,384]{3,2,0,1:T(8,128)(2,1)S(1)}, bf16[4,2,384,384]{3,2,0,1:T(8,128)(2,1)S(1)}, u32[]{:S(2)}, u32[]{:S(2)}) %collective-permute-start.8) | collective-permute-done | bytes 2359328 | tf_op jit(solution)/shard_map/ppermute | solution.py:52
  57.2 3.3 %collective-permute-done.7 = bf16[4,2,384,384]{3,2,0,1:T(8,128)(2,1)S(1)} collective-permute-done((bf16[4,2,384,384]{3,2,0,1:T(8,128)(2,1)S(1)}, bf16[4,2,384,384]{3,2,0,1:T(8,128)(2,1)S(1)}, u32[]{:S(2)}, u32[]{:S(2)}) %collective-permute-start.7) | collective-permute-done | bytes 2359328 | tf_op jit(solution)/shard_map/ppermute | solution.py:52
  60.7 2.8 %collective-permute-start.14 = (bf16[4,384,384]{2,1,0:T(8,128)(2,1)S(1)}, bf16[4,384,384]{2,1,0:T(8,128)(2,1)S(1)}, u32[]{:S(2)}, u32[]{:S(2)}) collective-permute-start(bf16[4,384,384]{2,1,0:T(8,128)(2,1)S(1)} %slice_bitcast_fusion), channel_id=1, source_target_pairs={{0,12},{1,13},{2,14},{3,15},{4,0},{5,1},{6,2},{7,3},{8,4},{9,5},{1... | collective-permute-start | bytes 3538952 | tf_op jit(solution)/shard_map/ppermute | solution.py:52
  63.4 3.1 %collective-permute-start.17 = (bf16[3,384,384]{2,1,0:T(8,128)(2,1)S(1)}, bf16[3,384,384]{2,1,0:T(8,128)(2,1)S(1)}, u32[]{:S(2)}, u32[]{:S(2)}) collective-permute-start(bf16[3,384,384]{2,1,0:T(8,128)(2,1)S(1)} %copy-done.2), channel_id=1, source_target_pairs={{0,16},{1,17},{2,18},{3,19},{4,20},{5,21},{6,22},{7,23},{8,24},{9,... | collective-permute-start | bytes 2654216 | tf_op jit(solution)/shard_map/ppermute | solution.py:52
  67.1 1.5 %collective-permute-done.other_pattern_ref = s32[3,3]{1,0:T(4,128)S(1)} collective-permute-done((s32[3,3]{1,0:T(4,128)S(1)}, s32[3,3]{1,0:T(4,128)S(1)}, u32[]{:S(2)}, u32[]{:S(2)}) %collective-permute-start) | collective-permute-done | bytes 68 | tf_op jit(solution)/shard_map/ppermute | solution.py:52
  68.6 2.7 %collective-permute-start.16 = (bf16[384,384]{1,0:T(8,128)(2,1)S(1)}, bf16[384,384]{1,0:T(8,128)(2,1)S(1)}, u32[]{:S(2)}, u32[]{:S(2)}) collective-permute-start(bf16[384,384]{1,0:T(8,128)(2,1)S(1)} %slice_bitcast_fusion.2), channel_id=1, source_target_pairs={{0,224},{1,225},{2,226},{3,227},{4,228},{5,229},{6,230},{7,231},{8... | collective-permute-start | bytes 884744 | tf_op jit(solution)/shard_map/ppermute | solution.py:52
  72.4 5.6 %collective-permute-done.15.rest_12_ = bf16[384,384]{1,0:T(8,128)(2,1)S(1)} collective-permute-done((bf16[384,384]{1,0:T(8,128)(2,1)S(1)}, bf16[384,384]{1,0:T(8,128)(2,1)S(1)}, u32[]{:S(2)}, u32[]{:S(2)}) %collective-permute-start.15) | collective-permute-done | bytes 294944 | tf_op jit(solution)/shard_map/ppermute | solution.py:52
  78.1 7.4 %shard_map.132 = (bf16[2,384,384]{2,1,0:T(8,128)(2,1)}, bf16[384,384]{1,0:T(8,128)(2,1)S(1)}, f32[32,8,128]{2,1,0:T(8,128)S(1)}) custom-call(s32[2]{0:T(128)S(1)} %copy-done.9, s32[3,3]{1,0:T(4,128)S(1)} %copy-done.7, s32[3,3]{1,0:T(4,128)S(1)} %collective-permute-done.other_pattern_ref, bf16[4,2,384,384]{3,2,1,0:T(8,128)(2,1)S(1)} %copy.15.rest_0_, ...), custom_call_target="tpu_custom_call" | custom-call | flops 3623878656 | bytes 18874368 | tf_op jit(solution)/shard_map/pallas_call | solution.py:306
  85.5 2.7 %collective-permute-start.19 = (bf16[384,384]{1,0:T(8,128)(2,1)S(1)}, bf16[384,384]{1,0:T(8,128)(2,1)S(1)}, u32[]{:S(2)}, u32[]{:S(2)}) collective-permute-start(bf16[384,384]{1,0:T(8,128)(2,1)S(1)} %get-tuple-element.23), channel_id=1, source_target_pairs={{0,16},{1,17},{2,18},{3,19},{4,20},{5,21},{6,22},{7,23},{8,24},{9,... | collective-permute-start | bytes 884744 | tf_op jit(solution)/shard_map/ppermute | solution.py:52
  88.2 14.6 %all_to_all.10.parts_ref = f32[32,8,128]{2,1,0:T(8,128)S(1)} all-to-all(f32[32,8,128]{2,1,0:T(8,128)S(1)} %get-tuple-element.25), channel_id=1, replica_groups={{0,1,2,3,4,5,6,7,8,9,10,11,12,13,14,15,16,17,18,19,20,21,22,23,24,25,26..., dimensions={0} | all-to-all | bytes 262144 | tf_op jit(solution)/shard_map/all_to_all | solution.py:338
  103.4 13.6 %all_to_all.11.parts_ref = f32[16,8,128]{2,1,0:T(8,128)S(1)} all-to-all(f32[16,8,128]{2,1,0:T(8,128)S(1)} %get-tuple-element.26), channel_id=1, replica_groups=mesh['row'=16,'col'=16] {'row'}, dimensions={0} | all-to-all | bytes 131072 | tf_op jit(solution)/shard_map/all_to_all | solution.py:347
  117.1 1.3 %shard_map.134 = (bf16[2,384,384]{2,1,0:T(8,128)(2,1)}, f32[3,96]{1,0:T(4,128)}, f32[3,96]{1,0:T(4,128)}) custom-call(bf16[384,384]{1,0:T(8,128)(2,1)S(1)} %collective-permute-done.19.got_ref, bf16[2,384,384]{2,1,0:T(8,128)(2,1)} %get-tuple-element.24.half_ref, f32[16,8,128]{2,1,0:T(8,128)S(1)} %all_to_all.11.parts_ref, ...), custom_call_target="tpu_custom_call", output_to_operand_aliasing={{0}: (1, {})} | custom-call | tf_op jit(solution)/shard_map/pallas_call | solution.py:348
  (52 shorter events, 4.3 us)
Async XLA Ops:
  1.8 4.5 %collective-permute-start.1 = (bf16[384,384]{1,0:T(8,128)(2,1)S(1)}, bf16[384,384]{1,0:T(8,128)(2,1)S(1)}, u32[]{:S(2)}, u32[]{:S(2)}) collective-permute-start(bf16[384,384]{1,0:T(8,128)(2,1)S(1)} %shard_map.129), channel_id=1, source_target_pairs={{0,16},{1,17},{2,18},{3,19},{4,20},{5,21},{6,22},{7,23},{8,24},{9,... | collective-permute-start | bytes 884744 | tf_op jit(solution)/shard_map/ppermute | solution.py:52
  6.5 17.3 %collective-permute-start.5 = (bf16[2,384,384]{2,1,0:T(8,128)(2,1)S(1)}, bf16[2,384,384]{2,1,0:T(8,128)(2,1)S(1)}, u32[]{:S(2)}, u32[]{:S(2)}) collective-permute-start(bf16[2,384,384]{2,1,0:T(8,128)(2,1)S(1)} %shard_map.130.rest_5_), channel_id=1, source_target_pairs={{0,32},{1,33},{2,34},{3,35},{4,36},{5,37},{6,38},{7,39},{8,40},{9,... | collective-permute-start | bytes 1769480 | tf_op jit(solution)/shard_map/ppermute | solution.py:52
  6.5 17.2 %collective-permute-start.6 = (bf16[2,384,384]{2,1,0:T(8,128)(2,1)S(1)}, bf16[2,384,384]{2,1,0:T(8,128)(2,1)S(1)}, u32[]{:S(2)}, u32[]{:S(2)}) collective-permute-start(bf16[2,384,384]{2,1,0:T(8,128)(2,1)S(1)} %shard_map.130.rest_5_), channel_id=1, source_target_pairs={{0,224},{1,225},{2,226},{3,227},{4,228},{5,229},{6,230},{7,231},{8... | collective-permute-start | bytes 1769480 | tf_op jit(solution)/shard_map/ppermute | solution.py:52
  10.5 13.3 %collective-permute-start.2 = (bf16[2,384,384]{2,1,0:T(8,128)(2,1)S(1)}, bf16[2,384,384]{2,1,0:T(8,128)(2,1)S(1)}, u32[]{:S(2)}, u32[]{:S(2)}) collective-permute-start(bf16[2,384,384]{2,1,0:T(8,128)(2,1)S(1)} %shard_map.130.rest_5_), channel_id=1, source_target_pairs={{0,1},{1,2},{2,3},{3,0},{4,5},{5,6},{6,7},{7,4},{8,9},{9,10},{10,1... | collective-permute-start | bytes 1769480 | tf_op jit(solution)/shard_map/ppermute | solution.py:52
  11.7 12.1 %collective-permute-start.3 = (bf16[2,384,384]{2,1,0:T(8,128)(2,1)S(1)}, bf16[2,384,384]{2,1,0:T(8,128)(2,1)S(1)}, u32[]{:S(2)}, u32[]{:S(2)}) collective-permute-start(bf16[2,384,384]{2,1,0:T(8,128)(2,1)S(1)} %shard_map.130.rest_5_), channel_id=1, source_target_pairs={{0,3},{1,0},{2,1},{3,2},{4,7},{5,4},{6,5},{7,6},{8,11},{9,8},{10,9... | collective-permute-start | bytes 1769480 | tf_op jit(solution)/shard_map/ppermute | solution.py:52
  13.1 14.9 %collective-permute-start.4 = (bf16[2,384,384]{2,1,0:T(8,128)(2,1)S(1)}, bf16[2,384,384]{2,1,0:T(8,128)(2,1)S(1)}, u32[]{:S(2)}, u32[]{:S(2)}) collective-permute-start(bf16[2,384,384]{2,1,0:T(8,128)(2,1)S(1)} %shard_map.130.rest_5_), channel_id=1, source_target_pairs={{0,2},{1,3},{2,0},{3,1},{4,6},{5,7},{6,4},{7,5},{8,10},{9,11},{10,... | collective-permute-start | bytes 1769480 | tf_op jit(solution)/shard_map/ppermute | solution.py:52
  28.4 38.3 %copy-start.5 = (s32[1,384]{1,0:T(1,128)S(1)}, s32[1,384]{1,0:T(1,128)}, u32[]{:S(2)}) copy-start(s32[1,384]{1,0:T(1,128)} %rest_16_.1) | copy-start | bytes 4612
  28.4 42.9 %copy-start.1 = (bf16[3,384,384]{2,1,0:T(8,128)(2,1)S(1)}, bf16[3,384,384]{2,1,0:T(8,128)(2,1)}, u32[]{:S(2)}) copy-start(bf16[3,384,384]{2,1,0:T(8,128)(2,1)} %ovl_ref.1) | copy-start | bytes 2654212
  28.4 42.9 %copy-start.3 = (bf16[384,384]{1,0:T(8,128)(2,1)S(1)}, bf16[384,384]{1,0:T(8,128)(2,1)}, u32[]{:S(2)}) copy-start(bf16[384,384]{1,0:T(8,128)(2,1)} %weighted_ref.1) | copy-start | bytes 884740
  28.4 28.6 %collective-permute-start.8 = (bf16[4,2,384,384]{3,2,0,1:T(8,128)(2,1)S(1)}, bf16[4,2,384,384]{3,2,0,1:T(8,128)(2,1)S(1)}, u32[]{:S(2)}, u32[]{:S(2)}) collective-permute-start(bf16[4,2,384,384]{3,2,0,1:T(8,128)(2,1)S(1)} %pad_maximum_fusion), channel_id=1, source_target_pairs={{0,12},{1,13},{2,14},{3,15},{4,0},{5,1},{6,2},{7,3},{8,4},{9,5},{1... | collective-permute-start | bytes 7077896 | tf_op jit(solution)/shard_map/ppermute | solution.py:52
  31.2 29.2 %collective-permute-start.7 = (bf16[4,2,384,384]{3,2,0,1:T(8,128)(2,1)S(1)}, bf16[4,2,384,384]{3,2,0,1:T(8,128)(2,1)S(1)}, u32[]{:S(2)}, u32[]{:S(2)}) collective-permute-start(bf16[4,2,384,384]{3,2,0,1:T(8,128)(2,1)S(1)} %pad_maximum_fusion), channel_id=1, source_target_pairs={{0,4},{1,5},{2,6},{3,7},{4,8},{5,9},{6,10},{7,11},{8,12},{9,13},{1... | collective-permute-start | bytes 7077896 | tf_op jit(solution)/shard_map/ppermute | solution.py:52
  31.2 14.2 %collective-permute-start.9 = (bf16[2,384,384]{2,1,0:T(8,128)(2,1)S(1)}, bf16[2,384,384]{2,1,0:T(8,128)(2,1)S(1)}, u32[]{:S(2)}, u32[]{:S(2)}) collective-permute-start(bf16[2,384,384]{2,1,0:T(8,128)(2,1)S(1)} %collective-permute-done.5.rest_6_), channel_id=1, source_target_pairs={{0,32},{1,33},{2,34},{3,35},{4,36},{5,37},{6,38},{7,39},{8,40},{9,... | collective-permute-start | bytes 1769480 | tf_op jit(solution)/shard_map/ppermute | solution.py:52
  31.2 14.2 %collective-permute-start.11 = (bf16[2,384,384]{2,1,0:T(8,128)(2,1)S(1)}, bf16[2,384,384]{2,1,0:T(8,128)(2,1)S(1)}, u32[]{:S(2)}, u32[]{:S(2)}) collective-permute-start(bf16[2,384,384]{2,1,0:T(8,128)(2,1)S(1)} %collective-permute-done.6.rest_11_), channel_id=1, source_target_pairs={{0,224},{1,225},{2,226},{3,227},{4,228},{5,229},{6,230},{7,231},{8... | collective-permute-start | bytes 1769480 | tf_op jit(solution)/shard_map/ppermute | solution.py:52
  45.5 15.1 %collective-permute-start.10 = (bf16[2,384,384]{2,1,0:T(8,128)(2,1)S(1)}, bf16[2,384,384]{2,1,0:T(8,128)(2,1)S(1)}, u32[]{:S(2)}, u32[]{:S(2)}) collective-permute-start(bf16[2,384,384]{2,1,0:T(8,128)(2,1)S(1)} %collective-permute-done.9.rest_7_), channel_id=1, source_target_pairs={{0,32},{1,33},{2,34},{3,35},{4,36},{5,37},{6,38},{7,39},{8,40},{9,... | collective-permute-start | bytes 1769480 | tf_op jit(solution)/shard_map/ppermute | solution.py:52
  45.5 15.1 %collective-permute-start.12 = (bf16[2,384,384]{2,1,0:T(8,128)(2,1)S(1)}, bf16[2,384,384]{2,1,0:T(8,128)(2,1)S(1)}, u32[]{:S(2)}, u32[]{:S(2)}) collective-permute-start(bf16[2,384,384]{2,1,0:T(8,128)(2,1)S(1)} %collective-permute-done.11.rest_10_), channel_id=1, source_target_pairs={{0,224},{1,225},{2,226},{3,227},{4,228},{5,229},{6,230},{7,231},{8... | collective-permute-start | bytes 1769480 | tf_op jit(solution)/shard_map/ppermute | solution.py:52
  60.6 17.5 %collective-permute-start.13 = (bf16[4,384,384]{2,1,0:T(8,128)(2,1)S(1)}, bf16[4,384,384]{2,1,0:T(8,128)(2,1)S(1)}, u32[]{:S(2)}, u32[]{:S(2)}) collective-permute-start(bf16[4,384,384]{2,1,0:T(8,128)(2,1)S(1)} %slice_bitcast_fusion.1), channel_id=1, source_target_pairs={{0,4},{1,5},{2,6},{3,7},{4,8},{5,9},{6,10},{7,11},{8,12},{9,13},{1... | collective-permute-start | bytes 3538952 | tf_op jit(solution)/shard_map/ppermute | solution.py:52
  60.7 17.4 %collective-permute-start.14 = (bf16[4,384,384]{2,1,0:T(8,128)(2,1)S(1)}, bf16[4,384,384]{2,1,0:T(8,128)(2,1)S(1)}, u32[]{:S(2)}, u32[]{:S(2)}) collective-permute-start(bf16[4,384,384]{2,1,0:T(8,128)(2,1)S(1)} %slice_bitcast_fusion), channel_id=1, source_target_pairs={{0,12},{1,13},{2,14},{3,15},{4,0},{5,1},{6,2},{7,3},{8,4},{9,5},{1... | collective-permute-start | bytes 3538952 | tf_op jit(solution)/shard_map/ppermute | solution.py:52
  63.4 9.0 %collective-permute-start.17 = (bf16[3,384,384]{2,1,0:T(8,128)(2,1)S(1)}, bf16[3,384,384]{2,1,0:T(8,128)(2,1)S(1)}, u32[]{:S(2)}, u32[]{:S(2)}) collective-permute-start(bf16[3,384,384]{2,1,0:T(8,128)(2,1)S(1)} %copy-done.2), channel_id=1, source_target_pairs={{0,16},{1,17},{2,18},{3,19},{4,20},{5,21},{6,22},{7,23},{8,24},{9,... | collective-permute-start | bytes 2654216 | tf_op jit(solution)/shard_map/ppermute | solution.py:52
  66.5 2.1 %collective-permute-start = (s32[3,3]{1,0:T(4,128)S(1)}, s32[3,3]{1,0:T(4,128)S(1)}, u32[]{:S(2)}, u32[]{:S(2)}) collective-permute-start(s32[3,3]{1,0:T(4,128)S(1)} %copy-done.7), channel_id=1, source_target_pairs={{0,16},{1,17},{2,18},{3,19},{4,20},{5,21},{6,22},{7,23},{8,24},{9,... | collective-permute-start | bytes 116 | tf_op jit(solution)/shard_map/ppermute | solution.py:52
  66.6 2.0 %collective-permute-start.18 = (s32[1,384]{1,0:T(1,128)S(1)}, s32[1,384]{1,0:T(1,128)S(1)}, u32[]{:S(2)}, u32[]{:S(2)}) collective-permute-start(s32[1,384]{1,0:T(1,128)S(1)} %copy-done.5), channel_id=1, source_target_pairs={{0,16},{1,17},{2,18},{3,19},{4,20},{5,21},{6,22},{7,23},{8,24},{9,... | collective-permute-start | bytes 4616 | tf_op jit(solution)/shard_map/ppermute | solution.py:52
  68.6 9.4 %collective-permute-start.15 = (bf16[384,384]{1,0:T(8,128)(2,1)S(1)}, bf16[384,384]{1,0:T(8,128)(2,1)S(1)}, u32[]{:S(2)}, u32[]{:S(2)}) collective-permute-start(bf16[384,384]{1,0:T(8,128)(2,1)S(1)} %slice_bitcast_fusion.3), channel_id=1, source_target_pairs={{0,32},{1,33},{2,34},{3,35},{4,36},{5,37},{6,38},{7,39},{8,40},{9,... | collective-permute-start | bytes 884744 | tf_op jit(solution)/shard_map/ppermute | solution.py:52
  68.6 9.4 %collective-permute-start.16 = (bf16[384,384]{1,0:T(8,128)(2,1)S(1)}, bf16[384,384]{1,0:T(8,128)(2,1)S(1)}, u32[]{:S(2)}, u32[]{:S(2)}) collective-permute-start(bf16[384,384]{1,0:T(8,128)(2,1)S(1)} %slice_bitcast_fusion.2), channel_id=1, source_target_pairs={{0,224},{1,225},{2,226},{3,227},{4,228},{5,229},{6,230},{7,231},{8... | collective-permute-start | bytes 884744 | tf_op jit(solution)/shard_map/ppermute | solution.py:52
  72.4 44.7 %copy-start.8 = (f32[3,96]{1,0:T(4,128)S(1)}, f32[3,96]{1,0:T(4,128)}, u32[]{:S(2)}) copy-start(f32[3,96]{1,0:T(4,128)} %positions_ref.1) | copy-start | bytes 3460
  85.5 31.6 %collective-permute-start.19 = (bf16[384,384]{1,0:T(8,128)(2,1)S(1)}, bf16[384,384]{1,0:T(8,128)(2,1)S(1)}, u32[]{:S(2)}, u32[]{:S(2)}) collective-permute-start(bf16[384,384]{1,0:T(8,128)(2,1)S(1)} %get-tuple-element.23), channel_id=1, source_target_pairs={{0,16},{1,17},{2,18},{3,19},{4,20},{5,21},{6,22},{7,23},{8,24},{9,... | collective-permute-start | bytes 884744 | tf_op jit(solution)/shard_map/ppermute | solution.py:52
  (6 other events, 141.1 us)

commit v6 on v5

--- a/solution.py
+++ b/solution.py
@@ -112,17 +112,20 @@
     return (jnp.transpose(atoms) == lanes).astype(jnp.float32)
 
 
-def by_line(rows, scale):
+def by_line(zero, one, scale):
     lines = lax.broadcasted_iota(jnp.int32, (8, LANES), 0)
     out = jnp.zeros((8, LANES), jnp.float32)
     for x in range(3):
-        out = jnp.where(lines == x, scale * rows[x], out)
+        out = jnp.where(lines == x, scale * zero[x], out)
+        out = jnp.where(lines == 3 + x, scale * one[x], out)
     return out
 
 
 def overlap_kernel(atom_ref, weighted_ref, ovl_ref, out_ref):
     rows = terms_of(weighted_ref[...].astype(jnp.float32), ovl_ref, one_hot_of(atom_ref))
-    out_ref[...] = by_line(rows, 2.0)
+    lines = lax.broadcasted_iota(jnp.int32, (8, LANES), 0)
+    own = (lines >= 3) == (position()[1] == 1)
+    out_ref[...] = jnp.where(own, by_line(rows, rows, 2.0), 0.0)
 
 
 def give_kernel(density_ref, give_ref, sem):
@@ -142,42 +145,97 @@
     theirs.wait()
 
 
-def purify_kernel(branch_ref, pattern_ref, other_pattern_ref, *rest):
-    wide, tall, rest = rest[:5], rest[5:14], rest[14:]
-    ham_ref, other_ham_ref, atom_ref, other_atom_ref, overlap_ref = rest[:5]
-    out_ref, give_ref, sums_ref, b_buf, total, done, out_sem = rest[5:]
-    line = wide[0]
-    z, core, at_x, at_y = position()
+def slot_of(level, half):
+    _, core, at_x, at_y = position()
+    slab = (level & 7) * 2 + half
+    by_x, by_y = ((slab >> 2) - at_x) & 3, ((slab & 3) - at_y) & 3
+    first = jnp.where(core == 0, by_y, by_x)
+    second = jnp.where(core == 0, by_x, by_y)
+    first = jnp.where(first == 3, 1, first + jnp.minimum(first, 1))
+    second = jnp.where(second == 3, 1, second + jnp.minimum(second, 1))
+    return second * 4 + first
+
+
+NEAR = 12
+
+
+def near_kernel(*refs):
+    wide, tall, (total_ref, b_far_ref, a_far_ref, b_buf) = refs[:3], refs[3:10], refs[10:]
+    z = position()[0]
     for half in range(HALVES):
-        for level, offset in enumerate(LEVELS + (4,)):
-            slab = ((z + offset) & 7) * 2 + half
-            by_x, by_y = ((slab >> 2) - at_x) & 3, ((slab & 3) - at_y) & 3
-            first = jnp.where(core == 0, by_y, by_x)
-            second = jnp.where(core == 0, by_x, by_y)
-            first = jnp.where(first == 3, 1, first + jnp.minimum(first, 1))
-            second = jnp.where(second == 3, 1, second + jnp.minimum(second, 1))
-            slot = second * 4 + first
-            b_buf[slot] = tall[level][half] if level < 7 else tall[7 + half][...]
-    for group in range(4):
+        for level, offset in enumerate(LEVELS):
+            b_buf[slot_of(z + offset, half)] = tall[level][half]
+        slot = slot_of(z + 4, half)
+        b_buf[slot] = jnp.zeros((ROWS, ROWS), jnp.bfloat16)
+
+        @pl.when(slot >= NEAR)
+        def _():
+            a_far_ref[half] = jnp.zeros(a_far_ref.shape[1:], jnp.bfloat16)
+
+        for t in range(NEAR):
+
+            @pl.when(slot == t)
+            def _():
+                a_far_ref[half] = wide[t // 4][t % 4]
+
+    b_far_ref[...] = b_buf[NEAR:]
+    for group in range(3):
         rows = b_buf[4 * group : 4 * group + 4].reshape(4 * ROWS, ROWS)
         for half in range(HALVES):
-            if group < 3:
-                slabs = [wide[group][i, half] for i in range(4)]
-            else:
-                slabs = [wide[3 + half][i] for i in range(4)]
             product = jnp.dot(
-                jnp.concatenate(slabs, axis=1),
+                jnp.concatenate([wide[group][i, half] for i in range(4)], axis=1),
                 rows,
                 preferred_element_type=jnp.float32,
             )
             if group == 0:
-                total[half] = product
+                total_ref[half] = product
             else:
-                total[half] += product
+                total_ref[half] += product
+
+
+def purify_kernel(
+    branch_ref,
+    pattern_ref,
+    other_pattern_ref,
+    block_ref,
+    line_low,
+    line_high,
+    z_low,
+    z_high,
+    total_ref,
+    b_far_ref,
+    a_far_ref,
+    ham_ref,
+    other_ham_ref,
+    atom_ref,
+    other_atom_ref,
+    overlap_ref,
+    out_ref,
+    give_ref,
+    sums_ref,
+    b_buf,
+    done,
+    out_sem,
+):
+    z, core, _, _ = position()
+    b_buf[: SLABS - NEAR] = b_far_ref[...]
+    for half, piece in enumerate((z_low, z_high)):
+        slot = slot_of(z + 4, half)
+        b_buf[SLABS - NEAR + half] = piece[...]
+
+        @pl.when(slot >= NEAR)
+        def _():
+            b_buf[slot - NEAR] = piece[...]
+
+    rows = b_buf[...].reshape((SLABS - NEAR + 2) * ROWS, ROWS)
     for half in range(HALVES):
-        square = total[half]
+        lead = line_low if half == 0 else line_high
+        columns = [lead[i] for i in range(4)] + [a_far_ref[i, half] for i in range(2)]
+        square = total_ref[half] + jnp.dot(
+            jnp.concatenate(columns, axis=1), rows, preferred_element_type=jnp.float32
+        )
         flip = branch_ref[core] == 1
-        raw = jnp.where(flip, 2.0 * line[0, half].astype(jnp.float32) - square, square)
+        raw = jnp.where(flip, 2.0 * block_ref[half].astype(jnp.float32) - square, square)
         for i in range(3):
             for j in range(3):
                 weight = jnp.where(core == half, pattern_ref[i, j], other_pattern_ref[i, j])
@@ -186,53 +244,62 @@
     out_copy = pltpu.make_async_copy(done.at[core], out_ref.at[core], out_sem)
     out_copy.start()
     mine = terms_of(done[core].astype(jnp.float32), ham_ref, one_hot_of(atom_ref))
-    mine = overlap_ref[...] + by_line(mine, -2.0)
     theirs = done[1 - core]
     give_ref[...] = theirs
     theirs = terms_of(theirs.astype(jnp.float32), other_ham_ref, one_hot_of(other_atom_ref))
-    theirs = by_line(theirs, -2.0)
-    zero, one = jnp.where(core == 0, mine, theirs), jnp.where(core == 0, theirs, mine)
+    zero = [jnp.where(core == 0, a, b) for a, b in zip(mine, theirs)]
+    one = [jnp.where(core == 0, b, a) for a, b in zip(mine, theirs)]
+    sums = overlap_ref[...] + by_line(zero, one, -2.0)
     for part in range(SLABS):
-        sums_ref[part] = zero
-        sums_ref[SLABS + part] = one
+        sums_ref[part] = sums
     out_copy.wait()
 
 
-def norm_kernel(parts_ref, velocities_ref, masses_ref, forces_ref, sums_ref, norms_ref):
+def norm_kernel(parts_ref, velocities_ref, masses_ref, all_ref):
     sums = parts_ref[0]
     for part in range(1, parts_ref.shape[0]):
         sums = sums + parts_ref[part]
-    forces = sums[:3, : forces_ref.shape[1]]
-    forces_ref[...] = forces
-    sums_ref[...] = sums
-    scaled = forces / jnp.sqrt(masses_ref[...])
     speeds = velocities_ref[...]
-    rows = lax.broadcasted_iota(jnp.int32, norms_ref.shape, 1)
-    norms_ref[...] = jnp.where(rows == 0, jnp.sum(scaled * scaled), jnp.sum(speeds * speeds))
+    atoms = masses_ref.shape[1]
+    for part in range(all_ref.shape[0]):
+        all_ref[part] = sums
+        all_ref[part, 6:7, :] = jnp.ones((1, LANES), jnp.float32)
+        all_ref[part, 6:7, :atoms] = masses_ref[...]
+        all_ref[part, 7:8, :] = jnp.broadcast_to(jnp.sum(speeds * speeds), (1, LANES))
 
 
 def update_kernel(
     got_ref,
     half_ref,
-    parts_ref,
-    sums_ref,
+    all_ref,
     positions_ref,
     velocities_ref,
     masses_ref,
     out_ref,
+    forces_ref,
     speeds_ref,
     places_ref,
     out_sem,
 ):
     del half_ref
-    out_copy = pltpu.make_async_copy(got_ref, out_ref.at[1 - position()[1]], out_sem)
+    z, core, _, _ = position()
+    out_copy = pltpu.make_async_copy(got_ref, out_ref.at[1 - core], out_sem)
     out_copy.start()
-    norms = parts_ref[0]
-    for part in range(1, parts_ref.shape[0]):
-        norms = norms + parts_ref[part]
-    force_norm, speed_norm = norms[0:1, 0:1], norms[1:2, 0:1]
+    squares = jnp.zeros((3, LANES), jnp.float32)
+    speed_norm = jnp.zeros((1, 1), jnp.float32)
+    for level in range(all_ref.shape[0] // 2):
+        zero, one = all_ref[2 * level], all_ref[2 * level + 1]
+        both = zero + one
+        for half, mass in enumerate((zero[6:7], one[6:7])):
+            scaled = both[3 * half : 3 * half + 3] / jnp.sqrt(mass)
+            squares = squares + scaled * scaled
+        speed_norm = speed_norm + zero[7:8, 0:1] + one[7:8, 0:1]
+    force_norm = jnp.sum(squares)
+    both = all_ref[2 * z] + all_ref[2 * z + 1]
+    forces = jnp.where(core == 0, both[0:3], both[3:6])[:, : forces_ref.shape[1]]
+    forces_ref[...] = forces
     root_mass = jnp.sqrt(masses_ref[...])
-    scaled = sums_ref[:3, : speeds_ref.shape[1]] / root_mass
+    scaled = forces / root_mass
     speeds = (
         (1.0 - mixing) * velocities_ref[...]
         + mixing * jnp.sqrt(speed_norm) * scaled / jnp.sqrt(force_norm + epsilon)
@@ -247,12 +314,15 @@
 VMEM = pl.BlockSpec(memory_space=pltpu.VMEM)
 HBM = pl.BlockSpec(memory_space=pltpu.HBM)
 
-COST = pl.CostEstimate(
-    flops=4 * ROWS * ROWS * ROWS * SLABS,
-    bytes_accessed=8 * ROWS * ROWS * SLABS,
-    transcendentals=0,
-)
-PARAMS = pltpu.CompilerParams(vmem_limit_bytes=28 * 1024 * 1024)
+def cost(slots):
+    return pl.CostEstimate(
+        flops=4 * ROWS * ROWS * ROWS * slots,
+        bytes_accessed=8 * ROWS * ROWS * slots,
+        transcendentals=0,
+    )
+
+
+PARAMS = pltpu.CompilerParams(vmem_limit_bytes=12 * 1024 * 1024)
 LITTLE = pltpu.CompilerParams(vmem_limit_bytes=2 * 1024 * 1024)
 
 
@@ -272,10 +342,9 @@
     velocities,
     masses,
 ):
-    block_type = jax.ShapeDtypeStruct((ROWS, ROWS), jnp.bfloat16)
     give = pl.pallas_call(
         give_kernel,
-        out_shape=block_type,
+        out_shape=jax.ShapeDtypeStruct((ROWS, ROWS), jnp.bfloat16),
         in_specs=[HBM],
         out_specs=VMEM,
         scratch_shapes=[pltpu.SemaphoreType.DMA],
@@ -303,29 +372,45 @@
         compiler_params=pltpu.CompilerParams(vmem_limit_bytes=4 * 1024 * 1024),
     )(orbital_atom, weighted, ovl_deriv)
 
+    total, b_far, a_far = pl.pallas_call(
+        near_kernel,
+        out_shape=(
+            small((HALVES, ROWS, ROWS)),
+            jax.ShapeDtypeStruct((SLABS - NEAR, ROWS, ROWS), jnp.bfloat16),
+            jax.ShapeDtypeStruct((2, HALVES, ROWS, ROWS), jnp.bfloat16),
+        ),
+        in_specs=[VMEM] * 10,
+        out_specs=(VMEM,) * 3,
+        scratch_shapes=[pltpu.VMEM((SLABS, ROWS, ROWS), jnp.bfloat16)],
+        compiler_params=PARAMS,
+        cost_estimate=cost(NEAR),
+    )(*wide[:3], *tall[:7])
     half, give, sums = pl.pallas_call(
         purify_kernel,
         out_shape=(
             jax.ShapeDtypeStruct((2, ROWS, ROWS), jnp.bfloat16),
-            block_type,
-            small((2 * SLABS, 8, LANES)),
+            jax.ShapeDtypeStruct((ROWS, ROWS), jnp.bfloat16),
+            small((SLABS, 8, LANES)),
         ),
-        in_specs=[SMEM] * 3 + [VMEM] * 19,
+        in_specs=[SMEM] * 3 + [VMEM] * 13,
         out_specs=(HBM, VMEM, VMEM),
         scratch_shapes=[
-            pltpu.VMEM((SLABS, ROWS, ROWS), jnp.bfloat16),
-            pltpu.VMEM((HALVES, ROWS, ROWS), jnp.float32),
+            pltpu.VMEM((SLABS - NEAR + 2, ROWS, ROWS), jnp.bfloat16),
             pltpu.VMEM((HALVES, ROWS, ROWS), jnp.bfloat16),
             pltpu.SemaphoreType.DMA,
         ],
         compiler_params=PARAMS,
-        cost_estimate=COST,
+        cost_estimate=cost(SLABS - NEAR + 2),
     )(
         branch,
         tile_pattern,
         other_pattern,
-        *wide,
-        *tall,
+        block,
+        *wide[3:],
+        *tall[7:],
+        total,
+        b_far,
+        a_far,
         ham_deriv,
         other_ham,
         orbital_atom,
@@ -334,30 +419,26 @@
     )
     got = send(give, core_swap())
 
-    planes = [[(2 * z + c) * SLABS + i for c in range(2) for i in range(SLABS)] for z in range(8)]
-    parts = lax.all_to_all(sums, AXES, 0, 0, axis_index_groups=planes)
+    parts = lax.all_to_all(sums, "col", 0, 0)
     mass_row = masses[None, :]
-    forces, sums, norms = pl.pallas_call(
+    parts = pl.pallas_call(
         norm_kernel,
-        out_shape=(small(positions.shape), small((8, LANES)), small((SLABS, 8, LANES))),
+        out_shape=small((SLABS, 8, LANES)),
         in_specs=[VMEM] * 3,
-        out_specs=(VMEM, VMEM, VMEM),
+        out_specs=VMEM,
         compiler_params=LITTLE,
     )(parts, velocities, mass_row)
-    parts = lax.all_to_all(norms, "row", 0, 0)
-    purified, new_velocities, new_positions = pl.pallas_call(
+    parts = lax.all_to_all(parts, "row", 0, 0)
+    purified, forces, new_velocities, new_positions = pl.pallas_call(
         update_kernel,
-        out_shape=(
-            jax.ShapeDtypeStruct((2, ROWS, ROWS), jnp.bfloat16),
-            small(positions.shape),
-            small(positions.shape),
-        ),
-        in_specs=[HBM, HBM] + [VMEM] * 5,
-        out_specs=(HBM, VMEM, VMEM),
+        out_shape=(jax.ShapeDtypeStruct((2, ROWS, ROWS), jnp.bfloat16),)
+        + (small(positions.shape),) * 3,
+        in_specs=[HBM, HBM] + [VMEM] * 4,
+        out_specs=(HBM, VMEM, VMEM, VMEM),
         scratch_shapes=[pltpu.SemaphoreType.DMA],
         input_output_aliases={1: 0},
         compiler_params=LITTLE,
-    )(got, half, parts, sums, positions, velocities, mass_row)
+    )(got, half, parts, positions, velocities, mass_row)
     return (purified, forces, new_velocities, new_positions)
 
 

time: 119 us -> 113 us (0.950)
  waiting for transfers between devices: 45.4 us -> 39.5 us
  blocking collectives: 28.3 us -> 25.3 us
  starting transfers between devices: 31.6 us -> 33.5 us
    ppermute x20, waiting for transfers between devices: 45.4 us -> 39.5 us  [send(): return lax.ppermute(value, AXES, table)]
    pallas_call x2 -> x3, Pallas kernels: 0.68 us -> 4.75 us  [the longest x1 4.56 us: local(): pl.pallas_call(near_kernel, out_shape=(small((HALVES, ROWS, ROWS)), jax.S...]
    pallas_call x1, Pallas kernels: 7.4 us -> 4.04 us  [local(): pl.pallas_call(purify_kernel, out_shape=(jax.ShapeDtypeStruct((2, ROWS, R...]
    all_to_all x2, blocking collectives: 28.3 us -> 25.3 us  [the longest x1 14.8 us: local(): parts = lax.all_to_all(parts, 'row', 0, 0)]
    ppermute x20, starting transfers between devices: 31.6 us -> 33.5 us  [send(): return lax.ppermute(value, AXES, table)]
  transfers between devices with their start and end apart: 20 -> 20, of which waited for: 8 -> 9; matrix products, arithmetic and copies ran while one was open for 1% -> 1% of each run, Pallas kernels for 1% -> 4%
where the time goes in v6:
time: 113 us; the launch traced here: 112 us
  waiting for transfers between devices  39.5 us (35%)
  starting transfers between devices  33.5 us (30%)
  blocking collectives  25.3 us (22%)
  Pallas kernels  10.6 us (9%)
  local copies, waits for them, and re-layouts  2.17 us (2%)
    ppermute x20, waiting for transfers between devices, send(): return lax.ppermute(value, AXES, table)  39.5 us
    ppermute x20, starting transfers between devices, send(): return lax.ppermute(value, AXES, table)  33.5 us
    all_to_all x1, blocking collectives, local(): parts = lax.all_to_all(parts, 'row', 0, 0)  14.8 us
    all_to_all x1, blocking collectives, local(): parts = lax.all_to_all(sums, 'col', 0, 0)  10.5 us
    pallas_call x1, Pallas kernels, local(): pl.pallas_call(near_kernel, out_shape=(small((HALVES, ROWS, ROWS)), jax.S...  4.56 us
    pallas_call x1, Pallas kernels, local(): pl.pallas_call(purify_kernel, out_shape=(jax.ShapeDtypeStruct((2, ROWS, R...  4.04 us
  transfers between devices with their start and end apart: 20, of which 9 were waited for; matrix products, arithmetic and copies ran while one was open for 1% of the time, Pallas kernels for 4%

profile of v6, /device:TPU:1, one launch (start us, length us, event | category | flops | bytes accessed | tf_op | source)
XLA Modules:
  0.0 112.4 jit_solution(2196952273063843910)
XLA Ops:
  1.8 3.3 %collective-permute-start.1 = (bf16[384,384]{1,0:T(8,128)(2,1)S(1)}, bf16[384,384]{1,0:T(8,128)(2,1)S(1)}, u32[]{:S(2)}, u32[]{:S(2)}) collective-permute-start(bf16[384,384]{1,0:T(8,128)(2,1)S(1)} %shard_map.129), channel_id=1, source_target_pairs={{0,16},{1,17},{2,18},{3,19},{4,20},{5,21},{6,22},{7,23},{8,24},{9,... | collective-permute-start | bytes 884744 | tf_op jit(solution)/shard_map/ppermute | solution.py:52
  5.1 1.2 %collective-permute-done.1.got_ref = bf16[384,384]{1,0:T(8,128)(2,1)S(1)} collective-permute-done((bf16[384,384]{1,0:T(8,128)(2,1)S(1)}, bf16[384,384]{1,0:T(8,128)(2,1)S(1)}, u32[]{:S(2)}, u32[]{:S(2)}) %collective-permute-start.1) | collective-permute-done | bytes 294944 | tf_op jit(solution)/shard_map/ppermute | solution.py:52
  6.5 2.7 %collective-permute-start.3 = (bf16[2,384,384]{2,1,0:T(8,128)(2,1)S(1)}, bf16[2,384,384]{2,1,0:T(8,128)(2,1)S(1)}, u32[]{:S(2)}, u32[]{:S(2)}) collective-permute-start(bf16[2,384,384]{2,1,0:T(8,128)(2,1)S(1)} %shard_map.130.refs_3_.block_ref), channel_id=1, source_target_pairs={{0,3},{1,0},{2,1},{3,2},{4,7},{5,4},{6,5},{7,6},{8,11},{9,8},{10,9... | collective-permute-start | bytes 1769480 | tf_op jit(solution)/shard_map/ppermute | solution.py:52
  9.2 1.4 %collective-permute-start.5 = (bf16[2,384,384]{2,1,0:T(8,128)(2,1)S(1)}, bf16[2,384,384]{2,1,0:T(8,128)(2,1)S(1)}, u32[]{:S(2)}, u32[]{:S(2)}) collective-permute-start(bf16[2,384,384]{2,1,0:T(8,128)(2,1)S(1)} %shard_map.130.refs_3_.block_ref), channel_id=1, source_target_pairs={{0,32},{1,33},{2,34},{3,35},{4,36},{5,37},{6,38},{7,39},{8,40},{9,... | collective-permute-start | bytes 1769480 | tf_op jit(solution)/shard_map/ppermute | solution.py:52
  10.6 3.9 %collective-permute-start.6 = (bf16[2,384,384]{2,1,0:T(8,128)(2,1)S(1)}, bf16[2,384,384]{2,1,0:T(8,128)(2,1)S(1)}, u32[]{:S(2)}, u32[]{:S(2)}) collective-permute-start(bf16[2,384,384]{2,1,0:T(8,128)(2,1)S(1)} %shard_map.130.refs_3_.block_ref), channel_id=1, source_target_pairs={{0,224},{1,225},{2,226},{3,227},{4,228},{5,229},{6,230},{7,231},{8... | collective-permute-start | bytes 1769480 | tf_op jit(solution)/shard_map/ppermute | solution.py:52
  14.6 8.5 %collective-permute-done.2 = bf16[2,384,384]{2,1,0:T(8,128)(2,1)S(1)} collective-permute-done((bf16[2,384,384]{2,1,0:T(8,128)(2,1)S(1)}, bf16[2,384,384]{2,1,0:T(8,128)(2,1)S(1)}, u32[]{:S(2)}, u32[]{:S(2)}) %collective-permute-start.2) | collective-permute-done | bytes 589856 | tf_op jit(solution)/shard_map/ppermute | solution.py:52
  23.1 3.7 %collective-permute-done.5.refs_4_ = bf16[2,384,384]{2,1,0:T(8,128)(2,1)S(1)} collective-permute-done((bf16[2,384,384]{2,1,0:T(8,128)(2,1)S(1)}, bf16[2,384,384]{2,1,0:T(8,128)(2,1)S(1)}, u32[]{:S(2)}, u32[]{:S(2)}) %collective-permute-start.5) | collective-permute-done | bytes 589856 | tf_op jit(solution)/shard_map/ppermute | solution.py:52
  27.3 2.4 %collective-permute-start.7 = (bf16[4,2,384,384]{3,2,0,1:T(8,128)(2,1)S(1)}, bf16[4,2,384,384]{3,2,0,1:T(8,128)(2,1)S(1)}, u32[]{:S(2)}, u32[]{:S(2)}) collective-permute-start(bf16[4,2,384,384]{3,2,0,1:T(8,128)(2,1)S(1)} %pad_maximum_fusion), channel_id=1, source_target_pairs={{0,4},{1,5},{2,6},{3,7},{4,8},{5,9},{6,10},{7,11},{8,12},{9,13},{1... | collective-permute-start | bytes 7077896 | tf_op jit(solution)/shard_map/ppermute | solution.py:52
  29.7 1.5 %collective-permute-start.8 = (bf16[4,2,384,384]{3,2,0,1:T(8,128)(2,1)S(1)}, bf16[4,2,384,384]{3,2,0,1:T(8,128)(2,1)S(1)}, u32[]{:S(2)}, u32[]{:S(2)}) collective-permute-start(bf16[4,2,384,384]{3,2,0,1:T(8,128)(2,1)S(1)} %pad_maximum_fusion), channel_id=1, source_target_pairs={{0,12},{1,13},{2,14},{3,15},{4,0},{5,1},{6,2},{7,3},{8,4},{9,5},{1... | collective-permute-start | bytes 7077896 | tf_op jit(solution)/shard_map/ppermute | solution.py:52
  31.1 3.1 %collective-permute-start.11 = (bf16[2,384,384]{2,1,0:T(8,128)(2,1)S(1)}, bf16[2,384,384]{2,1,0:T(8,128)(2,1)S(1)}, u32[]{:S(2)}, u32[]{:S(2)}) collective-permute-start(bf16[2,384,384]{2,1,0:T(8,128)(2,1)S(1)} %collective-permute-done.6.refs_9_), channel_id=1, source_target_pairs={{0,224},{1,225},{2,226},{3,227},{4,228},{5,229},{6,230},{7,231},{8... | collective-permute-start | bytes 1769480 | tf_op jit(solution)/shard_map/ppermute | solution.py:52
  34.2 12.3 %collective-permute-done.9.refs_5_ = bf16[2,384,384]{2,1,0:T(8,128)(2,1)S(1)} collective-permute-done((bf16[2,384,384]{2,1,0:T(8,128)(2,1)S(1)}, bf16[2,384,384]{2,1,0:T(8,128)(2,1)S(1)}, u32[]{:S(2)}, u32[]{:S(2)}) %collective-permute-start.9) | collective-permute-done | bytes 589856 | tf_op jit(solution)/shard_map/ppermute | solution.py:52
  46.6 2.7 %collective-permute-start.12 = (bf16[2,384,384]{2,1,0:T(8,128)(2,1)S(1)}, bf16[2,384,384]{2,1,0:T(8,128)(2,1)S(1)}, u32[]{:S(2)}, u32[]{:S(2)}) collective-permute-start(bf16[2,384,384]{2,1,0:T(8,128)(2,1)S(1)} %collective-permute-done.11.refs_8_), channel_id=1, source_target_pairs={{0,224},{1,225},{2,226},{3,227},{4,228},{5,229},{6,230},{7,231},{8... | collective-permute-start | bytes 1769480 | tf_op jit(solution)/shard_map/ppermute | solution.py:52
  49.2 8.3 %collective-permute-done.7 = bf16[4,2,384,384]{3,2,0,1:T(8,128)(2,1)S(1)} collective-permute-done((bf16[4,2,384,384]{3,2,0,1:T(8,128)(2,1)S(1)}, bf16[4,2,384,384]{3,2,0,1:T(8,128)(2,1)S(1)}, u32[]{:S(2)}, u32[]{:S(2)}) %collective-permute-start.7) | collective-permute-done | bytes 2359328 | tf_op jit(solution)/shard_map/ppermute | solution.py:52
  58.0 2.6 %collective-permute-done.10.refs_6_ = bf16[2,384,384]{2,1,0:T(8,128)(2,1)S(1)} collective-permute-done((bf16[2,384,384]{2,1,0:T(8,128)(2,1)S(1)}, bf16[2,384,384]{2,1,0:T(8,128)(2,1)S(1)}, u32[]{:S(2)}, u32[]{:S(2)}) %collective-permute-start.10) | collective-permute-done | bytes 589856 | tf_op jit(solution)/shard_map/ppermute | solution.py:52
  60.6 2.7 %collective-permute-start.14 = (bf16[4,384,384]{2,1,0:T(8,128)(2,1)S(1)}, bf16[4,384,384]{2,1,0:T(8,128)(2,1)S(1)}, u32[]{:S(2)}, u32[]{:S(2)}) collective-permute-start(bf16[4,384,384]{2,1,0:T(8,128)(2,1)S(1)} %slice_bitcast_fusion), channel_id=1, source_target_pairs={{0,12},{1,13},{2,14},{3,15},{4,0},{5,1},{6,2},{7,3},{8,4},{9,5},{1... | collective-permute-start | bytes 3538952 | tf_op jit(solution)/shard_map/ppermute | solution.py:52
  63.3 3.4 %collective-permute-start.17 = (bf16[3,384,384]{2,1,0:T(8,128)(2,1)S(1)}, bf16[3,384,384]{2,1,0:T(8,128)(2,1)S(1)}, u32[]{:S(2)}, u32[]{:S(2)}) collective-permute-start(bf16[3,384,384]{2,1,0:T(8,128)(2,1)S(1)} %copy-done.1), channel_id=1, source_target_pairs={{0,16},{1,17},{2,18},{3,19},{4,20},{5,21},{6,22},{7,23},{8,24},{9,... | collective-permute-start | bytes 2654216 | tf_op jit(solution)/shard_map/ppermute | solution.py:52
  67.3 1.5 %collective-permute-done.other_pattern_ref = s32[3,3]{1,0:T(4,128)S(1)} collective-permute-done((s32[3,3]{1,0:T(4,128)S(1)}, s32[3,3]{1,0:T(4,128)S(1)}, u32[]{:S(2)}, u32[]{:S(2)}) %collective-permute-start) | collective-permute-done | bytes 68 | tf_op jit(solution)/shard_map/ppermute | solution.py:52
  69.9 1.6 %collective-permute-start.16 = (bf16[384,384]{1,0:T(8,128)(2,1)S(1)}, bf16[384,384]{1,0:T(8,128)(2,1)S(1)}, u32[]{:S(2)}, u32[]{:S(2)}) collective-permute-start(bf16[384,384]{1,0:T(8,128)(2,1)S(1)} %slice_bitcast_fusion.2), channel_id=1, source_target_pairs={{0,224},{1,225},{2,226},{3,227},{4,228},{5,229},{6,230},{7,231},{8... | collective-permute-start | bytes 884744 | tf_op jit(solution)/shard_map/ppermute | solution.py:52
  72.6 4.6 %shard_map.131 = (f32[2,384,384]{2,1,0:T(8,128)S(1)}, bf16[4,384,384]{2,1,0:T(8,128)(2,1)S(1)}, bf16[2,2,384,384]{3,2,1,0:T(8,128)(2,1)S(1)}) custom-call(bf16[4,2,384,384]{3,2,1,0:T(8,128)(2,1)S(1)} %copy.15.refs_0_, bf16[4,2,384,384]{3,2,1,0:T(8,128)(2,1)S(1)} %copy.16.refs_1_, bf16[4,2,384,384]{3,2,1,0:T(8,128)(2,1)S(1)} %copy.17.refs_2_, ...), custom_call_target="tpu_custom_call" | custom-call | flops 2717908992 | bytes 14155776 | tf_op jit(solution)/shard_map/pallas_call | solution.py:375
  78.3 4.0 %shard_map.133 = (bf16[2,384,384]{2,1,0:T(8,128)(2,1)}, bf16[384,384]{1,0:T(8,128)(2,1)S(1)}, f32[16,8,128]{2,1,0:T(8,128)S(1)}) custom-call(s32[2]{0:T(128)S(1)} %copy-done.9, s32[3,3]{1,0:T(4,128)S(1)} %copy-done.7, s32[3,3]{1,0:T(4,128)S(1)} %collective-permute-done.other_pattern_ref, bf16[2,384,384]{2,1,0:T(8,128)(2,1)S(1)} %shard_map.130.refs_3_.block_ref, ...), custom_call_target="tpu_custom_call" | custom-call | flops 1358954496 | bytes 7077888 | tf_op jit(solution)/shard_map/pallas_call | solution.py:388
  82.4 3.1 %collective-permute-start.19 = (bf16[384,384]{1,0:T(8,128)(2,1)S(1)}, bf16[384,384]{1,0:T(8,128)(2,1)S(1)}, u32[]{:S(2)}, u32[]{:S(2)}) collective-permute-start(bf16[384,384]{1,0:T(8,128)(2,1)S(1)} %get-tuple-element.23), channel_id=1, source_target_pairs={{0,16},{1,17},{2,18},{3,19},{4,20},{5,21},{6,22},{7,23},{8,24},{9,... | collective-permute-start | bytes 884744 | tf_op jit(solution)/shard_map/ppermute | solution.py:52
  85.5 10.5 %all_to_all.10.parts_ref = f32[16,8,128]{2,1,0:T(8,128)S(1)} all-to-all(f32[16,8,128]{2,1,0:T(8,128)S(1)} %get-tuple-element.25), channel_id=1, replica_groups=mesh['row'=16,'col'=16] {'col'}, dimensions={0} | all-to-all | bytes 131072 | tf_op jit(solution)/shard_map/all_to_all | solution.py:422
  96.1 14.8 %all_to_all.11.all_ref = f32[16,8,128]{2,1,0:T(8,128)S(1)} all-to-all(f32[16,8,128]{2,1,0:T(8,128)S(1)} %shard_map.134), channel_id=1, replica_groups=mesh['row'=16,'col'=16] {'row'}, dimensions={0} | all-to-all | bytes 131072 | tf_op jit(solution)/shard_map/all_to_all | solution.py:431
  110.9 1.3 %shard_map.135 = (bf16[2,384,384]{2,1,0:T(8,128)(2,1)}, f32[3,96]{1,0:T(4,128)}, f32[3,96]{1,0:T(4,128)}, f32[3,96]{1,0:T(4,128)}) custom-call(bf16[384,384]{1,0:T(8,128)(2,1)S(1)} %collective-permute-done.19.got_ref, bf16[2,384,384]{2,1,0:T(8,128)(2,1)} %get-tuple-element.24.half_ref, ...), custom_call_target="tpu_custom_call", output_to_operand_aliasing={{0}: (1, {})} | custom-call | tf_op jit(solution)/shard_map/pallas_call | solution.py:432
  (53 shorter events, 6.2 us)
Async XLA Ops:
  1.8 4.5 %collective-permute-start.1 = (bf16[384,384]{1,0:T(8,128)(2,1)S(1)}, bf16[384,384]{1,0:T(8,128)(2,1)S(1)}, u32[]{:S(2)}, u32[]{:S(2)}) collective-permute-start(bf16[384,384]{1,0:T(8,128)(2,1)S(1)} %shard_map.129), channel_id=1, source_target_pairs={{0,16},{1,17},{2,18},{3,19},{4,20},{5,21},{6,22},{7,23},{8,24},{9,... | collective-permute-start | bytes 884744 | tf_op jit(solution)/shard_map/ppermute | solution.py:52
  6.5 16.6 %collective-permute-start.2 = (bf16[2,384,384]{2,1,0:T(8,128)(2,1)S(1)}, bf16[2,384,384]{2,1,0:T(8,128)(2,1)S(1)}, u32[]{:S(2)}, u32[]{:S(2)}) collective-permute-start(bf16[2,384,384]{2,1,0:T(8,128)(2,1)S(1)} %shard_map.130.refs_3_.block_ref), channel_id=1, source_target_pairs={{0,1},{1,2},{2,3},{3,0},{4,5},{5,6},{6,7},{7,4},{8,9},{9,10},{10,1... | collective-permute-start | bytes 1769480 | tf_op jit(solution)/shard_map/ppermute | solution.py:52
  6.5 16.5 %collective-permute-start.3 = (bf16[2,384,384]{2,1,0:T(8,128)(2,1)S(1)}, bf16[2,384,384]{2,1,0:T(8,128)(2,1)S(1)}, u32[]{:S(2)}, u32[]{:S(2)}) collective-permute-start(bf16[2,384,384]{2,1,0:T(8,128)(2,1)S(1)} %shard_map.130.refs_3_.block_ref), channel_id=1, source_target_pairs={{0,3},{1,0},{2,1},{3,2},{4,7},{5,4},{6,5},{7,6},{8,11},{9,8},{10,9... | collective-permute-start | bytes 1769480 | tf_op jit(solution)/shard_map/ppermute | solution.py:52
  9.2 13.9 %collective-permute-start.4 = (bf16[2,384,384]{2,1,0:T(8,128)(2,1)S(1)}, bf16[2,384,384]{2,1,0:T(8,128)(2,1)S(1)}, u32[]{:S(2)}, u32[]{:S(2)}) collective-permute-start(bf16[2,384,384]{2,1,0:T(8,128)(2,1)S(1)} %shard_map.130.refs_3_.block_ref), channel_id=1, source_target_pairs={{0,2},{1,3},{2,0},{3,1},{4,6},{5,7},{6,4},{7,5},{8,10},{9,11},{10,... | collective-permute-start | bytes 1769480 | tf_op jit(solution)/shard_map/ppermute | solution.py:52
  9.2 17.6 %collective-permute-start.5 = (bf16[2,384,384]{2,1,0:T(8,128)(2,1)S(1)}, bf16[2,384,384]{2,1,0:T(8,128)(2,1)S(1)}, u32[]{:S(2)}, u32[]{:S(2)}) collective-permute-start(bf16[2,384,384]{2,1,0:T(8,128)(2,1)S(1)} %shard_map.130.refs_3_.block_ref), channel_id=1, source_target_pairs={{0,32},{1,33},{2,34},{3,35},{4,36},{5,37},{6,38},{7,39},{8,40},{9,... | collective-permute-start | bytes 1769480 | tf_op jit(solution)/shard_map/ppermute | solution.py:52
  10.6 16.2 %collective-permute-start.6 = (bf16[2,384,384]{2,1,0:T(8,128)(2,1)S(1)}, bf16[2,384,384]{2,1,0:T(8,128)(2,1)S(1)}, u32[]{:S(2)}, u32[]{:S(2)}) collective-permute-start(bf16[2,384,384]{2,1,0:T(8,128)(2,1)S(1)} %shard_map.130.refs_3_.block_ref), channel_id=1, source_target_pairs={{0,224},{1,225},{2,226},{3,227},{4,228},{5,229},{6,230},{7,231},{8... | collective-permute-start | bytes 1769480 | tf_op jit(solution)/shard_map/ppermute | solution.py:52
  27.2 39.5 %copy-start.7 = (s32[3,3]{1,0:T(4,128)S(1)}, s32[3,3]{1,0:T(4,128)}, u32[]{:S(2)}) copy-start(s32[3,3]{1,0:T(4,128)} %pattern_ref.1) | copy-start | bytes 112
  27.2 39.6 %copy-start.5 = (s32[1,384]{1,0:T(1,128)S(1)}, s32[1,384]{1,0:T(1,128)}, u32[]{:S(2)}) copy-start(s32[1,384]{1,0:T(1,128)} %atom_ref.3) | copy-start | bytes 4612
  27.2 44.3 %copy-start.2 = (bf16[3,384,384]{2,1,0:T(8,128)(2,1)S(1)}, bf16[3,384,384]{2,1,0:T(8,128)(2,1)}, u32[]{:S(2)}) copy-start(bf16[3,384,384]{2,1,0:T(8,128)(2,1)} %ovl_ref.1) | copy-start | bytes 2654212
  27.2 44.3 %copy-start.3 = (bf16[384,384]{1,0:T(8,128)(2,1)S(1)}, bf16[384,384]{1,0:T(8,128)(2,1)}, u32[]{:S(2)}) copy-start(bf16[384,384]{1,0:T(8,128)(2,1)} %weighted_ref.1) | copy-start | bytes 884740
  27.3 30.3 %collective-permute-start.7 = (bf16[4,2,384,384]{3,2,0,1:T(8,128)(2,1)S(1)}, bf16[4,2,384,384]{3,2,0,1:T(8,128)(2,1)S(1)}, u32[]{:S(2)}, u32[]{:S(2)}) collective-permute-start(bf16[4,2,384,384]{3,2,0,1:T(8,128)(2,1)S(1)} %pad_maximum_fusion), channel_id=1, source_target_pairs={{0,4},{1,5},{2,6},{3,7},{4,8},{5,9},{6,10},{7,11},{8,12},{9,13},{1... | collective-permute-start | bytes 7077896 | tf_op jit(solution)/shard_map/ppermute | solution.py:52
  29.7 28.3 %collective-permute-start.8 = (bf16[4,2,384,384]{3,2,0,1:T(8,128)(2,1)S(1)}, bf16[4,2,384,384]{3,2,0,1:T(8,128)(2,1)S(1)}, u32[]{:S(2)}, u32[]{:S(2)}) collective-permute-start(bf16[4,2,384,384]{3,2,0,1:T(8,128)(2,1)S(1)} %pad_maximum_fusion), channel_id=1, source_target_pairs={{0,12},{1,13},{2,14},{3,15},{4,0},{5,1},{6,2},{7,3},{8,4},{9,5},{1... | collective-permute-start | bytes 7077896 | tf_op jit(solution)/shard_map/ppermute | solution.py:52
  31.1 15.4 %collective-permute-start.9 = (bf16[2,384,384]{2,1,0:T(8,128)(2,1)S(1)}, bf16[2,384,384]{2,1,0:T(8,128)(2,1)S(1)}, u32[]{:S(2)}, u32[]{:S(2)}) collective-permute-start(bf16[2,384,384]{2,1,0:T(8,128)(2,1)S(1)} %collective-permute-done.5.refs_4_), channel_id=1, source_target_pairs={{0,32},{1,33},{2,34},{3,35},{4,36},{5,37},{6,38},{7,39},{8,40},{9,... | collective-permute-start | bytes 1769480 | tf_op jit(solution)/shard_map/ppermute | solution.py:52
  31.1 15.4 %collective-permute-start.11 = (bf16[2,384,384]{2,1,0:T(8,128)(2,1)S(1)}, bf16[2,384,384]{2,1,0:T(8,128)(2,1)S(1)}, u32[]{:S(2)}, u32[]{:S(2)}) collective-permute-start(bf16[2,384,384]{2,1,0:T(8,128)(2,1)S(1)} %collective-permute-done.6.refs_9_), channel_id=1, source_target_pairs={{0,224},{1,225},{2,226},{3,227},{4,228},{5,229},{6,230},{7,231},{8... | collective-permute-start | bytes 1769480 | tf_op jit(solution)/shard_map/ppermute | solution.py:52
  46.6 14.1 %collective-permute-start.10 = (bf16[2,384,384]{2,1,0:T(8,128)(2,1)S(1)}, bf16[2,384,384]{2,1,0:T(8,128)(2,1)S(1)}, u32[]{:S(2)}, u32[]{:S(2)}) collective-permute-start(bf16[2,384,384]{2,1,0:T(8,128)(2,1)S(1)} %collective-permute-done.9.refs_5_), channel_id=1, source_target_pairs={{0,32},{1,33},{2,34},{3,35},{4,36},{5,37},{6,38},{7,39},{8,40},{9,... | collective-permute-start | bytes 1769480 | tf_op jit(solution)/shard_map/ppermute | solution.py:52
  46.6 14.1 %collective-permute-start.12 = (bf16[2,384,384]{2,1,0:T(8,128)(2,1)S(1)}, bf16[2,384,384]{2,1,0:T(8,128)(2,1)S(1)}, u32[]{:S(2)}, u32[]{:S(2)}) collective-permute-start(bf16[2,384,384]{2,1,0:T(8,128)(2,1)S(1)} %collective-permute-done.11.refs_8_), channel_id=1, source_target_pairs={{0,224},{1,225},{2,226},{3,227},{4,228},{5,229},{6,230},{7,231},{8... | collective-permute-start | bytes 1769480 | tf_op jit(solution)/shard_map/ppermute | solution.py:52
  60.6 17.6 %collective-permute-start.13 = (bf16[4,384,384]{2,1,0:T(8,128)(2,1)S(1)}, bf16[4,384,384]{2,1,0:T(8,128)(2,1)S(1)}, u32[]{:S(2)}, u32[]{:S(2)}) collective-permute-start(bf16[4,384,384]{2,1,0:T(8,128)(2,1)S(1)} %slice_bitcast_fusion.1), channel_id=1, source_target_pairs={{0,4},{1,5},{2,6},{3,7},{4,8},{5,9},{6,10},{7,11},{8,12},{9,13},{1... | collective-permute-start | bytes 3538952 | tf_op jit(solution)/shard_map/ppermute | solution.py:52
  60.6 17.6 %collective-permute-start.14 = (bf16[4,384,384]{2,1,0:T(8,128)(2,1)S(1)}, bf16[4,384,384]{2,1,0:T(8,128)(2,1)S(1)}, u32[]{:S(2)}, u32[]{:S(2)}) collective-permute-start(bf16[4,384,384]{2,1,0:T(8,128)(2,1)S(1)} %slice_bitcast_fusion), channel_id=1, source_target_pairs={{0,12},{1,13},{2,14},{3,15},{4,0},{5,1},{6,2},{7,3},{8,4},{9,5},{1... | collective-permute-start | bytes 3538952 | tf_op jit(solution)/shard_map/ppermute | solution.py:52
  63.3 13.9 %collective-permute-start.17 = (bf16[3,384,384]{2,1,0:T(8,128)(2,1)S(1)}, bf16[3,384,384]{2,1,0:T(8,128)(2,1)S(1)}, u32[]{:S(2)}, u32[]{:S(2)}) collective-permute-start(bf16[3,384,384]{2,1,0:T(8,128)(2,1)S(1)} %copy-done.1), channel_id=1, source_target_pairs={{0,16},{1,17},{2,18},{3,19},{4,20},{5,21},{6,22},{7,23},{8,24},{9,... | collective-permute-start | bytes 2654216 | tf_op jit(solution)/shard_map/ppermute | solution.py:52
  66.8 2.1 %collective-permute-start = (s32[3,3]{1,0:T(4,128)S(1)}, s32[3,3]{1,0:T(4,128)S(1)}, u32[]{:S(2)}, u32[]{:S(2)}) collective-permute-start(s32[3,3]{1,0:T(4,128)S(1)} %copy-done.7), channel_id=1, source_target_pairs={{0,16},{1,17},{2,18},{3,19},{4,20},{5,21},{6,22},{7,23},{8,24},{9,... | collective-permute-start | bytes 116 | tf_op jit(solution)/shard_map/ppermute | solution.py:52
  66.9 3.1 %collective-permute-start.18 = (s32[1,384]{1,0:T(1,128)S(1)}, s32[1,384]{1,0:T(1,128)S(1)}, u32[]{:S(2)}, u32[]{:S(2)}) collective-permute-start(s32[1,384]{1,0:T(1,128)S(1)} %copy-done.5), channel_id=1, source_target_pairs={{0,16},{1,17},{2,18},{3,19},{4,20},{5,21},{6,22},{7,23},{8,24},{9,... | collective-permute-start | bytes 4616 | tf_op jit(solution)/shard_map/ppermute | solution.py:52
  68.8 9.4 %collective-permute-start.15 = (bf16[384,384]{1,0:T(8,128)(2,1)S(1)}, bf16[384,384]{1,0:T(8,128)(2,1)S(1)}, u32[]{:S(2)}, u32[]{:S(2)}) collective-permute-start(bf16[384,384]{1,0:T(8,128)(2,1)S(1)} %slice_bitcast_fusion.3), channel_id=1, source_target_pairs={{0,32},{1,33},{2,34},{3,35},{4,36},{5,37},{6,38},{7,39},{8,40},{9,... | collective-permute-start | bytes 884744 | tf_op jit(solution)/shard_map/ppermute | solution.py:52
  69.9 8.3 %collective-permute-start.16 = (bf16[384,384]{1,0:T(8,128)(2,1)S(1)}, bf16[384,384]{1,0:T(8,128)(2,1)S(1)}, u32[]{:S(2)}, u32[]{:S(2)}) collective-permute-start(bf16[384,384]{1,0:T(8,128)(2,1)S(1)} %slice_bitcast_fusion.2), channel_id=1, source_target_pairs={{0,224},{1,225},{2,226},{3,227},{4,228},{5,229},{6,230},{7,231},{8... | collective-permute-start | bytes 884744 | tf_op jit(solution)/shard_map/ppermute | solution.py:52
  82.4 28.5 %collective-permute-start.19 = (bf16[384,384]{1,0:T(8,128)(2,1)S(1)}, bf16[384,384]{1,0:T(8,128)(2,1)S(1)}, u32[]{:S(2)}, u32[]{:S(2)}) collective-permute-start(bf16[384,384]{1,0:T(8,128)(2,1)S(1)} %get-tuple-element.23), channel_id=1, source_target_pairs={{0,16},{1,17},{2,18},{3,19},{4,20},{5,21},{6,22},{7,23},{8,24},{9,... | collective-permute-start | bytes 884744 | tf_op jit(solution)/shard_map/ppermute | solution.py:52
  (6 other events, 110.8 us)

commit v7 on v6

--- a/solution.py
+++ b/solution.py
@@ -56,13 +56,15 @@
     return lax.optimization_barrier((value,) + others)[0]
 
 
+EARLY = 3 << 32
+
+
 def gather(block):
     z_back = send(block, z_by(1))
     z_fore = send(block, z_by(-1))
     back = send(block, first_by(1))
     fore = send(block, first_by(-1))
     far = send(block, first_by(2))
-    back, fore, far = after((back, fore, far), z_back, z_fore)
     line = jnp.stack([block, back, fore, far])
     line_back = send(line, second_by(1))
     line_fore = send(line, second_by(-1))
@@ -70,24 +72,21 @@
     z_fore_two = send(z_fore, z_by(-1))
     z_back_three = send(z_back_two, z_by(1))
     z_fore_three = send(z_fore_two, z_by(-1))
-    low, high = after((line_back[:, 0], line_fore[:, 1]), z_back_three, z_fore_three)
+    levels = (block, z_back, z_back_two, z_back_three, z_fore_three, z_fore_two, z_fore)
+    columns = pl.pallas_call(
+        column_kernel,
+        out_shape=jax.ShapeDtypeStruct((SLABS, ROWS, ROWS), jnp.bfloat16),
+        in_specs=[VMEM] * 7,
+        out_specs=VMEM,
+        compiler_params=LITTLE,
+        cost_estimate=pl.CostEstimate(flops=EARLY, bytes_accessed=1 << 22, transcendentals=0),
+    )(*levels)
+    low, high = after((line_back[:, 0], line_fore[:, 1]), columns)
     line_low = send(low, second_by(1))
     line_high = send(high, second_by(-1))
     z_low = send(z_back_three[0], z_by(1))
     z_high = send(z_fore_three[1], z_by(-1))
-    wide = (line, line_back, line_fore, line_low, line_high)
-    tall = (
-        block,
-        z_back,
-        z_back_two,
-        z_back_three,
-        z_fore_three,
-        z_fore_two,
-        z_fore,
-        z_low,
-        z_high,
-    )
-    return wide, tall
+    return (line, line_back, line_fore), (line_low, line_high), columns, (z_low, z_high)
 
 
 LEVELS = (0, -1, -2, -3, 3, 2, 1)
@@ -159,14 +158,20 @@
 NEAR = 12
 
 
-def near_kernel(*refs):
-    wide, tall, (total_ref, b_far_ref, a_far_ref, b_buf) = refs[:3], refs[3:10], refs[10:]
+def column_kernel(*refs):
+    tall, out_ref = refs[:-1], refs[-1]
     z = position()[0]
     for half in range(HALVES):
         for level, offset in enumerate(LEVELS):
-            b_buf[slot_of(z + offset, half)] = tall[level][half]
+            out_ref[slot_of(z + offset, half)] = tall[level][half]
+        out_ref[slot_of(z + 4, half)] = jnp.zeros((ROWS, ROWS), jnp.bfloat16)
+
+
+def near_kernel(*refs):
+    wide, b_buf, (total_ref, b_far_ref, a_far_ref) = refs[:3], refs[3], refs[4:]
+    z = position()[0]
+    for half in range(HALVES):
         slot = slot_of(z + 4, half)
-        b_buf[slot] = jnp.zeros((ROWS, ROWS), jnp.bfloat16)
 
         @pl.when(slot >= NEAR)
         def _():
@@ -358,7 +363,7 @@
         scratch_shapes=[pltpu.SemaphoreType.DMA((2,))],
         compiler_params=LITTLE,
     )(density, send(give, core_swap()))
-    wide, tall = gather(block)
+    first, last, columns, opposite = gather(block)
 
     other_ham = send(ham_deriv, core_swap())
     other_atom = send(orbital_atom, core_swap())
@@ -379,12 +384,11 @@
             jax.ShapeDtypeStruct((SLABS - NEAR, ROWS, ROWS), jnp.bfloat16),
             jax.ShapeDtypeStruct((2, HALVES, ROWS, ROWS), jnp.bfloat16),
         ),
-        in_specs=[VMEM] * 10,
+        in_specs=[VMEM] * 4,
         out_specs=(VMEM,) * 3,
-        scratch_shapes=[pltpu.VMEM((SLABS, ROWS, ROWS), jnp.bfloat16)],
         compiler_params=PARAMS,
         cost_estimate=cost(NEAR),
-    )(*wide[:3], *tall[:7])
+    )(*first, columns)
     half, give, sums = pl.pallas_call(
         purify_kernel,
         out_shape=(
@@ -406,8 +410,8 @@
         tile_pattern,
         other_pattern,
         block,
-        *wide[3:],
-        *tall[7:],
+        *last,
+        *opposite,
         total,
         b_far,
         a_far,

time: 113 us -> 111 us (0.982)
  blocking collectives: 25.3 us -> 27.4 us
  waiting for transfers between devices: 39.5 us -> 37.5 us
  starting transfers between devices: 33.5 us -> 32 us
    all_to_all x1, blocking collectives: 10.5 us -> 12.6 us  [local(): parts = lax.all_to_all(sums, 'col', 0, 0)]
    ppermute x20, waiting for transfers between devices: 39.5 us -> 37.5 us  [send(): return lax.ppermute(value, AXES, table)]
    ppermute x20, starting transfers between devices: 33.5 us -> 32 us  [send(): return lax.ppermute(value, AXES, table)]
  transfers between devices with their start and end apart: 20 -> 20, of which waited for: 9 -> 8; matrix products, arithmetic and copies ran while one was open for 1% -> 1% of each run, Pallas kernels for 4% -> 5%
where the time goes in v7:
time: 111 us
  waiting for transfers between devices  37.5 us (34%)
  starting transfers between devices  32 us (29%)
  blocking collectives  27.4 us (25%)
  Pallas kernels  10.6 us (10%)
  local copies, waits for them, and re-layouts  2.13 us (2%)
    ppermute x20, waiting for transfers between devices, send(): return lax.ppermute(value, AXES, table)  37.5 us
    ppermute x20, starting transfers between devices, send(): return lax.ppermute(value, AXES, table)  32 us
    all_to_all x1, blocking collectives, local(): parts = lax.all_to_all(parts, 'row', 0, 0)  14.8 us
    all_to_all x1, blocking collectives, local(): parts = lax.all_to_all(sums, 'col', 0, 0)  12.6 us
    pallas_call x1, Pallas kernels, local(): pl.pallas_call(near_kernel, out_shape=(small((HALVES, ROWS, ROWS)), jax.S...  4.15 us
    pallas_call x1, Pallas kernels, local(): pl.pallas_call(purify_kernel, out_shape=(jax.ShapeDtypeStruct((2, ROWS, R...  4.09 us
  transfers between devices with their start and end apart: 20, of which 8 were waited for; matrix products, arithmetic and copies ran while one was open for 1% of the time, Pallas kernels for 5%

profile of v7, /device:TPU:1, one launch (start us, length us, event | category | flops | bytes accessed | tf_op | source)
XLA Modules:
  0.0 111.2 jit_solution(15101258775283798487)
XLA Ops:
  1.8 3.3 %collective-permute-start.1 = (bf16[384,384]{1,0:T(8,128)(2,1)S(1)}, bf16[384,384]{1,0:T(8,128)(2,1)S(1)}, u32[]{:S(2)}, u32[]{:S(2)}) collective-permute-start(bf16[384,384]{1,0:T(8,128)(2,1)S(1)} %shard_map.129), channel_id=1, source_target_pairs={{0,16},{1,17},{2,18},{3,19},{4,20},{5,21},{6,22},{7,23},{8,24},{9,... | collective-permute-start | bytes 884744 | tf_op jit(solution)/shard_map/ppermute | solution.py:52
  5.1 1.2 %collective-permute-done.1.got_ref = bf16[384,384]{1,0:T(8,128)(2,1)S(1)} collective-permute-done((bf16[384,384]{1,0:T(8,128)(2,1)S(1)}, bf16[384,384]{1,0:T(8,128)(2,1)S(1)}, u32[]{:S(2)}, u32[]{:S(2)}) %collective-permute-start.1) | collective-permute-done | bytes 294944 | tf_op jit(solution)/shard_map/ppermute | solution.py:52
  6.5 3.9 %collective-permute-start.10 = (bf16[2,384,384]{2,1,0:T(8,128)(2,1)S(1)}, bf16[2,384,384]{2,1,0:T(8,128)(2,1)S(1)}, u32[]{:S(2)}, u32[]{:S(2)}) collective-permute-start(bf16[2,384,384]{2,1,0:T(8,128)(2,1)S(1)} %shard_map.130.refs_0_.block_ref), channel_id=1, source_target_pairs={{0,224},{1,225},{2,226},{3,227},{4,228},{5,229},{6,230},{7,231},{8... | collective-permute-start | bytes 1769480 | tf_op jit(solution)/shard_map/ppermute | solution.py:52
  10.5 2.7 %collective-permute-start.4 = (bf16[2,384,384]{2,1,0:T(8,128)(2,1)S(1)}, bf16[2,384,384]{2,1,0:T(8,128)(2,1)S(1)}, u32[]{:S(2)}, u32[]{:S(2)}) collective-permute-start(bf16[2,384,384]{2,1,0:T(8,128)(2,1)S(1)} %shard_map.130.refs_0_.block_ref), channel_id=1, source_target_pairs={{0,2},{1,3},{2,0},{3,1},{4,6},{5,7},{6,4},{7,5},{8,10},{9,11},{10,... | collective-permute-start | bytes 1769480 | tf_op jit(solution)/shard_map/ppermute | solution.py:52
  14.7 9.1 %collective-permute-done.7.refs_1_ = bf16[2,384,384]{2,1,0:T(8,128)(2,1)S(1)} collective-permute-done((bf16[2,384,384]{2,1,0:T(8,128)(2,1)S(1)}, bf16[2,384,384]{2,1,0:T(8,128)(2,1)S(1)}, u32[]{:S(2)}, u32[]{:S(2)}) %collective-permute-start.7) | collective-permute-done | bytes 589856 | tf_op jit(solution)/shard_map/ppermute | solution.py:52
  23.8 2.7 %collective-permute-start.11 = (bf16[2,384,384]{2,1,0:T(8,128)(2,1)S(1)}, bf16[2,384,384]{2,1,0:T(8,128)(2,1)S(1)}, u32[]{:S(2)}, u32[]{:S(2)}) collective-permute-start(bf16[2,384,384]{2,1,0:T(8,128)(2,1)S(1)} %collective-permute-done.10.refs_6_), channel_id=1, source_target_pairs={{0,224},{1,225},{2,226},{3,227},{4,228},{5,229},{6,230},{7,231},{8... | collective-permute-start | bytes 1769480 | tf_op jit(solution)/shard_map/ppermute | solution.py:52
  27.8 1.4 %collective-permute-start.5 = (bf16[4,2,384,384]{3,2,0,1:T(8,128)(2,1)S(1)}, bf16[4,2,384,384]{3,2,0,1:T(8,128)(2,1)S(1)}, u32[]{:S(2)}, u32[]{:S(2)}) collective-permute-start(bf16[4,2,384,384]{3,2,0,1:T(8,128)(2,1)S(1)} %pad_maximum_fusion), channel_id=1, source_target_pairs={{0,4},{1,5},{2,6},{3,7},{4,8},{5,9},{6,10},{7,11},{8,12},{9,13},{1... | collective-permute-start | bytes 7077896 | tf_op jit(solution)/shard_map/ppermute | solution.py:52
  29.2 1.5 %collective-permute-start.6 = (bf16[4,2,384,384]{3,2,0,1:T(8,128)(2,1)S(1)}, bf16[4,2,384,384]{3,2,0,1:T(8,128)(2,1)S(1)}, u32[]{:S(2)}, u32[]{:S(2)}) collective-permute-start(bf16[4,2,384,384]{3,2,0,1:T(8,128)(2,1)S(1)} %pad_maximum_fusion), channel_id=1, source_target_pairs={{0,12},{1,13},{2,14},{3,15},{4,0},{5,1},{6,2},{7,3},{8,4},{9,5},{1... | collective-permute-start | bytes 7077896 | tf_op jit(solution)/shard_map/ppermute | solution.py:52
  30.7 8.2 %collective-permute-done.8.refs_2_ = bf16[2,384,384]{2,1,0:T(8,128)(2,1)S(1)} collective-permute-done((bf16[2,384,384]{2,1,0:T(8,128)(2,1)S(1)}, bf16[2,384,384]{2,1,0:T(8,128)(2,1)S(1)}, u32[]{:S(2)}, u32[]{:S(2)}) %collective-permute-start.8) | collective-permute-done | bytes 589856 | tf_op jit(solution)/shard_map/ppermute | solution.py:52
  38.9 2.7 %collective-permute-start.12 = (bf16[2,384,384]{2,1,0:T(8,128)(2,1)S(1)}, bf16[2,384,384]{2,1,0:T(8,128)(2,1)S(1)}, u32[]{:S(2)}, u32[]{:S(2)}) collective-permute-start(bf16[2,384,384]{2,1,0:T(8,128)(2,1)S(1)} %collective-permute-done.11.refs_5_), channel_id=1, source_target_pairs={{0,224},{1,225},{2,226},{3,227},{4,228},{5,229},{6,230},{7,231},{8... | collective-permute-start | bytes 1769480 | tf_op jit(solution)/shard_map/ppermute | solution.py:52
  41.6 11.6 %collective-permute-done.9.refs_3_ = bf16[2,384,384]{2,1,0:T(8,128)(2,1)S(1)} collective-permute-done((bf16[2,384,384]{2,1,0:T(8,128)(2,1)S(1)}, bf16[2,384,384]{2,1,0:T(8,128)(2,1)S(1)}, u32[]{:S(2)}, u32[]{:S(2)}) %collective-permute-start.9) | collective-permute-done | bytes 589856 | tf_op jit(solution)/shard_map/ppermute | solution.py:52
  53.7 3.5 %collective-permute-done.5 = bf16[4,2,384,384]{3,2,0,1:T(8,128)(2,1)S(1)} collective-permute-done((bf16[4,2,384,384]{3,2,0,1:T(8,128)(2,1)S(1)}, bf16[4,2,384,384]{3,2,0,1:T(8,128)(2,1)S(1)}, u32[]{:S(2)}, u32[]{:S(2)}) %collective-permute-start.5) | collective-permute-done | bytes 2359328 | tf_op jit(solution)/shard_map/ppermute | solution.py:52
  57.4 1.3 %collective-permute-start.13 = (bf16[4,384,384]{2,1,0:T(8,128)(2,1)S(1)}, bf16[4,384,384]{2,1,0:T(8,128)(2,1)S(1)}, u32[]{:S(2)}, u32[]{:S(2)}) collective-permute-start(bf16[4,384,384]{2,1,0:T(8,128)(2,1)S(1)} %slice_bitcast_fusion.1), channel_id=1, source_target_pairs={{0,4},{1,5},{2,6},{3,7},{4,8},{5,9},{6,10},{7,11},{8,12},{9,13},{1... | collective-permute-start | bytes 3538952 | tf_op jit(solution)/shard_map/ppermute | solution.py:52
  58.7 1.5 %collective-permute-start.14 = (bf16[4,384,384]{2,1,0:T(8,128)(2,1)S(1)}, bf16[4,384,384]{2,1,0:T(8,128)(2,1)S(1)}, u32[]{:S(2)}, u32[]{:S(2)}) collective-permute-start(bf16[4,384,384]{2,1,0:T(8,128)(2,1)S(1)} %slice_bitcast_fusion), channel_id=1, source_target_pairs={{0,12},{1,13},{2,14},{3,15},{4,0},{5,1},{6,2},{7,3},{8,4},{9,5},{1... | collective-permute-start | bytes 3538952 | tf_op jit(solution)/shard_map/ppermute | solution.py:52
  60.2 3.2 %collective-permute-start.17 = (bf16[3,384,384]{2,1,0:T(8,128)(2,1)S(1)}, bf16[3,384,384]{2,1,0:T(8,128)(2,1)S(1)}, u32[]{:S(2)}, u32[]{:S(2)}) collective-permute-start(bf16[3,384,384]{2,1,0:T(8,128)(2,1)S(1)} %copy-done.1), channel_id=1, source_target_pairs={{0,16},{1,17},{2,18},{3,19},{4,20},{5,21},{6,22},{7,23},{8,24},{9,... | collective-permute-start | bytes 2654216 | tf_op jit(solution)/shard_map/ppermute | solution.py:52
  64.0 1.5 %collective-permute-done.other_pattern_ref = s32[3,3]{1,0:T(4,128)S(1)} collective-permute-done((s32[3,3]{1,0:T(4,128)S(1)}, s32[3,3]{1,0:T(4,128)S(1)}, u32[]{:S(2)}, u32[]{:S(2)}) %collective-permute-start) | collective-permute-done | bytes 68 | tf_op jit(solution)/shard_map/ppermute | solution.py:52
  65.5 2.7 %collective-permute-start.16 = (bf16[384,384]{1,0:T(8,128)(2,1)S(1)}, bf16[384,384]{1,0:T(8,128)(2,1)S(1)}, u32[]{:S(2)}, u32[]{:S(2)}) collective-permute-start(bf16[384,384]{1,0:T(8,128)(2,1)S(1)} %slice_bitcast_fusion.2), channel_id=1, source_target_pairs={{0,224},{1,225},{2,226},{3,227},{4,228},{5,229},{6,230},{7,231},{8... | collective-permute-start | bytes 884744 | tf_op jit(solution)/shard_map/ppermute | solution.py:52
  69.3 4.1 %shard_map.132 = (f32[2,384,384]{2,1,0:T(8,128)S(1)}, bf16[4,384,384]{2,1,0:T(8,128)(2,1)S(1)}, bf16[2,2,384,384]{3,2,1,0:T(8,128)(2,1)S(1)}) custom-call(bf16[4,2,384,384]{3,2,1,0:T(8,128)(2,1)S(1)} %copy.15.refs_0_, bf16[4,2,384,384]{3,2,1,0:T(8,128)(2,1)S(1)} %copy.16.refs_1_, bf16[4,2,384,384]{3,2,1,0:T(8,128)(2,1)S(1)} %copy.17.refs_2_, ...), custom_call_target="tpu_custom_call" | custom-call | flops 2717908992 | bytes 14155776 | tf_op jit(solution)/shard_map/pallas_call | solution.py:380
  73.4 1.5 %collective-permute-done.15.z_low = bf16[384,384]{1,0:T(8,128)(2,1)S(1)} collective-permute-done((bf16[384,384]{1,0:T(8,128)(2,1)S(1)}, bf16[384,384]{1,0:T(8,128)(2,1)S(1)}, u32[]{:S(2)}, u32[]{:S(2)}) %collective-permute-start.15) | collective-permute-done | bytes 294944 | tf_op jit(solution)/shard_map/ppermute | solution.py:52
  75.0 4.1 %shard_map.134 = (bf16[2,384,384]{2,1,0:T(8,128)(2,1)}, bf16[384,384]{1,0:T(8,128)(2,1)S(1)}, f32[16,8,128]{2,1,0:T(8,128)S(1)}) custom-call(s32[2]{0:T(128)S(1)} %copy-done.9, s32[3,3]{1,0:T(4,128)S(1)} %copy-done.7, s32[3,3]{1,0:T(4,128)S(1)} %collective-permute-done.other_pattern_ref, bf16[2,384,384]{2,1,0:T(8,128)(2,1)S(1)} %shard_map.130.refs_0_.block_ref, ...), custom_call_target="tpu_custom_call" | custom-call | flops 1358954496 | bytes 7077888 | tf_op jit(solution)/shard_map/pallas_call | solution.py:392
  79.1 3.1 %collective-permute-start.19 = (bf16[384,384]{1,0:T(8,128)(2,1)S(1)}, bf16[384,384]{1,0:T(8,128)(2,1)S(1)}, u32[]{:S(2)}, u32[]{:S(2)}) collective-permute-start(bf16[384,384]{1,0:T(8,128)(2,1)S(1)} %get-tuple-element.17), channel_id=1, source_target_pairs={{0,16},{1,17},{2,18},{3,19},{4,20},{5,21},{6,22},{7,23},{8,24},{9,... | collective-permute-start | bytes 884744 | tf_op jit(solution)/shard_map/ppermute | solution.py:52
  82.1 12.6 %all_to_all.10.parts_ref = f32[16,8,128]{2,1,0:T(8,128)S(1)} all-to-all(f32[16,8,128]{2,1,0:T(8,128)S(1)} %get-tuple-element.19), channel_id=1, replica_groups=mesh['row'=16,'col'=16] {'col'}, dimensions={0} | all-to-all | bytes 131072 | tf_op jit(solution)/shard_map/all_to_all | solution.py:426
  94.8 14.8 %all_to_all.11.all_ref = f32[16,8,128]{2,1,0:T(8,128)S(1)} all-to-all(f32[16,8,128]{2,1,0:T(8,128)S(1)} %shard_map.135), channel_id=1, replica_groups=mesh['row'=16,'col'=16] {'row'}, dimensions={0} | all-to-all | bytes 131072 | tf_op jit(solution)/shard_map/all_to_all | solution.py:435
  109.7 1.3 %shard_map.136 = (bf16[2,384,384]{2,1,0:T(8,128)(2,1)}, f32[3,96]{1,0:T(4,128)}, f32[3,96]{1,0:T(4,128)}, f32[3,96]{1,0:T(4,128)}) custom-call(bf16[384,384]{1,0:T(8,128)(2,1)S(1)} %collective-permute-done.19.got_ref, bf16[2,384,384]{2,1,0:T(8,128)(2,1)} %get-tuple-element.18.half_ref, ...), custom_call_target="tpu_custom_call", output_to_operand_aliasing={{0}: (1, {})} | custom-call | tf_op jit(solution)/shard_map/pallas_call | solution.py:436
  (54 shorter events, 6.7 us)
Async XLA Ops:
  1.8 4.5 %collective-permute-start.1 = (bf16[384,384]{1,0:T(8,128)(2,1)S(1)}, bf16[384,384]{1,0:T(8,128)(2,1)S(1)}, u32[]{:S(2)}, u32[]{:S(2)}) collective-permute-start(bf16[384,384]{1,0:T(8,128)(2,1)S(1)} %shard_map.129), channel_id=1, source_target_pairs={{0,16},{1,17},{2,18},{3,19},{4,20},{5,21},{6,22},{7,23},{8,24},{9,... | collective-permute-start | bytes 884744 | tf_op jit(solution)/shard_map/ppermute | solution.py:52
  6.5 17.3 %collective-permute-start.7 = (bf16[2,384,384]{2,1,0:T(8,128)(2,1)S(1)}, bf16[2,384,384]{2,1,0:T(8,128)(2,1)S(1)}, u32[]{:S(2)}, u32[]{:S(2)}) collective-permute-start(bf16[2,384,384]{2,1,0:T(8,128)(2,1)S(1)} %shard_map.130.refs_0_.block_ref), channel_id=1, source_target_pairs={{0,32},{1,33},{2,34},{3,35},{4,36},{5,37},{6,38},{7,39},{8,40},{9,... | collective-permute-start | bytes 1769480 | tf_op jit(solution)/shard_map/ppermute | solution.py:52
  6.5 17.2 %collective-permute-start.10 = (bf16[2,384,384]{2,1,0:T(8,128)(2,1)S(1)}, bf16[2,384,384]{2,1,0:T(8,128)(2,1)S(1)}, u32[]{:S(2)}, u32[]{:S(2)}) collective-permute-start(bf16[2,384,384]{2,1,0:T(8,128)(2,1)S(1)} %shard_map.130.refs_0_.block_ref), channel_id=1, source_target_pairs={{0,224},{1,225},{2,226},{3,227},{4,228},{5,229},{6,230},{7,231},{8... | collective-permute-start | bytes 1769480 | tf_op jit(solution)/shard_map/ppermute | solution.py:52
  10.5 16.0 %collective-permute-start.4 = (bf16[2,384,384]{2,1,0:T(8,128)(2,1)S(1)}, bf16[2,384,384]{2,1,0:T(8,128)(2,1)S(1)}, u32[]{:S(2)}, u32[]{:S(2)}) collective-permute-start(bf16[2,384,384]{2,1,0:T(8,128)(2,1)S(1)} %shard_map.130.refs_0_.block_ref), channel_id=1, source_target_pairs={{0,2},{1,3},{2,0},{3,1},{4,6},{5,7},{6,4},{7,5},{8,10},{9,11},{10,... | collective-permute-start | bytes 1769480 | tf_op jit(solution)/shard_map/ppermute | solution.py:52
  13.2 14.2 %collective-permute-start.3 = (bf16[2,384,384]{2,1,0:T(8,128)(2,1)S(1)}, bf16[2,384,384]{2,1,0:T(8,128)(2,1)S(1)}, u32[]{:S(2)}, u32[]{:S(2)}) collective-permute-start(bf16[2,384,384]{2,1,0:T(8,128)(2,1)S(1)} %shard_map.130.refs_0_.block_ref), channel_id=1, source_target_pairs={{0,3},{1,0},{2,1},{3,2},{4,7},{5,4},{6,5},{7,6},{8,11},{9,8},{10,9... | collective-permute-start | bytes 1769480 | tf_op jit(solution)/shard_map/ppermute | solution.py:52
  14.1 13.4 %collective-permute-start.2 = (bf16[2,384,384]{2,1,0:T(8,128)(2,1)S(1)}, bf16[2,384,384]{2,1,0:T(8,128)(2,1)S(1)}, u32[]{:S(2)}, u32[]{:S(2)}) collective-permute-start(bf16[2,384,384]{2,1,0:T(8,128)(2,1)S(1)} %shard_map.130.refs_0_.block_ref), channel_id=1, source_target_pairs={{0,1},{1,2},{2,3},{3,0},{4,5},{5,6},{6,7},{7,4},{8,9},{9,10},{10,1... | collective-permute-start | bytes 1769480 | tf_op jit(solution)/shard_map/ppermute | solution.py:52
  23.8 15.2 %collective-permute-start.8 = (bf16[2,384,384]{2,1,0:T(8,128)(2,1)S(1)}, bf16[2,384,384]{2,1,0:T(8,128)(2,1)S(1)}, u32[]{:S(2)}, u32[]{:S(2)}) collective-permute-start(bf16[2,384,384]{2,1,0:T(8,128)(2,1)S(1)} %collective-permute-done.7.refs_1_), channel_id=1, source_target_pairs={{0,32},{1,33},{2,34},{3,35},{4,36},{5,37},{6,38},{7,39},{8,40},{9,... | collective-permute-start | bytes 1769480 | tf_op jit(solution)/shard_map/ppermute | solution.py:52
  23.8 15.2 %collective-permute-start.11 = (bf16[2,384,384]{2,1,0:T(8,128)(2,1)S(1)}, bf16[2,384,384]{2,1,0:T(8,128)(2,1)S(1)}, u32[]{:S(2)}, u32[]{:S(2)}) collective-permute-start(bf16[2,384,384]{2,1,0:T(8,128)(2,1)S(1)} %collective-permute-done.10.refs_6_), channel_id=1, source_target_pairs={{0,224},{1,225},{2,226},{3,227},{4,228},{5,229},{6,230},{7,231},{8... | collective-permute-start | bytes 1769480 | tf_op jit(solution)/shard_map/ppermute | solution.py:52
  27.8 29.3 %collective-permute-start.5 = (bf16[4,2,384,384]{3,2,0,1:T(8,128)(2,1)S(1)}, bf16[4,2,384,384]{3,2,0,1:T(8,128)(2,1)S(1)}, u32[]{:S(2)}, u32[]{:S(2)}) collective-permute-start(bf16[4,2,384,384]{3,2,0,1:T(8,128)(2,1)S(1)} %pad_maximum_fusion), channel_id=1, source_target_pairs={{0,4},{1,5},{2,6},{3,7},{4,8},{5,9},{6,10},{7,11},{8,12},{9,13},{1... | collective-permute-start | bytes 7077896 | tf_op jit(solution)/shard_map/ppermute | solution.py:52
  29.2 28.1 %collective-permute-start.6 = (bf16[4,2,384,384]{3,2,0,1:T(8,128)(2,1)S(1)}, bf16[4,2,384,384]{3,2,0,1:T(8,128)(2,1)S(1)}, u32[]{:S(2)}, u32[]{:S(2)}) collective-permute-start(bf16[4,2,384,384]{3,2,0,1:T(8,128)(2,1)S(1)} %pad_maximum_fusion), channel_id=1, source_target_pairs={{0,12},{1,13},{2,14},{3,15},{4,0},{5,1},{6,2},{7,3},{8,4},{9,5},{1... | collective-permute-start | bytes 7077896 | tf_op jit(solution)/shard_map/ppermute | solution.py:52
  38.9 14.2 %collective-permute-start.9 = (bf16[2,384,384]{2,1,0:T(8,128)(2,1)S(1)}, bf16[2,384,384]{2,1,0:T(8,128)(2,1)S(1)}, u32[]{:S(2)}, u32[]{:S(2)}) collective-permute-start(bf16[2,384,384]{2,1,0:T(8,128)(2,1)S(1)} %collective-permute-done.8.refs_2_), channel_id=1, source_target_pairs={{0,32},{1,33},{2,34},{3,35},{4,36},{5,37},{6,38},{7,39},{8,40},{9,... | collective-permute-start | bytes 1769480 | tf_op jit(solution)/shard_map/ppermute | solution.py:52
  38.9 14.2 %collective-permute-start.12 = (bf16[2,384,384]{2,1,0:T(8,128)(2,1)S(1)}, bf16[2,384,384]{2,1,0:T(8,128)(2,1)S(1)}, u32[]{:S(2)}, u32[]{:S(2)}) collective-permute-start(bf16[2,384,384]{2,1,0:T(8,128)(2,1)S(1)} %collective-permute-done.11.refs_5_), channel_id=1, source_target_pairs={{0,224},{1,225},{2,226},{3,227},{4,228},{5,229},{6,230},{7,231},{8... | collective-permute-start | bytes 1769480 | tf_op jit(solution)/shard_map/ppermute | solution.py:52
  53.7 14.5 %copy-start.2 = (bf16[3,384,384]{2,1,0:T(8,128)(2,1)S(1)}, bf16[3,384,384]{2,1,0:T(8,128)(2,1)}, u32[]{:S(2)}) copy-start(bf16[3,384,384]{2,1,0:T(8,128)(2,1)} %ovl_ref.1) | copy-start | bytes 2654212
  57.4 17.5 %collective-permute-start.13 = (bf16[4,384,384]{2,1,0:T(8,128)(2,1)S(1)}, bf16[4,384,384]{2,1,0:T(8,128)(2,1)S(1)}, u32[]{:S(2)}, u32[]{:S(2)}) collective-permute-start(bf16[4,384,384]{2,1,0:T(8,128)(2,1)S(1)} %slice_bitcast_fusion.1), channel_id=1, source_target_pairs={{0,4},{1,5},{2,6},{3,7},{4,8},{5,9},{6,10},{7,11},{8,12},{9,13},{1... | collective-permute-start | bytes 3538952 | tf_op jit(solution)/shard_map/ppermute | solution.py:52
  58.7 16.3 %collective-permute-start.14 = (bf16[4,384,384]{2,1,0:T(8,128)(2,1)S(1)}, bf16[4,384,384]{2,1,0:T(8,128)(2,1)S(1)}, u32[]{:S(2)}, u32[]{:S(2)}) collective-permute-start(bf16[4,384,384]{2,1,0:T(8,128)(2,1)S(1)} %slice_bitcast_fusion), channel_id=1, source_target_pairs={{0,12},{1,13},{2,14},{3,15},{4,0},{5,1},{6,2},{7,3},{8,4},{9,5},{1... | collective-permute-start | bytes 3538952 | tf_op jit(solution)/shard_map/ppermute | solution.py:52
  60.2 13.2 %collective-permute-start.17 = (bf16[3,384,384]{2,1,0:T(8,128)(2,1)S(1)}, bf16[3,384,384]{2,1,0:T(8,128)(2,1)S(1)}, u32[]{:S(2)}, u32[]{:S(2)}) collective-permute-start(bf16[3,384,384]{2,1,0:T(8,128)(2,1)S(1)} %copy-done.1), channel_id=1, source_target_pairs={{0,16},{1,17},{2,18},{3,19},{4,20},{5,21},{6,22},{7,23},{8,24},{9,... | collective-permute-start | bytes 2654216 | tf_op jit(solution)/shard_map/ppermute | solution.py:52
  63.4 2.1 %collective-permute-start = (s32[3,3]{1,0:T(4,128)S(1)}, s32[3,3]{1,0:T(4,128)S(1)}, u32[]{:S(2)}, u32[]{:S(2)}) collective-permute-start(s32[3,3]{1,0:T(4,128)S(1)} %copy-done.7), channel_id=1, source_target_pairs={{0,16},{1,17},{2,18},{3,19},{4,20},{5,21},{6,22},{7,23},{8,24},{9,... | collective-permute-start | bytes 116 | tf_op jit(solution)/shard_map/ppermute | solution.py:52
  63.7 1.8 %collective-permute-start.18 = (s32[1,384]{1,0:T(1,128)S(1)}, s32[1,384]{1,0:T(1,128)S(1)}, u32[]{:S(2)}, u32[]{:S(2)}) collective-permute-start(s32[1,384]{1,0:T(1,128)S(1)} %copy-done.5), channel_id=1, source_target_pairs={{0,16},{1,17},{2,18},{3,19},{4,20},{5,21},{6,22},{7,23},{8,24},{9,... | collective-permute-start | bytes 4616 | tf_op jit(solution)/shard_map/ppermute | solution.py:52
  65.5 9.4 %collective-permute-start.15 = (bf16[384,384]{1,0:T(8,128)(2,1)S(1)}, bf16[384,384]{1,0:T(8,128)(2,1)S(1)}, u32[]{:S(2)}, u32[]{:S(2)}) collective-permute-start(bf16[384,384]{1,0:T(8,128)(2,1)S(1)} %slice_bitcast_fusion.3), channel_id=1, source_target_pairs={{0,32},{1,33},{2,34},{3,35},{4,36},{5,37},{6,38},{7,39},{8,40},{9,... | collective-permute-start | bytes 884744 | tf_op jit(solution)/shard_map/ppermute | solution.py:52
  65.5 9.4 %collective-permute-start.16 = (bf16[384,384]{1,0:T(8,128)(2,1)S(1)}, bf16[384,384]{1,0:T(8,128)(2,1)S(1)}, u32[]{:S(2)}, u32[]{:S(2)}) collective-permute-start(bf16[384,384]{1,0:T(8,128)(2,1)S(1)} %slice_bitcast_fusion.2), channel_id=1, source_target_pairs={{0,224},{1,225},{2,226},{3,227},{4,228},{5,229},{6,230},{7,231},{8... | collective-permute-start | bytes 884744 | tf_op jit(solution)/shard_map/ppermute | solution.py:52
  74.9 19.7 %copy-start.4 = (f32[3,96]{1,0:T(4,128)S(1)}, f32[3,96]{1,0:T(4,128)}, u32[]{:S(2)}) copy-start(f32[3,96]{1,0:T(4,128)} %velocities_ref.3) | copy-start | bytes 3460
  75.0 19.7 %copy-start.6 = (f32[96]{0:T(128)S(1)}, f32[96]{0:T(128)}, u32[]{:S(2)}) copy-start(f32[96]{0:T(128)} %param.19) | copy-start | bytes 1156
  75.0 34.7 %copy-start.8 = (f32[3,96]{1,0:T(4,128)S(1)}, f32[3,96]{1,0:T(4,128)}, u32[]{:S(2)}) copy-start(f32[3,96]{1,0:T(4,128)} %positions_ref.1) | copy-start | bytes 3460
  79.1 30.6 %collective-permute-start.19 = (bf16[384,384]{1,0:T(8,128)(2,1)S(1)}, bf16[384,384]{1,0:T(8,128)(2,1)S(1)}, u32[]{:S(2)}, u32[]{:S(2)}) collective-permute-start(bf16[384,384]{1,0:T(8,128)(2,1)S(1)} %get-tuple-element.17), channel_id=1, source_target_pairs={{0,16},{1,17},{2,18},{3,19},{4,20},{5,21},{6,22},{7,23},{8,24},{9,... | collective-permute-start | bytes 884744 | tf_op jit(solution)/shard_map/ppermute | solution.py:52
  (6 other events, 47.7 us)

commit v8 on v7

--- a/solution.py
+++ b/solution.py
@@ -198,6 +198,24 @@
                 total_ref[half] += product
 
 
+def opposite_kernel(z_low, z_high, part_ref, b_far_ref, a_far_ref, total_ref, b_last_ref):
+    z = position()[0]
+    b_last_ref[...] = b_far_ref[...]
+    for half, piece in enumerate((z_low, z_high)):
+        slot = slot_of(z + 4, half)
+
+        @pl.when(slot >= NEAR)
+        def _():
+            b_last_ref[slot - NEAR] = piece[...]
+
+    rows = jnp.concatenate([z_low[...], z_high[...]], axis=0)
+    for half in range(HALVES):
+        columns = jnp.concatenate([a_far_ref[i, half] for i in range(2)], axis=1)
+        total_ref[half] = part_ref[half] + jnp.dot(
+            columns, rows, preferred_element_type=jnp.float32
+        )
+
+
 def purify_kernel(
     branch_ref,
     pattern_ref,
@@ -205,11 +223,8 @@
     block_ref,
     line_low,
     line_high,
-    z_low,
-    z_high,
     total_ref,
-    b_far_ref,
-    a_far_ref,
+    b_last_ref,
     ham_ref,
     other_ham_ref,
     atom_ref,
@@ -218,24 +233,14 @@
     out_ref,
     give_ref,
     sums_ref,
-    b_buf,
     done,
     out_sem,
 ):
-    z, core, _, _ = position()
-    b_buf[: SLABS - NEAR] = b_far_ref[...]
-    for half, piece in enumerate((z_low, z_high)):
-        slot = slot_of(z + 4, half)
-        b_buf[SLABS - NEAR + half] = piece[...]
-
-        @pl.when(slot >= NEAR)
-        def _():
-            b_buf[slot - NEAR] = piece[...]
-
-    rows = b_buf[...].reshape((SLABS - NEAR + 2) * ROWS, ROWS)
+    core = position()[1]
+    rows = b_last_ref[...].reshape((SLABS - NEAR) * ROWS, ROWS)
     for half in range(HALVES):
         lead = line_low if half == 0 else line_high
-        columns = [lead[i] for i in range(4)] + [a_far_ref[i, half] for i in range(2)]
+        columns = [lead[i] for i in range(4)]
         square = total_ref[half] + jnp.dot(
             jnp.concatenate(columns, axis=1), rows, preferred_element_type=jnp.float32
         )
@@ -389,6 +394,17 @@
         compiler_params=PARAMS,
         cost_estimate=cost(NEAR),
     )(*first, columns)
+    total, b_last = pl.pallas_call(
+        opposite_kernel,
+        out_shape=(
+            small((HALVES, ROWS, ROWS)),
+            jax.ShapeDtypeStruct((SLABS - NEAR, ROWS, ROWS), jnp.bfloat16),
+        ),
+        in_specs=[VMEM] * 5,
+        out_specs=(VMEM, VMEM),
+        compiler_params=PARAMS,
+        cost_estimate=cost(2),
+    )(*opposite, total, b_far, a_far)
     half, give, sums = pl.pallas_call(
         purify_kernel,
         out_shape=(
@@ -396,25 +412,22 @@
             jax.ShapeDtypeStruct((ROWS, ROWS), jnp.bfloat16),
             small((SLABS, 8, LANES)),
         ),
-        in_specs=[SMEM] * 3 + [VMEM] * 13,
+        in_specs=[SMEM] * 3 + [VMEM] * 10,
         out_specs=(HBM, VMEM, VMEM),
         scratch_shapes=[
-            pltpu.VMEM((SLABS - NEAR + 2, ROWS, ROWS), jnp.bfloat16),
             pltpu.VMEM((HALVES, ROWS, ROWS), jnp.bfloat16),
             pltpu.SemaphoreType.DMA,
         ],
         compiler_params=PARAMS,
-        cost_estimate=cost(SLABS - NEAR + 2),
+        cost_estimate=cost(SLABS - NEAR),
     )(
         branch,
         tile_pattern,
         other_pattern,
         block,
         *last,
-        *opposite,
         total,
-        b_far,
-        a_far,
+        b_last,
         ham_deriv,
         other_ham,
         orbital_atom,

time: 111 us -> 111 us (level)
  no operation moved by 1% of the time
where the time goes in v8:
time: 111 us; the launch traced here: 110 us
  waiting for transfers between devices  36.6 us (33%)
  starting transfers between devices  32.1 us (29%)
  blocking collectives  27.4 us (25%)
  Pallas kernels  10.8 us (10%)
  local copies, waits for them, and re-layouts  2.13 us (2%)
    ppermute x20, waiting for transfers between devices, send(): return lax.ppermute(value, AXES, table)  36.6 us
    ppermute x20, starting transfers between devices, send(): return lax.ppermute(value, AXES, table)  32.1 us
    all_to_all x1, blocking collectives, local(): parts = lax.all_to_all(parts, 'row', 0, 0)  14.8 us
    all_to_all x1, blocking collectives, local(): parts = lax.all_to_all(sums, 'col', 0, 0)  12.6 us
    pallas_call x1, Pallas kernels, local(): pl.pallas_call(near_kernel, out_shape=(small((HALVES, ROWS, ROWS)), jax.S...  4.15 us
    pallas_call x1, Pallas kernels, local(): pl.pallas_call(purify_kernel, out_shape=(jax.ShapeDtypeStruct((2, ROWS, R...  3.29 us
  transfers between devices with their start and end apart: 20, of which 8 were waited for; matrix products, arithmetic and copies ran while one was open for 1% of the time, Pallas kernels for 5%

profile of v8, /device:TPU:1, one launch (start us, length us, event | category | flops | bytes accessed | tf_op | source)
XLA Modules:
  0.0 110.3 jit_solution(1519152684217205636)
XLA Ops:
  0.6 1.1 copy-done
  1.8 3.3 %collective-permute-start.1 = (bf16[384,384]{1,0:T(8,128)(2,1)S(1)}, bf16[384,384]{1,0:T(8,128)(2,1)S(1)}, u32[]{:S(2)}, u32[]{:S(2)}) collective-permute-start(bf16[384,384]{1,0:T(8,128)(2,1)S(1)} %shard_map.129), channel_id=1, source_target_pairs={{0,16},{1,17},{2,18},{3,19},{4,20},{5,21},{6,22},{7,23},{8,24},{9,... | collective-permute-start | bytes 884744 | tf_op jit(solution)/shard_map/ppermute | solution.py:52
  5.1 1.2 %collective-permute-done.1.got_ref = bf16[384,384]{1,0:T(8,128)(2,1)S(1)} collective-permute-done((bf16[384,384]{1,0:T(8,128)(2,1)S(1)}, bf16[384,384]{1,0:T(8,128)(2,1)S(1)}, u32[]{:S(2)}, u32[]{:S(2)}) %collective-permute-start.1) | collective-permute-done | bytes 294944 | tf_op jit(solution)/shard_map/ppermute | solution.py:52
  6.5 3.9 %collective-permute-start.10 = (bf16[2,384,384]{2,1,0:T(8,128)(2,1)S(1)}, bf16[2,384,384]{2,1,0:T(8,128)(2,1)S(1)}, u32[]{:S(2)}, u32[]{:S(2)}) collective-permute-start(bf16[2,384,384]{2,1,0:T(8,128)(2,1)S(1)} %shard_map.130.refs_0_.block_ref), channel_id=1, source_target_pairs={{0,224},{1,225},{2,226},{3,227},{4,228},{5,229},{6,230},{7,231},{8... | collective-permute-start | bytes 1769480 | tf_op jit(solution)/shard_map/ppermute | solution.py:52
  10.5 2.7 %collective-permute-start.4 = (bf16[2,384,384]{2,1,0:T(8,128)(2,1)S(1)}, bf16[2,384,384]{2,1,0:T(8,128)(2,1)S(1)}, u32[]{:S(2)}, u32[]{:S(2)}) collective-permute-start(bf16[2,384,384]{2,1,0:T(8,128)(2,1)S(1)} %shard_map.130.refs_0_.block_ref), channel_id=1, source_target_pairs={{0,2},{1,3},{2,0},{3,1},{4,6},{5,7},{6,4},{7,5},{8,10},{9,11},{10,... | collective-permute-start | bytes 1769480 | tf_op jit(solution)/shard_map/ppermute | solution.py:52
  14.7 9.1 %collective-permute-done.7.refs_1_ = bf16[2,384,384]{2,1,0:T(8,128)(2,1)S(1)} collective-permute-done((bf16[2,384,384]{2,1,0:T(8,128)(2,1)S(1)}, bf16[2,384,384]{2,1,0:T(8,128)(2,1)S(1)}, u32[]{:S(2)}, u32[]{:S(2)}) %collective-permute-start.7) | collective-permute-done | bytes 589856 | tf_op jit(solution)/shard_map/ppermute | solution.py:52
  23.8 2.7 %collective-permute-start.11 = (bf16[2,384,384]{2,1,0:T(8,128)(2,1)S(1)}, bf16[2,384,384]{2,1,0:T(8,128)(2,1)S(1)}, u32[]{:S(2)}, u32[]{:S(2)}) collective-permute-start(bf16[2,384,384]{2,1,0:T(8,128)(2,1)S(1)} %collective-permute-done.10.refs_6_), channel_id=1, source_target_pairs={{0,224},{1,225},{2,226},{3,227},{4,228},{5,229},{6,230},{7,231},{8... | collective-permute-start | bytes 1769480 | tf_op jit(solution)/shard_map/ppermute | solution.py:52
  27.8 1.4 %collective-permute-start.5 = (bf16[4,2,384,384]{3,2,0,1:T(8,128)(2,1)S(1)}, bf16[4,2,384,384]{3,2,0,1:T(8,128)(2,1)S(1)}, u32[]{:S(2)}, u32[]{:S(2)}) collective-permute-start(bf16[4,2,384,384]{3,2,0,1:T(8,128)(2,1)S(1)} %pad_maximum_fusion), channel_id=1, source_target_pairs={{0,4},{1,5},{2,6},{3,7},{4,8},{5,9},{6,10},{7,11},{8,12},{9,13},{1... | collective-permute-start | bytes 7077896 | tf_op jit(solution)/shard_map/ppermute | solution.py:52
  29.2 1.5 %collective-permute-start.6 = (bf16[4,2,384,384]{3,2,0,1:T(8,128)(2,1)S(1)}, bf16[4,2,384,384]{3,2,0,1:T(8,128)(2,1)S(1)}, u32[]{:S(2)}, u32[]{:S(2)}) collective-permute-start(bf16[4,2,384,384]{3,2,0,1:T(8,128)(2,1)S(1)} %pad_maximum_fusion), channel_id=1, source_target_pairs={{0,12},{1,13},{2,14},{3,15},{4,0},{5,1},{6,2},{7,3},{8,4},{9,5},{1... | collective-permute-start | bytes 7077896 | tf_op jit(solution)/shard_map/ppermute | solution.py:52
  30.7 8.2 %collective-permute-done.8.refs_2_ = bf16[2,384,384]{2,1,0:T(8,128)(2,1)S(1)} collective-permute-done((bf16[2,384,384]{2,1,0:T(8,128)(2,1)S(1)}, bf16[2,384,384]{2,1,0:T(8,128)(2,1)S(1)}, u32[]{:S(2)}, u32[]{:S(2)}) %collective-permute-start.8) | collective-permute-done | bytes 589856 | tf_op jit(solution)/shard_map/ppermute | solution.py:52
  38.9 2.7 %collective-permute-start.12 = (bf16[2,384,384]{2,1,0:T(8,128)(2,1)S(1)}, bf16[2,384,384]{2,1,0:T(8,128)(2,1)S(1)}, u32[]{:S(2)}, u32[]{:S(2)}) collective-permute-start(bf16[2,384,384]{2,1,0:T(8,128)(2,1)S(1)} %collective-permute-done.11.refs_5_), channel_id=1, source_target_pairs={{0,224},{1,225},{2,226},{3,227},{4,228},{5,229},{6,230},{7,231},{8... | collective-permute-start | bytes 1769480 | tf_op jit(solution)/shard_map/ppermute | solution.py:52
  41.6 11.6 %collective-permute-done.9.refs_3_ = bf16[2,384,384]{2,1,0:T(8,128)(2,1)S(1)} collective-permute-done((bf16[2,384,384]{2,1,0:T(8,128)(2,1)S(1)}, bf16[2,384,384]{2,1,0:T(8,128)(2,1)S(1)}, u32[]{:S(2)}, u32[]{:S(2)}) %collective-permute-start.9) | collective-permute-done | bytes 589856 | tf_op jit(solution)/shard_map/ppermute | solution.py:52
  53.7 3.5 %collective-permute-done.5 = bf16[4,2,384,384]{3,2,0,1:T(8,128)(2,1)S(1)} collective-permute-done((bf16[4,2,384,384]{3,2,0,1:T(8,128)(2,1)S(1)}, bf16[4,2,384,384]{3,2,0,1:T(8,128)(2,1)S(1)}, u32[]{:S(2)}, u32[]{:S(2)}) %collective-permute-start.5) | collective-permute-done | bytes 2359328 | tf_op jit(solution)/shard_map/ppermute | solution.py:52
  57.4 1.3 %collective-permute-start.13 = (bf16[4,384,384]{2,1,0:T(8,128)(2,1)S(1)}, bf16[4,384,384]{2,1,0:T(8,128)(2,1)S(1)}, u32[]{:S(2)}, u32[]{:S(2)}) collective-permute-start(bf16[4,384,384]{2,1,0:T(8,128)(2,1)S(1)} %slice_bitcast_fusion.1), channel_id=1, source_target_pairs={{0,4},{1,5},{2,6},{3,7},{4,8},{5,9},{6,10},{7,11},{8,12},{9,13},{1... | collective-permute-start | bytes 3538952 | tf_op jit(solution)/shard_map/ppermute | solution.py:52
  58.7 1.5 %collective-permute-start.14 = (bf16[4,384,384]{2,1,0:T(8,128)(2,1)S(1)}, bf16[4,384,384]{2,1,0:T(8,128)(2,1)S(1)}, u32[]{:S(2)}, u32[]{:S(2)}) collective-permute-start(bf16[4,384,384]{2,1,0:T(8,128)(2,1)S(1)} %slice_bitcast_fusion), channel_id=1, source_target_pairs={{0,12},{1,13},{2,14},{3,15},{4,0},{5,1},{6,2},{7,3},{8,4},{9,5},{1... | collective-permute-start | bytes 3538952 | tf_op jit(solution)/shard_map/ppermute | solution.py:52
  60.2 3.2 %collective-permute-start.17 = (bf16[3,384,384]{2,1,0:T(8,128)(2,1)S(1)}, bf16[3,384,384]{2,1,0:T(8,128)(2,1)S(1)}, u32[]{:S(2)}, u32[]{:S(2)}) collective-permute-start(bf16[3,384,384]{2,1,0:T(8,128)(2,1)S(1)} %copy-done.2), channel_id=1, source_target_pairs={{0,16},{1,17},{2,18},{3,19},{4,20},{5,21},{6,22},{7,23},{8,24},{9,... | collective-permute-start | bytes 2654216 | tf_op jit(solution)/shard_map/ppermute | solution.py:52
  63.8 2.7 %collective-permute-start.16 = (bf16[384,384]{1,0:T(8,128)(2,1)S(1)}, bf16[384,384]{1,0:T(8,128)(2,1)S(1)}, u32[]{:S(2)}, u32[]{:S(2)}) collective-permute-start(bf16[384,384]{1,0:T(8,128)(2,1)S(1)} %slice_bitcast_fusion.2), channel_id=1, source_target_pairs={{0,224},{1,225},{2,226},{3,227},{4,228},{5,229},{6,230},{7,231},{8... | collective-permute-start | bytes 884744 | tf_op jit(solution)/shard_map/ppermute | solution.py:52
  67.6 4.1 %shard_map.132 = (f32[2,384,384]{2,1,0:T(8,128)S(1)}, bf16[4,384,384]{2,1,0:T(8,128)(2,1)S(1)}, bf16[2,2,384,384]{3,2,1,0:T(8,128)(2,1)S(1)}) custom-call(bf16[4,2,384,384]{3,2,1,0:T(8,128)(2,1)S(1)} %copy.15.refs_0_, bf16[4,2,384,384]{3,2,1,0:T(8,128)(2,1)S(1)} %copy.16.refs_1_, bf16[4,2,384,384]{3,2,1,0:T(8,128)(2,1)S(1)} %copy.17.refs_2_, ...), custom_call_target="tpu_custom_call" | custom-call | flops 2717908992 | bytes 14155776 | tf_op jit(solution)/shard_map/pallas_call | solution.py:385
  71.8 1.8 %collective-permute-done.15.z_low = bf16[384,384]{1,0:T(8,128)(2,1)S(1)} collective-permute-done((bf16[384,384]{1,0:T(8,128)(2,1)S(1)}, bf16[384,384]{1,0:T(8,128)(2,1)S(1)}, u32[]{:S(2)}, u32[]{:S(2)}) %collective-permute-start.15) | collective-permute-done | bytes 294944 | tf_op jit(solution)/shard_map/ppermute | solution.py:52
  75.6 3.3 %shard_map.135 = (bf16[2,384,384]{2,1,0:T(8,128)(2,1)}, bf16[384,384]{1,0:T(8,128)(2,1)S(1)}, f32[16,8,128]{2,1,0:T(8,128)S(1)}) custom-call(s32[2]{0:T(128)S(1)} %copy-done.9, s32[3,3]{1,0:T(4,128)S(1)} %copy-done.7, s32[3,3]{1,0:T(4,128)S(1)} %collective-permute-done.other_pattern_ref, bf16[2,384,384]{2,1,0:T(8,128)(2,1)S(1)} %shard_map.130.refs_0_.block_ref, ...), custom_call_target="tpu_custom_call" | custom-call | flops 905969664 | bytes 4718592 | tf_op jit(solution)/shard_map/pallas_call | solution.py:408
  78.9 2.4 %collective-permute-start.19 = (bf16[384,384]{1,0:T(8,128)(2,1)S(1)}, bf16[384,384]{1,0:T(8,128)(2,1)S(1)}, u32[]{:S(2)}, u32[]{:S(2)}) collective-permute-start(bf16[384,384]{1,0:T(8,128)(2,1)S(1)} %get-tuple-element.21), channel_id=1, source_target_pairs={{0,16},{1,17},{2,18},{3,19},{4,20},{5,21},{6,22},{7,23},{8,24},{9,... | collective-permute-start | bytes 884744 | tf_op jit(solution)/shard_map/ppermute | solution.py:52
  81.3 12.6 %all_to_all.10.parts_ref = f32[16,8,128]{2,1,0:T(8,128)S(1)} all-to-all(f32[16,8,128]{2,1,0:T(8,128)S(1)} %get-tuple-element.23), channel_id=1, replica_groups=mesh['row'=16,'col'=16] {'col'}, dimensions={0} | all-to-all | bytes 131072 | tf_op jit(solution)/shard_map/all_to_all | solution.py:439
  94.0 14.8 %all_to_all.11.all_ref = f32[16,8,128]{2,1,0:T(8,128)S(1)} all-to-all(f32[16,8,128]{2,1,0:T(8,128)S(1)} %shard_map.136), channel_id=1, replica_groups=mesh['row'=16,'col'=16] {'row'}, dimensions={0} | all-to-all | bytes 131072 | tf_op jit(solution)/shard_map/all_to_all | solution.py:448
  108.9 1.3 %shard_map.137 = (bf16[2,384,384]{2,1,0:T(8,128)(2,1)}, f32[3,96]{1,0:T(4,128)}, f32[3,96]{1,0:T(4,128)}, f32[3,96]{1,0:T(4,128)}) custom-call(bf16[384,384]{1,0:T(8,128)(2,1)S(1)} %collective-permute-done.19.got_ref, bf16[2,384,384]{2,1,0:T(8,128)(2,1)} %get-tuple-element.22.half_ref, ...), custom_call_target="tpu_custom_call", output_to_operand_aliasing={{0}: (1, {})} | custom-call | tf_op jit(solution)/shard_map/pallas_call | solution.py:449
  (55 shorter events, 7.3 us)
Async XLA Ops:
  1.8 4.5 %collective-permute-start.1 = (bf16[384,384]{1,0:T(8,128)(2,1)S(1)}, bf16[384,384]{1,0:T(8,128)(2,1)S(1)}, u32[]{:S(2)}, u32[]{:S(2)}) collective-permute-start(bf16[384,384]{1,0:T(8,128)(2,1)S(1)} %shard_map.129), channel_id=1, source_target_pairs={{0,16},{1,17},{2,18},{3,19},{4,20},{5,21},{6,22},{7,23},{8,24},{9,... | collective-permute-start | bytes 884744 | tf_op jit(solution)/shard_map/ppermute | solution.py:52
  6.5 17.3 %collective-permute-start.7 = (bf16[2,384,384]{2,1,0:T(8,128)(2,1)S(1)}, bf16[2,384,384]{2,1,0:T(8,128)(2,1)S(1)}, u32[]{:S(2)}, u32[]{:S(2)}) collective-permute-start(bf16[2,384,384]{2,1,0:T(8,128)(2,1)S(1)} %shard_map.130.refs_0_.block_ref), channel_id=1, source_target_pairs={{0,32},{1,33},{2,34},{3,35},{4,36},{5,37},{6,38},{7,39},{8,40},{9,... | collective-permute-start | bytes 1769480 | tf_op jit(solution)/shard_map/ppermute | solution.py:52
  6.5 17.2 %collective-permute-start.10 = (bf16[2,384,384]{2,1,0:T(8,128)(2,1)S(1)}, bf16[2,384,384]{2,1,0:T(8,128)(2,1)S(1)}, u32[]{:S(2)}, u32[]{:S(2)}) collective-permute-start(bf16[2,384,384]{2,1,0:T(8,128)(2,1)S(1)} %shard_map.130.refs_0_.block_ref), channel_id=1, source_target_pairs={{0,224},{1,225},{2,226},{3,227},{4,228},{5,229},{6,230},{7,231},{8... | collective-permute-start | bytes 1769480 | tf_op jit(solution)/shard_map/ppermute | solution.py:52
  10.5 16.0 %collective-permute-start.4 = (bf16[2,384,384]{2,1,0:T(8,128)(2,1)S(1)}, bf16[2,384,384]{2,1,0:T(8,128)(2,1)S(1)}, u32[]{:S(2)}, u32[]{:S(2)}) collective-permute-start(bf16[2,384,384]{2,1,0:T(8,128)(2,1)S(1)} %shard_map.130.refs_0_.block_ref), channel_id=1, source_target_pairs={{0,2},{1,3},{2,0},{3,1},{4,6},{5,7},{6,4},{7,5},{8,10},{9,11},{10,... | collective-permute-start | bytes 1769480 | tf_op jit(solution)/shard_map/ppermute | solution.py:52
  13.2 14.2 %collective-permute-start.3 = (bf16[2,384,384]{2,1,0:T(8,128)(2,1)S(1)}, bf16[2,384,384]{2,1,0:T(8,128)(2,1)S(1)}, u32[]{:S(2)}, u32[]{:S(2)}) collective-permute-start(bf16[2,384,384]{2,1,0:T(8,128)(2,1)S(1)} %shard_map.130.refs_0_.block_ref), channel_id=1, source_target_pairs={{0,3},{1,0},{2,1},{3,2},{4,7},{5,4},{6,5},{7,6},{8,11},{9,8},{10,9... | collective-permute-start | bytes 1769480 | tf_op jit(solution)/shard_map/ppermute | solution.py:52
  14.1 13.4 %collective-permute-start.2 = (bf16[2,384,384]{2,1,0:T(8,128)(2,1)S(1)}, bf16[2,384,384]{2,1,0:T(8,128)(2,1)S(1)}, u32[]{:S(2)}, u32[]{:S(2)}) collective-permute-start(bf16[2,384,384]{2,1,0:T(8,128)(2,1)S(1)} %shard_map.130.refs_0_.block_ref), channel_id=1, source_target_pairs={{0,1},{1,2},{2,3},{3,0},{4,5},{5,6},{6,7},{7,4},{8,9},{9,10},{10,1... | collective-permute-start | bytes 1769480 | tf_op jit(solution)/shard_map/ppermute | solution.py:52
  23.8 15.2 %collective-permute-start.8 = (bf16[2,384,384]{2,1,0:T(8,128)(2,1)S(1)}, bf16[2,384,384]{2,1,0:T(8,128)(2,1)S(1)}, u32[]{:S(2)}, u32[]{:S(2)}) collective-permute-start(bf16[2,384,384]{2,1,0:T(8,128)(2,1)S(1)} %collective-permute-done.7.refs_1_), channel_id=1, source_target_pairs={{0,32},{1,33},{2,34},{3,35},{4,36},{5,37},{6,38},{7,39},{8,40},{9,... | collective-permute-start | bytes 1769480 | tf_op jit(solution)/shard_map/ppermute | solution.py:52
  23.8 15.2 %collective-permute-start.11 = (bf16[2,384,384]{2,1,0:T(8,128)(2,1)S(1)}, bf16[2,384,384]{2,1,0:T(8,128)(2,1)S(1)}, u32[]{:S(2)}, u32[]{:S(2)}) collective-permute-start(bf16[2,384,384]{2,1,0:T(8,128)(2,1)S(1)} %collective-permute-done.10.refs_6_), channel_id=1, source_target_pairs={{0,224},{1,225},{2,226},{3,227},{4,228},{5,229},{6,230},{7,231},{8... | collective-permute-start | bytes 1769480 | tf_op jit(solution)/shard_map/ppermute | solution.py:52
  27.8 29.3 %collective-permute-start.5 = (bf16[4,2,384,384]{3,2,0,1:T(8,128)(2,1)S(1)}, bf16[4,2,384,384]{3,2,0,1:T(8,128)(2,1)S(1)}, u32[]{:S(2)}, u32[]{:S(2)}) collective-permute-start(bf16[4,2,384,384]{3,2,0,1:T(8,128)(2,1)S(1)} %pad_maximum_fusion), channel_id=1, source_target_pairs={{0,4},{1,5},{2,6},{3,7},{4,8},{5,9},{6,10},{7,11},{8,12},{9,13},{1... | collective-permute-start | bytes 7077896 | tf_op jit(solution)/shard_map/ppermute | solution.py:52
  29.2 28.1 %collective-permute-start.6 = (bf16[4,2,384,384]{3,2,0,1:T(8,128)(2,1)S(1)}, bf16[4,2,384,384]{3,2,0,1:T(8,128)(2,1)S(1)}, u32[]{:S(2)}, u32[]{:S(2)}) collective-permute-start(bf16[4,2,384,384]{3,2,0,1:T(8,128)(2,1)S(1)} %pad_maximum_fusion), channel_id=1, source_target_pairs={{0,12},{1,13},{2,14},{3,15},{4,0},{5,1},{6,2},{7,3},{8,4},{9,5},{1... | collective-permute-start | bytes 7077896 | tf_op jit(solution)/shard_map/ppermute | solution.py:52
  38.9 14.2 %collective-permute-start.9 = (bf16[2,384,384]{2,1,0:T(8,128)(2,1)S(1)}, bf16[2,384,384]{2,1,0:T(8,128)(2,1)S(1)}, u32[]{:S(2)}, u32[]{:S(2)}) collective-permute-start(bf16[2,384,384]{2,1,0:T(8,128)(2,1)S(1)} %collective-permute-done.8.refs_2_), channel_id=1, source_target_pairs={{0,32},{1,33},{2,34},{3,35},{4,36},{5,37},{6,38},{7,39},{8,40},{9,... | collective-permute-start | bytes 1769480 | tf_op jit(solution)/shard_map/ppermute | solution.py:52
  38.9 14.2 %collective-permute-start.12 = (bf16[2,384,384]{2,1,0:T(8,128)(2,1)S(1)}, bf16[2,384,384]{2,1,0:T(8,128)(2,1)S(1)}, u32[]{:S(2)}, u32[]{:S(2)}) collective-permute-start(bf16[2,384,384]{2,1,0:T(8,128)(2,1)S(1)} %collective-permute-done.11.refs_5_), channel_id=1, source_target_pairs={{0,224},{1,225},{2,226},{3,227},{4,228},{5,229},{6,230},{7,231},{8... | collective-permute-start | bytes 1769480 | tf_op jit(solution)/shard_map/ppermute | solution.py:52
  53.6 12.9 %copy-start.1 = (bf16[3,384,384]{2,1,0:T(8,128)(2,1)S(1)}, bf16[3,384,384]{2,1,0:T(8,128)(2,1)}, u32[]{:S(2)}) copy-start(bf16[3,384,384]{2,1,0:T(8,128)(2,1)} %ovl_ref.1) | copy-start | bytes 2654212
  57.4 18.1 %collective-permute-start.13 = (bf16[4,384,384]{2,1,0:T(8,128)(2,1)S(1)}, bf16[4,384,384]{2,1,0:T(8,128)(2,1)S(1)}, u32[]{:S(2)}, u32[]{:S(2)}) collective-permute-start(bf16[4,384,384]{2,1,0:T(8,128)(2,1)S(1)} %slice_bitcast_fusion.1), channel_id=1, source_target_pairs={{0,4},{1,5},{2,6},{3,7},{4,8},{5,9},{6,10},{7,11},{8,12},{9,13},{1... | collective-permute-start | bytes 3538952 | tf_op jit(solution)/shard_map/ppermute | solution.py:52
  58.7 16.9 %collective-permute-start.14 = (bf16[4,384,384]{2,1,0:T(8,128)(2,1)S(1)}, bf16[4,384,384]{2,1,0:T(8,128)(2,1)S(1)}, u32[]{:S(2)}, u32[]{:S(2)}) collective-permute-start(bf16[4,384,384]{2,1,0:T(8,128)(2,1)S(1)} %slice_bitcast_fusion), channel_id=1, source_target_pairs={{0,12},{1,13},{2,14},{3,15},{4,0},{5,1},{6,2},{7,3},{8,4},{9,5},{1... | collective-permute-start | bytes 3538952 | tf_op jit(solution)/shard_map/ppermute | solution.py:52
  60.2 15.3 %collective-permute-start.17 = (bf16[3,384,384]{2,1,0:T(8,128)(2,1)S(1)}, bf16[3,384,384]{2,1,0:T(8,128)(2,1)S(1)}, u32[]{:S(2)}, u32[]{:S(2)}) collective-permute-start(bf16[3,384,384]{2,1,0:T(8,128)(2,1)S(1)} %copy-done.2), channel_id=1, source_target_pairs={{0,16},{1,17},{2,18},{3,19},{4,20},{5,21},{6,22},{7,23},{8,24},{9,... | collective-permute-start | bytes 2654216 | tf_op jit(solution)/shard_map/ppermute | solution.py:52
  63.5 10.1 %collective-permute-start.15 = (bf16[384,384]{1,0:T(8,128)(2,1)S(1)}, bf16[384,384]{1,0:T(8,128)(2,1)S(1)}, u32[]{:S(2)}, u32[]{:S(2)}) collective-permute-start(bf16[384,384]{1,0:T(8,128)(2,1)S(1)} %slice_bitcast_fusion.3), channel_id=1, source_target_pairs={{0,32},{1,33},{2,34},{3,35},{4,36},{5,37},{6,38},{7,39},{8,40},{9,... | collective-permute-start | bytes 884744 | tf_op jit(solution)/shard_map/ppermute | solution.py:52
  63.8 10.6 %collective-permute-start.16 = (bf16[384,384]{1,0:T(8,128)(2,1)S(1)}, bf16[384,384]{1,0:T(8,128)(2,1)S(1)}, u32[]{:S(2)}, u32[]{:S(2)}) collective-permute-start(bf16[384,384]{1,0:T(8,128)(2,1)S(1)} %slice_bitcast_fusion.2), channel_id=1, source_target_pairs={{0,224},{1,225},{2,226},{3,227},{4,228},{5,229},{6,230},{7,231},{8... | collective-permute-start | bytes 884744 | tf_op jit(solution)/shard_map/ppermute | solution.py:52
  73.6 2.0 %collective-permute-start.18 = (s32[1,384]{1,0:T(1,128)S(1)}, s32[1,384]{1,0:T(1,128)S(1)}, u32[]{:S(2)}, u32[]{:S(2)}) collective-permute-start(s32[1,384]{1,0:T(1,128)S(1)} %copy-done.5), channel_id=1, source_target_pairs={{0,16},{1,17},{2,18},{3,19},{4,20},{5,21},{6,22},{7,23},{8,24},{9,... | collective-permute-start | bytes 4616 | tf_op jit(solution)/shard_map/ppermute | solution.py:52
  74.4 1.2 %collective-permute-start = (s32[3,3]{1,0:T(4,128)S(1)}, s32[3,3]{1,0:T(4,128)S(1)}, u32[]{:S(2)}, u32[]{:S(2)}) collective-permute-start(s32[3,3]{1,0:T(4,128)S(1)} %copy-done.7), channel_id=1, source_target_pairs={{0,16},{1,17},{2,18},{3,19},{4,20},{5,21},{6,22},{7,23},{8,24},{9,... | collective-permute-start | bytes 116 | tf_op jit(solution)/shard_map/ppermute | solution.py:52
  75.6 18.3 %copy-start.4 = (f32[3,96]{1,0:T(4,128)S(1)}, f32[3,96]{1,0:T(4,128)}, u32[]{:S(2)}) copy-start(f32[3,96]{1,0:T(4,128)} %velocities_ref.3) | copy-start | bytes 3460
  75.6 18.3 %copy-start.6 = (f32[96]{0:T(128)S(1)}, f32[96]{0:T(128)}, u32[]{:S(2)}) copy-start(f32[96]{0:T(128)} %param.19) | copy-start | bytes 1156
  75.6 33.3 %copy-start.8 = (f32[3,96]{1,0:T(4,128)S(1)}, f32[3,96]{1,0:T(4,128)}, u32[]{:S(2)}) copy-start(f32[3,96]{1,0:T(4,128)} %positions_ref.1) | copy-start | bytes 3460
  78.9 30.0 %collective-permute-start.19 = (bf16[384,384]{1,0:T(8,128)(2,1)S(1)}, bf16[384,384]{1,0:T(8,128)(2,1)S(1)}, u32[]{:S(2)}, u32[]{:S(2)}) collective-permute-start(bf16[384,384]{1,0:T(8,128)(2,1)S(1)} %get-tuple-element.21), channel_id=1, source_target_pairs={{0,16},{1,17},{2,18},{3,19},{4,20},{5,21},{6,22},{7,23},{8,24},{9,... | collective-permute-start | bytes 884744 | tf_op jit(solution)/shard_map/ppermute | solution.py:52
  (6 other events, 43.9 us)
